TPU v7x, 32 devices: a whole 2x2x4 slice. The times are simulated.
32 devices in a mesh: va: 4 (over y, x), vb: 4 (over z), pair: 2 (over core).
Axes of the slice: x: 2, y: 2, z: 4, core: 2. Of those that a mesh axis runs over, the one named last changes fastest.
Arguments:
- left_fit: bfloat16 [30, 2048, 1536], P('pair', 'va'), may hold values from -0.5 to 0.5
- right_fit: bfloat16 [30, 2048, 1536], P('pair', 'vb'), may hold values from -0.5 to 0.5
- occ_energy: float32 [8], replicated, may hold values from -1.5 to -0.3
- virt_energy: float32 [2048], replicated, may hold values from 0.2 to 2
- pair_list: int32 [30, 2], P('pair'), may hold values from 0 to 7, as said below
- domain_blocks: int32 [30, 12], P('pair'), may hold values from 0 to 31, as said below
Outputs:
- density: float32 [4096, 8, 2048], P(('vb', 'pair'), None, 'va')
Inputs may be any that keep to these rules, and one draw needn't show every extreme that they name: `domain_blocks`: the 12 entries of a row are distinct. `pair_list`: each row holds two orbitals i <= j, and no two rows are the same pair.
All inputs are finite; a program needn't handle non-finite values.
Results may differ from a plain program's by a relative error of at most 0.0028.
Values may be sent and summed in bfloat16 or wider, within the bound.
A program may use at most 256 MiB of HBM per device.

v0:
```python
import jax
import jax.numpy as jnp
from jax import lax
from jax.sharding import PartitionSpec as P

BLOCK = 128
NOCC = 8
AUX_BLK = 32


def pick_energy(occ_energy, column):
    levels = jnp.arange(occ_energy.shape[0], dtype=jnp.int32)
    return jnp.sum(jnp.where(column[:, None] == levels[None, :], occ_energy[None, :], 0.0), axis=1)


def shards(left_fit, right_fit, occ_energy, virt_energy, pair_list, domain_blocks):
    side_count = lax.axis_size("va")
    vb_count = lax.axis_size("vb")
    pair_count = lax.axis_size("pair")
    tile_rows = left_fit.shape[1]
    local_pairs = left_fit.shape[0]
    dom_blocks = domain_blocks.shape[1]
    va_index = lax.axis_index("va")
    vb_index = lax.axis_index("vb")
    energy_a = lax.dynamic_slice_in_dim(virt_energy, va_index * tile_rows, tile_rows)
    energy_b = lax.dynamic_slice_in_dim(virt_energy, vb_index * tile_rows, tile_rows)
    coulomb = jnp.einsum(
        "pak,pbk->pab", left_fit, right_fit, preferred_element_type=jnp.float32
    ).astype(jnp.bfloat16)
    sub_rows = tile_rows // side_count
    outgoing = coulomb.reshape(local_pairs, side_count, sub_rows, side_count, sub_rows)
    outgoing = outgoing.transpose(1, 3, 0, 2, 4).reshape(
        side_count * side_count, local_pairs * sub_rows * sub_rows
    )
    spread = lax.all_to_all(outgoing, ("va", "vb"), split_axis=0, concat_axis=0, tiled=True)
    spread = (
        spread.reshape(side_count, side_count, -1)
        .transpose(1, 0, 2)
        .reshape(side_count * side_count, -1)
    )
    returned = lax.all_to_all(spread, ("va", "vb"), split_axis=0, concat_axis=0, tiled=True)
    swapped = returned.reshape(side_count, side_count, local_pairs, sub_rows, sub_rows)
    swapped = swapped.transpose(2, 1, 4, 0, 3).reshape(local_pairs, tile_rows, tile_rows)
    first_energy = pick_energy(occ_energy, pair_list[:, 0])
    second_energy = pick_energy(occ_energy, pair_list[:, 1])
    energy_gap = (
        energy_a[None, :, None]
        + energy_b[None, None, :]
        - (first_energy + second_energy)[:, None, None]
    )
    coulomb_wide = coulomb.astype(jnp.float32)
    amplitude = ((2.0 * coulomb_wide - swapped.astype(jnp.float32)) / energy_gap).astype(
        jnp.bfloat16
    )
    contracted = jnp.einsum(
        "pbq,pab->pqa", right_fit, amplitude, preferred_element_type=jnp.float32
    )
    pieces = contracted.reshape(local_pairs * dom_blocks, BLOCK, tile_rows)
    block_ids = domain_blocks.reshape(-1)
    owner_ids = jnp.repeat(pair_list[:, 0], dom_blocks)
    slab_blocks = AUX_BLK // (vb_count * pair_count)
    sectioned_order = (
        block_ids // slab_blocks % pair_count * (AUX_BLK // pair_count)
        + block_ids // (slab_blocks * pair_count) * slab_blocks
        + block_ids % slab_blocks
    )
    block_count = lax.axis_size("pair") * (AUX_BLK * BLOCK // pair_count) // BLOCK
    inside = (sectioned_order >= 0) & (sectioned_order < block_count)
    target = jnp.where(inside, sectioned_order * NOCC + owner_ids, block_count * NOCC)
    summed = jax.ops.segment_sum(pieces, target, num_segments=block_count * NOCC + 1)[
        : block_count * NOCC
    ]
    summed = summed.reshape(block_count, NOCC, BLOCK, tile_rows).transpose(0, 2, 1, 3)
    chip_share = lax.psum_scatter(
        summed.reshape(block_count * BLOCK, NOCC, tile_rows),
        "pair",
        scatter_dimension=0,
        tiled=True,
    )
    density = lax.psum_scatter(chip_share, "vb", scatter_dimension=0, tiled=True)
    return density


def solution(mesh):
    return jax.shard_map(
        shards,
        mesh=mesh,
        in_specs=(
            P("pair", "va", None),
            P("pair", "vb", None),
            P(),
            P(),
            P("pair", None),
            P("pair", None),
        ),
        out_specs=P(("vb", "pair"), None, "va"),
        check_vma=False,
    )
```

profile of v0, /device:TPU:0, one launch (start us, length us, event | category | flops | bytes accessed | tf_op | source)
XLA Modules:
  0.0 1689.6 jit_solution(14715066837969007290)
XLA Ops:
  6.5 22.9 %convolution_convert_fusion = bf16[15,512,512]{2,1,0:T(8,128)(2,1)} fusion(bf16[15,512,1536]{2,1,0:T(8,128)(2,1)} %param.6, bf16[15,512,1536]{2,1,0:T(8,128)(2,1)} %param.7), kind=kOutput, calls=%fused_computation.7 | convolution fusion | flops 12083527680 | bytes 55050240 | tf_op jit(solution)/shard_map/pak,pbk->pab/dot_general | solution.py:27
  29.4 11.9 reshape.272
  49.8 14.0 all_to_all.16
  64.3 48.2 %reduce.1 = bf16[16,245760]{1,0:T(8,128)(2,1)} reduce(bf16[16,1,245760]{2,1,0:T(2,128)(2,1)} %all_to_all.16, bf16[]{:T(256)} %broadcast.218), dimensions={1}, to_apply=%all_to_all.16.reduce_sub_computation | reduce | bytes 15728642 | tf_op jit(solution)/shard_map/all_to_all | solution.py:35
  123.8 182.2 %all_to_all.20 = bf16[16,2,122880]{2,1,0:T(2,128)(2,1)} all-to-all(bf16[16,2,122880]{2,1,0:T(2,128)(2,1)} %reshape.288), channel_id=1, replica_groups=mesh['va'=4,'vb'=4,'pair'=2] {'va','vb'}, dimensions={0} | all-to-all | bytes 15728640 | tf_op jit(solution)/shard_map/all_to_all | solution.py:35
  305.9 15.8 reshape.289
  321.8 47.6 %reduce = bf16[16,245760]{1,0:T(8,128)(2,1)} reduce(bf16[16,1,245760]{2,1,0:T(2,128)(2,1)} %reshape.289, bf16[]{:T(256)} %constant.80), dimensions={1}, to_apply=%all_to_all.13.reduce_sub_computation | reduce | bytes 15728642 | tf_op jit(solution)/shard_map/all_to_all | solution.py:35
  376.2 11.5 copy.25
  387.7 13.1 all_to_all.17
  400.8 59.3 %reduce.2 = bf16[16,245760]{1,0:T(8,128)(2,1)} reduce(bf16[16,1,245760]{2,1,0:T(2,128)(2,1)} %all_to_all.17, bf16[]{:T(256)} %broadcast.218), dimensions={1}, to_apply=%all_to_all.17.reduce_sub_computation | reduce | bytes 15728642 | tf_op jit(solution)/shard_map/all_to_all | solution.py:41
  460.1 11.4 reshape.290
  476.8 189.4 %all-to-all-done.1 = bf16[16,2,122880]{2,1,0:T(2,128)(2,1)} async-done(((bf16[16,2,122880]{2,1,0:T(2,128)(2,1)}), bf16[16,2,122880]{2,1,0:T(2,128)(2,1)}, u32[]{:S(2)}, u32[]{:S(2)}) %all-to-all-start.1) | async-done | bytes 7864352 | tf_op jit(solution)/shard_map/all_to_all | solution.py:41
  666.3 15.8 reshape.291
  682.1 18.9 %convert_element_type.30 = f32[16,1,245760]{2,1,0:T(1,128)} convert(bf16[16,1,245760]{2,1,0:T(2,128)(2,1)} %reshape.291) | non-fusion elementwise | flops 3932160 | bytes 23592960 | tf_op jit(solution)/shard_map/convert_element_type | solution.py:52
  701.0 18.9 %copy.27 = f32[15,4,128,4,128]{4,3,2,1,0:T(4,128)} copy(f32[15,4,128,4,128]{2,4,0,1,3:T(8,128)} %bitcast.25) | data formatting | bytes 31457280 | tf_op jit(solution)/shard_map/convert_element_type | solution.py:52
  719.9 19.4 %reshape.277 = f32[15,512,512]{2,1,0:T(8,128)} reshape(f32[15,4,128,4,128]{4,3,2,1,0:T(4,128)} %copy.27) | data formatting | bytes 31457280 | tf_op jit(solution)/shard_map/convert_element_type | solution.py:52
  739.3 35.9 %convolution_bitcast_fusion = f32[15,1536,512]{1,2,0:T(8,128)} fusion(bf16[15,512,1536]{2,1,0:T(8,128)(2,1)} %param.7, f32[15,512,512]{2,1,0:T(8,128)} %reshape.277, bf16[15,512,512]{2,1,0:T(8,128)(2,1)} %convolution_convert_fusion, f32[15]{0:T(128)S(1)} %add.117, f32[512,512]{1,0:T(8,128)S(1)} %broadcast_add_fusion), kind=kOutput, calls=%fused_computation.1 | convolution fusion | flops 12103188480 | bytes 95420480 | tf_op jit(solution)/shard_map/pbq,pab->pqa/dot_general | solution.py:55
  775.2 45.9 %copy.28 = f32[15,1536,512]{2,1,0:T(8,128)} copy(f32[15,1536,512]{1,2,0:T(8,128)} %convolution_bitcast_fusion) | data formatting | bytes 94371840 | tf_op jit(solution)/shard_map/pbq,pab->pqa/dot_general | solution.py:55
  821.1 21.3 %broadcast_in_dim.34 = f32[257,128,512]{2,1,0:T(8,128)} broadcast(f32[]{:T(128)} %constant.59.clone.1), dimensions={} | broadcast | bytes 67371008 | tf_op jit(solution)/shard_map/broadcast_in_dim | solution.py:70
  842.4 105.3 %scatter_fusion = f32[257,128,512]{2,1,0:T(8,128)} fusion(f32[257,128,512]{2,1,0:T(8,128)} %broadcast_in_dim.34, s32[180]{0:T(256)S(1)} %bitcast.28, f32[180,128,512]{2,1,0:T(8,128)} %bitcast.24), kind=kCustom, calls=%fused_computation | custom fusion | flops 11796480 | bytes 141558480 | tf_op jit(solution)/shard_map/scatter-add | solution.py:70
  947.7 43.6 %slice.13 = f32[256,128,512]{2,1,0:T(8,128)} slice(f32[257,128,512]{2,1,0:T(8,128)} %scatter_fusion), slice={[0:256], [0:128], [0:512]} | slice | bytes 134217728 | tf_op jit(solution)/shard_map/slice | solution.py:70
  991.3 56.3 %copy.29 = f32[32,128,8,512]{3,2,1,0:T(8,128)} copy(f32[32,128,8,512]{3,1,2,0:T(8,128)} %bitcast.10) | data formatting | bytes 134217728 | tf_op jit(solution)/shard_map/transpose | solution.py:73
  1047.7 79.2 %reduce-scatter.3.cloned.1.call-done = f32[2048,8,512]{2,1,0:T(8,128)} async-done(((f32[4096,8,512]{2,1,0:T(8,128)}), f32[2048,8,512]{2,1,0:T(8,128)}) %reduce-scatter.3.cloned.1.call-update) | async-done | bytes 33554448 | tf_op jit(solution)/shard_map/reduce_scatter | solution.py:74
  1126.9 555.7 %reduce-scatter.5.cloned.1.call-done = f32[512,8,512]{2,1,0:T(8,128)} async-done(((f32[2048,8,512]{2,1,0:T(8,128)}), f32[512,8,512]{2,1,0:T(8,128)}) %reduce-scatter.5.cloned.1.call-update) | async-done | bytes 8388624 | tf_op jit(solution)/shard_map/reduce_scatter | solution.py:80
  (26 shorter events, 32.5 us)
Async XLA Ops:
  460.1 16.2 copy-start
  460.1 16.2 copy-start.2
  460.1 16.4 copy-start.3
  460.1 16.5 copy-start.1
  471.4 194.9 %all-to-all-start.1 = ((bf16[16,2,122880]{2,1,0:T(2,128)(2,1)}), bf16[16,2,122880]{2,1,0:T(2,128)(2,1)}, u32[]{:S(2)}, u32[]{:S(2)}) async-start(bf16[16,2,122880]{2,1,0:T(2,128)(2,1)} %reshape.290), calls=%async_computation.1 | async-start | bytes 15728640 | tf_op jit(solution)/shard_map/all_to_all | solution.py:41
  476.2 650.7 %reduce-scatter.3.cloned.1.call-start = ((), (), s32[]{:S(2)}) async-start(), calls=%async_computation.4 | async-start | bytes 100663296 | tf_op jit(solution)/shard_map/reduce_scatter | solution.py:74
  1047.6 635.0 %reduce-scatter.5.cloned.1.call-start = ((), (), s32[]{:S(2)}) async-start(), calls=%async_computation.5 | async-start | bytes 41943040 | tf_op jit(solution)/shard_map/reduce_scatter | solution.py:80
Sparse Core Ops, SparseCore 0:
  1047.7 79.1 reduce-scatter.2
  1129.3 553.2 reduce-scatter.4
where the time goes:
time: 1700 us; the launch traced here: 1690 us
  waiting for transfers between devices  824 us (48%)
  local copies, waits for them, and re-layouts  326 us (19%)
  other arithmetic  279 us (16%)
  blocking collectives  182 us (11%)
  matrix products  58.8 us (3%)
    reduce_scatter x1, waiting for transfers between devices, shards(): lax.psum_scatter(chip_share, 'vb', scatter_dimension=0, tiled=True)  556 us
    all_to_all x1, waiting for transfers between devices, shards(): lax.all_to_all(spread, ('va', 'vb'), split_axis=0, concat_axis=0, tiled=T...  189 us
    all_to_all x1, blocking collectives, shards(): lax.all_to_all(outgoing, ('va', 'vb'), split_axis=0, concat_axis=0, tiled...  182 us
    scatter-add x1, other arithmetic, shards(): jax.ops.segment_sum(pieces, target, num_segments=block_count * NOCC + 1)  105 us
    all_to_all x2, other arithmetic, shards(): lax.all_to_all(outgoing, ('va', 'vb'), split_axis=0, concat_axis=0, tiled...  95.8 us
    reduce_scatter x1, waiting for transfers between devices, shards(): lax.psum_scatter(summed.reshape(block_count * BLOCK, NOCC, tile_rows), 'p...  79.2 us
    all_to_all x1, other arithmetic, shards(): lax.all_to_all(spread, ('va', 'vb'), split_axis=0, concat_axis=0, tiled=T...  59.3 us
    transpose x1, local copies, waits for them, and re-layouts, shards(): summed.reshape(block_count, NOCC, BLOCK, tile_rows).transpose(0, 2, 1, 3)  56.3 us
  transfers between devices with their start and end apart: 3, of which 3 were waited for; matrix products, arithmetic and copies ran while one was open for 0% of the time, Pallas kernels for 0%

commit v1 on v0

v1 whole, which is shorter than its diff:
```python
import functools

import jax
import jax.numpy as jnp
from jax import lax
from jax.experimental import pallas as pl
from jax.experimental.pallas import tpu as pltpu
from jax.sharding import PartitionSpec as P

BLOCK = 128
NOCC = 8
AUX_BLK = 32
MESH = pl.DeviceIdType.MESH


def pick_energy(occ_energy, column):
    levels = jnp.arange(occ_energy.shape[0], dtype=jnp.int32)
    return jnp.sum(jnp.where(column[:, None] == levels[None, :], occ_energy[None, :], 0.0), axis=1)


def mirror_kernel(side, batches, tile, out, plane, column, s1, r1, s2, r2, s3, r3, own_sem):
    me_a = lax.axis_index("va")
    me_b = lax.axis_index("vb")
    me_p = lax.axis_index("pair")
    size = tile.shape[0] // batches

    def other(base, step):
        return lax.rem(base + step, side)

    barrier = pltpu.get_barrier_semaphore()
    for step in range(1, side):
        pl.semaphore_signal(
            barrier, inc=1, device_id=(other(me_a, step), me_b, me_p), device_id_type=MESH
        )
        pl.semaphore_signal(
            barrier, inc=1, device_id=(me_a, other(me_b, step), me_p), device_id_type=MESH
        )
    pl.semaphore_wait(barrier, 2 * (side - 1))

    def send(src, dst, send_sem, recv_sem, to_a, to_b):
        return pltpu.make_async_remote_copy(
            src_ref=src,
            dst_ref=dst,
            send_sem=send_sem,
            recv_sem=recv_sem,
            device_id=(to_a, to_b, me_p),
            device_id_type=MESH,
        )

    def span(k):
        return pl.ds(k * size, size)

    def first(k, c):
        return send(tile.at[span(k), c], plane.at[me_a, span(k)], s1.at[k, c], r1.at[k, me_a], c, me_b)

    def first_arrival(k, i):
        return send(tile.at[span(k), i], plane.at[i, span(k)], s1.at[k, i], r1.at[k, i], i, me_b)

    def second(k, i, src, direct):
        dst = out.at[span(k), me_a] if direct else column.at[me_b, span(k)]
        return send(src, dst, s2.at[k, i], r2.at[k, me_b], me_a, i)

    def second_arrival(k, j):
        return send(tile.at[span(k), j], column.at[j, span(k)], s2.at[k, j], r2.at[k, j], me_a, j)

    def third(k, j):
        return send(column.at[j, span(k)], out.at[span(k), me_a], s3.at[k, j], r3.at[k, me_a], j, me_b)

    def third_arrival(k, c):
        return send(column.at[c, span(k)], out.at[span(k), c], s3.at[k, c], r3.at[k, c], c, me_b)

    off_diagonal = me_a != me_b

    def start_first(k):
        @pl.when(off_diagonal)
        def _():
            for step in range(1, side):
                first(k, other(me_a, step)).start()

    def start_second(k):
        for step in range(1, side):
            i = other(me_b, step)

            @pl.when(i == me_a)
            def _():
                second(k, i, tile.at[span(k), me_a], False).start()

            @pl.when(i != me_a)
            def _():
                first_arrival(k, i).wait_recv()

                @pl.when(off_diagonal)
                def _():
                    second(k, i, plane.at[i, span(k)], False).start()

                @pl.when(me_a == me_b)
                def _():
                    second(k, i, plane.at[i, span(k)], True).start()

    def start_third(k):
        for step in range(1, side):
            j = other(me_b, step)
            second_arrival(k, j).wait_recv()

            @pl.when(j != me_a)
            def _():
                third(k, j).start()

    own = pltpu.make_async_copy(tile, out, own_sem)

    @pl.when(me_a == me_b)
    def _():
        own.start()

    for k in range(min(2, batches)):
        start_first(k)
    for k in range(batches + 1):
        if k < batches:
            start_second(k)
        if k + 2 < batches:
            start_first(k + 2)
        if k >= 1:
            start_third(k - 1)
    for k in range(batches):

        @pl.when(off_diagonal)
        def _():
            for step in range(1, side):
                c = other(me_a, step)
                third_arrival(k, c).wait_recv()
                first(k, c).wait_send()

        for step in range(1, side):
            i = other(me_b, step)
            second(k, i, tile.at[span(k), me_a], False).wait_send()

            @pl.when(i != me_a)
            def _():
                third(k, i).wait_send()

    @pl.when(me_a == me_b)
    def _():
        own.wait()


def mirror(tile, side):
    pairs, rows, columns = tile.shape
    batches = max(k for k in range(1, 6) if pairs % k == 0)
    strip = rows // side
    cut = jax.ShapeDtypeStruct((pairs, side, strip, columns), tile.dtype)
    held = jax.ShapeDtypeStruct((side, pairs, strip, columns), tile.dtype)
    sems = pltpu.SemaphoreType.DMA((batches, side))
    out, _, _ = pl.pallas_call(
        functools.partial(mirror_kernel, side, batches),
        out_shape=(cut, held, held),
        in_specs=[pl.BlockSpec(memory_space=pl.ANY)],
        out_specs=(pl.BlockSpec(memory_space=pl.ANY),) * 3,
        scratch_shapes=[sems] * 6 + [pltpu.SemaphoreType.DMA],
        compiler_params=pltpu.CompilerParams(collective_id=0, has_side_effects=True),
        name="mirror",
    )(tile.reshape(pairs, side, strip, columns))
    return out.reshape(pairs, rows, columns)


def contract_kernel(dom_blocks, cells, right, amplitude, keep, send, total, staged, keep_sem, send_sem):
    pair = pl.program_id(0)

    @pl.when(pair == 0)
    def _():
        @pl.loop(0, total.shape[0])
        def _(cell):
            total[cell] = jnp.zeros(total.shape[1:], total.dtype)

    for block in range(dom_blocks):
        cell = cells[pair * dom_blocks + block]
        total[cell] += lax.dot_general(
            right[0, :, block * BLOCK : (block + 1) * BLOCK],
            amplitude[0],
            (((0,), (0,)), ((), ())),
            preferred_element_type=jnp.float32,
        )

    @pl.when(pair == pl.num_programs(0) - 1)
    def _():
        half = staged.shape[0]
        keep_copy = pltpu.make_async_copy(total.at[pl.ds(0, half)], keep, keep_sem)
        keep_copy.start()

        @pl.loop(0, half)
        def _(cell):
            staged[cell] = total[half + cell].astype(staged.dtype)

        send_copy = pltpu.make_async_copy(staged, send, send_sem)
        send_copy.start()
        keep_copy.wait()
        send_copy.wait()


def contract(cells, right, amplitude, part, width, send_type):
    pairs, rows, dom = right.shape
    half = AUX_BLK * NOCC // 2
    return pl.pallas_call(
        functools.partial(contract_kernel, dom // BLOCK),
        out_shape=(
            jax.ShapeDtypeStruct((half, BLOCK, width), jnp.float32),
            jax.ShapeDtypeStruct((half, BLOCK, width), send_type),
        ),
        grid_spec=pltpu.PrefetchScalarGridSpec(
            num_scalar_prefetch=1,
            grid=(pairs,),
            in_specs=[
                pl.BlockSpec((1, rows, dom), lambda p, cells: (p, 0, 0)),
                pl.BlockSpec((1, rows, width), lambda p, cells: (p, 0, part)),
            ],
            out_specs=(pl.BlockSpec(memory_space=pl.ANY),) * 2,
            scratch_shapes=[
                pltpu.VMEM((2 * half, BLOCK, width), jnp.float32),
                pltpu.VMEM((half, BLOCK, width), send_type),
                pltpu.SemaphoreType.DMA,
                pltpu.SemaphoreType.DMA,
            ],
        ),
        compiler_params=pltpu.CompilerParams(vmem_limit_bytes=56 << 20),
        cost_estimate=pl.CostEstimate(
            flops=2 * pairs * rows * dom * width,
            bytes_accessed=2 * pairs * rows * (dom + width) + 6 * half * BLOCK * width,
            transcendentals=0,
        ),
        name="contract",
    )(cells, right, amplitude)


def reduce_owned(total_of, count):
    me = lax.axis_index("vb")
    result = total_of(me)
    arrivals = []
    for sign, hops in ((1, count // 2), (-1, (count - 1) // 2)):
        if hops == 0:
            continue
        ring = [(d, (d + sign) % count) for d in range(count)]
        running = total_of((me + sign * hops) % count).astype(jnp.bfloat16)
        for hop in range(1, hops + 1):
            running = lax.ppermute(running, "vb", ring)
            if hop < hops:
                mine = total_of((me + sign * (hops - hop)) % count)
                running = (mine + running.astype(jnp.float32)).astype(jnp.bfloat16)
        arrivals.append(running)
    for arrival in arrivals:
        result = result + arrival.astype(jnp.float32)
    return result


def shards(left_fit, right_fit, occ_energy, virt_energy, pair_list, domain_blocks):
    side = lax.axis_size("va")
    vb_count = lax.axis_size("vb")
    pair_count = lax.axis_size("pair")
    tile_rows = left_fit.shape[1]
    dom_blocks = domain_blocks.shape[1]
    va_index = lax.axis_index("va")
    vb_index = lax.axis_index("vb")
    pair_index = lax.axis_index("pair")
    energy_a = lax.dynamic_slice_in_dim(virt_energy, va_index * tile_rows, tile_rows)
    energy_b = lax.dynamic_slice_in_dim(virt_energy, vb_index * tile_rows, tile_rows)

    coulomb = jnp.einsum(
        "pak,pbk->pab", left_fit, right_fit, preferred_element_type=jnp.float32
    ).astype(jnp.bfloat16)
    swapped = mirror(coulomb, side)
    turned = jnp.swapaxes(coulomb, 1, 2)
    first_energy = pick_energy(occ_energy, pair_list[:, 0])
    second_energy = pick_energy(occ_energy, pair_list[:, 1])
    energy_gap = (
        energy_a[None, None, :] + energy_b[None, :, None] - (first_energy + second_energy)[:, None, None]
    )
    amplitude = (
        (2.0 * turned.astype(jnp.float32) - swapped.astype(jnp.float32)) / energy_gap
    ).astype(jnp.bfloat16)

    slab = AUX_BLK // (vb_count * pair_count)
    owner = domain_blocks // slab
    apart = (owner % pair_count - pair_index) % pair_count
    cells = ((apart * vb_count + owner // pair_count) * slab + domain_blocks % slab) * NOCC
    cells = (cells + pair_list[:, :1]).reshape(-1).astype(jnp.int32)

    send_type = jnp.bfloat16 if vb_count <= 4 else jnp.float32
    parts = max(1, tile_rows // 256)
    width = tile_rows // parts
    swap = [(c, (c + 1) % pair_count) for c in range(pair_count)]
    pieces = []
    for part in range(parts):
        keep, send = contract(cells, right_fit, amplitude, part, width, send_type)
        got = lax.ppermute(send, "pair", swap)
        shape = (vb_count, slab * NOCC, BLOCK, width)
        keep, got = keep.reshape(shape), got.reshape(shape)

        def total_of(owner, keep=keep, got=got):
            mine = lax.dynamic_index_in_dim(keep, owner, 0, False)
            return mine + lax.dynamic_index_in_dim(got, owner, 0, False).astype(jnp.float32)

        mine = reduce_owned(total_of, vb_count).reshape(slab, NOCC, BLOCK, width)
        pieces.append(mine.transpose(0, 2, 1, 3).reshape(slab * BLOCK, NOCC, width))
    return jnp.concatenate(pieces, axis=2)


def solution(mesh):
    return jax.shard_map(
        shards,
        mesh=mesh,
        in_specs=(
            P("pair", "va", None),
            P("pair", "vb", None),
            P(),
            P(),
            P("pair", None),
            P("pair", None),
        ),
        out_specs=P(("vb", "pair"), None, "va"),
        check_vma=False,
    )
```

time: 1700 us -> 658 us (0.39)
  waiting for transfers between devices: 824 us -> 253 us
  local copies, waits for them, and re-layouts: 326 us -> 19.4 us
  Pallas kernels: 0 us -> 303 us
  other arithmetic: 279 us -> 55 us
  blocking collectives: 182 us -> 0 us
  matrix products: 58.8 us -> 22.9 us
    reduce_scatter x2 -> x0, waiting for transfers between devices: 635 us -> none  [the longest x1 556 us: shards(): lax.psum_scatter(chip_share, 'vb', scatter_dimension=0, tiled=True)]
    pallas_call x0 -> x3, Pallas kernels: none -> 303 us  [the longest x1 245 us: mirror(): pl.pallas_call(functools.partial(mirror_kernel, side, batches), out_shape...]
    ppermute x0 -> x8, waiting for transfers between devices: none -> 253 us  [the longest x6 247 us: reduce_owned(): running = lax.ppermute(running, 'vb', ring)]
    all_to_all x1 -> x0, waiting for transfers between devices: 189 us -> none  [shards(): lax.all_to_all(spread, ('va', 'vb'), split_axis=0, concat_axis=0, tiled=T...]
    all_to_all x1 -> x0, blocking collectives: 182 us -> none  [shards(): lax.all_to_all(outgoing, ('va', 'vb'), split_axis=0, concat_axis=0, tiled...]
    all_to_all x3 -> x0, other arithmetic: 155 us -> none  [the longest x2 95.8 us: shards(): lax.all_to_all(outgoing, ('va', 'vb'), split_axis=0, concat_axis=0, tiled...]
    scatter-add x1 -> x0, other arithmetic: 105 us -> none  [shards(): jax.ops.segment_sum(pieces, target, num_segments=block_count * NOCC + 1)]
    transpose x2 -> x0, local copies, waits for them, and re-layouts: 67.7 us -> none  [the longest x1 56.3 us: shards(): summed.reshape(block_count, NOCC, BLOCK, tile_rows).transpose(0, 2, 1, 3)]
  transfers between devices with their start and end apart: 3 -> 8, of which waited for: 3 -> 7; matrix products, arithmetic and copies ran while one was open for 0% -> 4% of each run, Pallas kernels for 0% -> 4%
where the time goes in v1:
time: 658 us; the launch traced here: 657 us
  Pallas kernels  303 us (46%)
  waiting for transfers between devices  253 us (38%)
  other arithmetic  55 us (8%)
  matrix products  22.9 us (3%)
  local copies, waits for them, and re-layouts  19.4 us (3%)
    ppermute x6, waiting for transfers between devices, reduce_owned(): running = lax.ppermute(running, 'vb', ring)  247 us
    pallas_call x1, Pallas kernels, mirror(): pl.pallas_call(functools.partial(mirror_kernel, side, batches), out_shape...  245 us
    pallas_call x2, Pallas kernels, contract(): pl.pallas_call(functools.partial(contract_kernel, dom // BLOCK), out_shap...  57.3 us
    dot_general x1, matrix products, shards(): jnp.einsum('pak,pbk->pab', left_fit, right_fit, preferred_element_type=jn...  22.9 us
    convert_element_type x2, other arithmetic, reduce_owned(): running = total_of((me + sign * hops) % count).astype(jnp.bfloat16)  13.7 us
    add x1, other arithmetic, reduce_owned(): result = result + arrival.astype(jnp.float32)  13.7 us
  transfers between devices with their start and end apart: 8, of which 7 were waited for; matrix products, arithmetic and copies ran while one was open for 4% of the time, Pallas kernels for 4%

profile of v1, /device:TPU:0, one launch (start us, length us, event | category | flops | bytes accessed | tf_op | source)
XLA Modules:
  0.0 657.4 jit_solution(14973053469715179772)
XLA Ops:
  0.0 0.8 slice_bitcast_fusion
  0.8 0.8 fusion.17
  2.2 22.9 %convolution_convert_fusion = bf16[15,512,512]{1,2,0:T(8,128)(2,1)} fusion(bf16[15,512,1536]{2,1,0:T(8,128)(2,1)} %param.6, bf16[15,512,1536]{2,1,0:T(8,128)(2,1)} %right.3), kind=kOutput, calls=%fused_computation.4 | convolution fusion | flops 12083527680 | bytes 55050240 | tf_op jit(solution)/shard_map/pak,pbk->pab/dot_general | solution.py:265
  25.1 10.7 %copy.16 = bf16[15,512,512]{2,1,0:T(8,128)(2,1)} copy(bf16[15,512,512]{1,2,0:T(8,128)(2,1)} %convolution_convert_fusion) | data formatting | bytes 15728640 | tf_op jit(solution)/shard_map/reshape | solution.py:161
  35.7 245.5 %mirror.1 = (bf16[15,4,128,512]{3,2,1,0:T(8,128)(2,1)}, bf16[4,15,128,512]{3,2,1,0:T(8,128)(2,1)}, bf16[4,15,128,512]{3,2,1,0:T(8,128)(2,1)}) custom-call(bf16[15,4,128,512]{3,2,1,0:T(8,128)(2,1)} %bitcast.48), custom_call_target="tpu_custom_call" | custom-call | tf_op jit(solution)/shard_map/mirror/pallas_call | solution.py:153
  281.5 10.2 %fusion.1.amplitude = bf16[15,512,512]{2,1,0:T(8,128)(2,1)} fusion(bf16[15,512,512]{1,2,0:T(8,128)(2,1)} %convolution_convert_fusion, bf16[15,4,128,512]{3,2,1,0:T(8,128)(2,1)} %get-tuple-element.10, f32[15]{0:T(128)S(1)} %add.185, f32[512,512]{1,0:T(8,128)S(1)} %broadcast_add_fusion), kind=kLoop, calls=%fused_computation.2 | loop fusion | flops 27525120 | bytes 24641596 | tf_op jit(solution)/shard_map/convert_element_type | solution.py:277
  291.7 29.0 %contract.3 = (f32[128,128,256]{2,1,0:T(8,128)}, bf16[128,128,256]{2,1,0:T(8,128)(2,1)}) custom-call(s32[180]{0:T(256)} %reshape.91.cells, bf16[15,512,1536]{2,1,0:T(8,128)(2,1)} %right.3, bf16[15,512,512]{2,1,0:T(8,128)(2,1)} %fusion.1.amplitude), custom_call_target="tpu_custom_call" | custom-call | flops 6039797760 | bytes 52690944 | tf_op jit(solution)/shard_map/contract/pallas_call | solution.py:202
  320.8 28.3 %contract.2 = (f32[128,128,256]{2,1,0:T(8,128)}, bf16[128,128,256]{2,1,0:T(8,128)(2,1)}) custom-call(s32[180]{0:T(256)} %reshape.91.cells, bf16[15,512,1536]{2,1,0:T(8,128)(2,1)} %right.3, bf16[15,512,512]{2,1,0:T(8,128)(2,1)} %fusion.1.amplitude), custom_call_target="tpu_custom_call" | custom-call | flops 6039797760 | bytes 52690944 | tf_op jit(solution)/shard_map/contract/pallas_call | solution.py:202
  349.7 7.6 %fusion.8 = (bf16[32,128,256]{2,1,0:T(8,128)(2,1)}, bf16[32,128,256]{2,1,0:T(8,128)(2,1)S(1)}) fusion(f32[4,32,128,256]{3,2,1,0:T(8,128)} %bitcast.49, s32[]{:T(128)S(6)} %select_n.95, bf16[4,32,128,256]{3,2,1,0:T(8,128)(2,1)} %bitcast.15, s32[]{:T(128)S(6)} %select_n.97), kind=kLoop, calls=%fused_computation.19 | loop fusion | flops 6291456 | bytes 16777224 | tf_op jit(solution)/shard_map/convert_element_type | solution.py:241
  357.3 5.5 collective-permute-done
  362.8 6.1 fusion.6
  369.0 3.8 collective-permute-start.7
  372.8 35.2 %collective-permute-done.5 = bf16[32,128,256]{2,1,0:T(8,128)(2,1)} collective-permute-done((bf16[32,128,256]{2,1,0:T(8,128)(2,1)}, bf16[32,128,256]{2,1,0:T(8,128)(2,1)}, u32[]{:S(2)}, u32[]{:S(2)}) %collective-permute-start.5) | collective-permute-done | bytes 2097184 | tf_op jit(solution)/shard_map/ppermute | solution.py:243
  408.1 5.8 fusion.2
  413.9 39.0 %collective-permute-done.1 = bf16[32,128,256]{2,1,0:T(8,128)(2,1)} collective-permute-done((bf16[32,128,256]{2,1,0:T(8,128)(2,1)}, bf16[32,128,256]{2,1,0:T(8,128)(2,1)}, u32[]{:S(2)}, u32[]{:S(2)}) %collective-permute-start.1) | collective-permute-done | bytes 2097184 | tf_op jit(solution)/shard_map/ppermute | solution.py:243
  452.9 5.9 fusion.4
  458.7 38.3 %collective-permute-done.7 = bf16[32,128,256]{2,1,0:T(8,128)(2,1)} collective-permute-done((bf16[32,128,256]{2,1,0:T(8,128)(2,1)S(1)}, bf16[32,128,256]{2,1,0:T(8,128)(2,1)}, u32[]{:S(2)}, u32[]{:S(2)}) %collective-permute-start.7) | collective-permute-done | bytes 2097184 | tf_op jit(solution)/shard_map/ppermute | solution.py:243
  497.0 45.8 %collective-permute-done.3 = bf16[32,128,256]{2,1,0:T(8,128)(2,1)} collective-permute-done((bf16[32,128,256]{2,1,0:T(8,128)(2,1)}, bf16[32,128,256]{2,1,0:T(8,128)(2,1)}, u32[]{:S(2)}, u32[]{:S(2)}) %collective-permute-start.3) | collective-permute-done | bytes 2097184 | tf_op jit(solution)/shard_map/ppermute | solution.py:243
  542.8 44.9 %collective-permute-done.6 = bf16[32,128,256]{2,1,0:T(8,128)(2,1)} collective-permute-done((bf16[32,128,256]{2,1,0:T(8,128)(2,1)}, bf16[32,128,256]{2,1,0:T(8,128)(2,1)}, u32[]{:S(2)}, u32[]{:S(2)}) %collective-permute-start.6) | collective-permute-done | bytes 2097184 | tf_op jit(solution)/shard_map/ppermute | solution.py:243
  587.7 44.1 %collective-permute-done.2 = bf16[32,128,256]{2,1,0:T(8,128)(2,1)} collective-permute-done((bf16[32,128,256]{2,1,0:T(8,128)(2,1)}, bf16[32,128,256]{2,1,0:T(8,128)(2,1)}, u32[]{:S(2)}, u32[]{:S(2)}) %collective-permute-start.2) | collective-permute-done | bytes 2097184 | tf_op jit(solution)/shard_map/ppermute | solution.py:243
  631.8 13.7 %fusion.3 = (f32[32,128,256]{2,1,0:T(8,128)}, f32[32,128,256]{2,1,0:T(8,128)}) fusion(bf16[32,128,256]{2,1,0:T(8,128)(2,1)} %collective-permute-done.7, bf16[32,128,256]{2,1,0:T(8,128)(2,1)} %collective-permute-done.6, f32[4,32,128,256]{3,2,1,0:T(8,128)} %bitcast.51, s32[]{:T(128)S(6)} %select_n.91, bf16[4,32,128,256]{3,2,1,0:T(8,128)(2,1)} %bitcast.15, ...), kind=kLoop, calls=%fused_computation.8 | loop fusion | flops 12582912 | bytes 29360132 | tf_op jit(solution)/shard_map/add | solution.py:249
  645.5 4.8 copy.14
  650.3 2.4 copy.13
  652.7 4.7 pad_maximum_fusion
  (21 shorter events, 1.7 us)
Async XLA Ops:
  35.7 245.5 %copy-start.3 = (f32[8]{0:T(128)S(1)}, f32[8]{0:T(128)}, u32[]{:S(2)}) copy-start(f32[8]{0:T(128)} %param.8) | copy-start | bytes 100
  35.7 245.6 %copy-start.2 = (f32[2048]{0:T(1024)S(1)}, f32[2048]{0:T(1024)}, u32[]{:S(2)}) copy-start(f32[2048]{0:T(1024)} %param.9) | copy-start | bytes 24580
  320.7 29.0 %collective-permute-start.4 = (bf16[128,128,256]{2,1,0:T(8,128)(2,1)}, bf16[128,128,256]{2,1,0:T(8,128)(2,1)}, u32[]{:S(2)}, u32[]{:S(2)}) collective-permute-start(bf16[128,128,256]{2,1,0:T(8,128)(2,1)} %get-tuple-element.14), channel_id=1, source_target_pairs={{0,1},{1,0},{2,3},{3,2},{4,5},{5,4},{6,7},{7,6},{8,9},{9,8},{10,11... | collective-permute-start | bytes 25165832 | tf_op jit(solution)/shard_map/ppermute | solution.py:292
  349.1 13.7 %collective-permute-start = (bf16[128,128,256]{2,1,0:T(8,128)(2,1)}, bf16[128,128,256]{2,1,0:T(8,128)(2,1)}, u32[]{:S(2)}, u32[]{:S(2)}) collective-permute-start(bf16[128,128,256]{2,1,0:T(8,128)(2,1)} %get-tuple-element.12), channel_id=1, source_target_pairs={{0,1},{1,0},{2,3},{3,2},{4,5},{5,4},{6,7},{7,6},{8,9},{9,8},{10,11... | collective-permute-start | bytes 25165832 | tf_op jit(solution)/shard_map/ppermute | solution.py:292
  349.7 13.1 %copy-start = (f32[128,128,256]{2,1,0:T(8,128)S(1)}, f32[128,128,256]{2,1,0:T(8,128)}, u32[]{:S(2)}) copy-start(f32[128,128,256]{2,1,0:T(8,128)} %get-tuple-element.11) | copy-start | bytes 50331652
  357.3 50.8 %collective-permute-start.5 = (bf16[32,128,256]{2,1,0:T(8,128)(2,1)}, bf16[32,128,256]{2,1,0:T(8,128)(2,1)}, u32[]{:S(2)}, u32[]{:S(2)}) collective-permute-start(bf16[32,128,256]{2,1,0:T(8,128)(2,1)} %get-tuple-element.19), channel_id=1, source_target_pairs={{0,2},{2,4},{4,6},{6,0},{1,3},{3,5},{5,7},{7,1},{8,10},{10,12},{12... | collective-permute-start | bytes 6291464 | tf_op jit(solution)/shard_map/ppermute | solution.py:243
  369.0 83.9 %collective-permute-start.1 = (bf16[32,128,256]{2,1,0:T(8,128)(2,1)}, bf16[32,128,256]{2,1,0:T(8,128)(2,1)}, u32[]{:S(2)}, u32[]{:S(2)}) collective-permute-start(bf16[32,128,256]{2,1,0:T(8,128)(2,1)} %get-tuple-element.17), channel_id=1, source_target_pairs={{0,2},{2,4},{4,6},{6,0},{1,3},{3,5},{5,7},{7,1},{8,10},{10,12},{12... | collective-permute-start | bytes 6291464 | tf_op jit(solution)/shard_map/ppermute | solution.py:243
  369.0 128.1 %collective-permute-start.7 = (bf16[32,128,256]{2,1,0:T(8,128)(2,1)S(1)}, bf16[32,128,256]{2,1,0:T(8,128)(2,1)}, u32[]{:S(2)}, u32[]{:S(2)}) collective-permute-start(bf16[32,128,256]{2,1,0:T(8,128)(2,1)S(1)} %get-tuple-element.20), channel_id=1, source_target_pairs={{0,6},{2,0},{4,2},{6,4},{1,7},{3,1},{5,3},{7,5},{8,14},{10,8},{12,... | collective-permute-start | bytes 6291464 | tf_op jit(solution)/shard_map/ppermute | solution.py:243
  372.8 170.0 %collective-permute-start.3 = (bf16[32,128,256]{2,1,0:T(8,128)(2,1)}, bf16[32,128,256]{2,1,0:T(8,128)(2,1)}, u32[]{:S(2)}, u32[]{:S(2)}) collective-permute-start(bf16[32,128,256]{2,1,0:T(8,128)(2,1)} %get-tuple-element.18), channel_id=1, source_target_pairs={{0,6},{2,0},{4,2},{6,4},{1,7},{3,1},{5,3},{7,5},{8,14},{10,8},{12,... | collective-permute-start | bytes 6291464 | tf_op jit(solution)/shard_map/ppermute | solution.py:243
  413.8 173.9 %collective-permute-start.6 = (bf16[32,128,256]{2,1,0:T(8,128)(2,1)}, bf16[32,128,256]{2,1,0:T(8,128)(2,1)}, u32[]{:S(2)}, u32[]{:S(2)}) collective-permute-start(bf16[32,128,256]{2,1,0:T(8,128)(2,1)} %fusion.2), channel_id=1, source_target_pairs={{0,2},{2,4},{4,6},{6,0},{1,3},{3,5},{5,7},{7,1},{8,10},{10,12},{12... | collective-permute-start | bytes 6291464 | tf_op jit(solution)/shard_map/ppermute | solution.py:243
  458.7 173.0 %collective-permute-start.2 = (bf16[32,128,256]{2,1,0:T(8,128)(2,1)}, bf16[32,128,256]{2,1,0:T(8,128)(2,1)}, u32[]{:S(2)}, u32[]{:S(2)}) collective-permute-start(bf16[32,128,256]{2,1,0:T(8,128)(2,1)} %fusion.4), channel_id=1, source_target_pairs={{0,2},{2,4},{4,6},{6,0},{1,3},{3,5},{5,7},{7,1},{8,10},{10,12},{12... | collective-permute-start | bytes 6291464 | tf_op jit(solution)/shard_map/ppermute | solution.py:243
  645.5 4.8 copy-start.1

commit v2 on v1

v2 whole, which is shorter than its diff:
```python
import functools

import jax
import jax.numpy as jnp
from jax import lax
from jax.experimental import pallas as pl
from jax.experimental.pallas import tpu as pltpu
from jax.sharding import PartitionSpec as P

BLOCK = 128
NOCC = 8
AUX_BLK = 32


def pick_energy(occ_energy, column):
    levels = jnp.arange(occ_energy.shape[0], dtype=jnp.int32)
    return jnp.sum(jnp.where(column[:, None] == levels[None, :], occ_energy[None, :], 0.0), axis=1)


def pick(stack, index):
    return lax.dynamic_index_in_dim(stack, index, 0, False)


def partners(side, step):
    return [(d, d ^ step) for d in range(side)]


def mirror(tile, side):
    pairs, rows, columns = tile.shape
    me_a = lax.axis_index("va")
    me_b = lax.axis_index("vb")
    strips = tile.reshape(pairs, side, rows // side, columns)

    def strip(index):
        return lax.dynamic_index_in_dim(strips, index, 1, False)

    def leg(get, axis):
        held = [get(0)]
        for step in range(1, side):
            held.append(lax.ppermute(get(step), axis, partners(side, step)))
        return jnp.stack(held)

    plane = leg(lambda step: strip(me_a ^ step), "va")
    column = leg(lambda step: pick(plane, me_a ^ me_b ^ step), "vb")
    back = leg(lambda step: pick(column, me_a ^ me_b ^ step), "va")
    ordered = [pick(back, me_a ^ c) for c in range(side)]
    return jnp.stack(ordered, axis=1).reshape(pairs, rows, columns)


def contract_kernel(dom_blocks, cells, right, amplitude, keep, send, total, staged, keep_sem, send_sem):
    pair = pl.program_id(0)

    @pl.when(pair == 0)
    def _():
        @pl.loop(0, total.shape[0])
        def _(cell):
            total[cell] = jnp.zeros(total.shape[1:], total.dtype)

    for block in range(dom_blocks):
        cell = cells[pair * dom_blocks + block]
        total[cell] += lax.dot_general(
            right[0, :, block * BLOCK : (block + 1) * BLOCK],
            amplitude[0],
            (((0,), (0,)), ((), ())),
            preferred_element_type=jnp.float32,
        )

    @pl.when(pair == pl.num_programs(0) - 1)
    def _():
        half = staged.shape[0]
        keep_copy = pltpu.make_async_copy(total.at[pl.ds(0, half)], keep, keep_sem)
        keep_copy.start()

        @pl.loop(0, half)
        def _(cell):
            staged[cell] = total[half + cell].astype(staged.dtype)

        send_copy = pltpu.make_async_copy(staged, send, send_sem)
        send_copy.start()
        keep_copy.wait()
        send_copy.wait()


def contract(cells, right, amplitude, send_type):
    pairs, rows, dom = right.shape
    width = amplitude.shape[2]
    half = AUX_BLK * NOCC // 2
    return pl.pallas_call(
        functools.partial(contract_kernel, dom // BLOCK),
        out_shape=(
            jax.ShapeDtypeStruct((half, BLOCK, width), jnp.float32),
            jax.ShapeDtypeStruct((half, BLOCK, width), send_type),
        ),
        grid_spec=pltpu.PrefetchScalarGridSpec(
            num_scalar_prefetch=1,
            grid=(pairs,),
            in_specs=[
                pl.BlockSpec((1, rows, dom), lambda p, cells: (p, 0, 0)),
                pl.BlockSpec((1, rows, width), lambda p, cells: (p, 0, 0)),
            ],
            out_specs=(pl.BlockSpec(memory_space=pl.ANY),) * 2,
            scratch_shapes=[
                pltpu.VMEM((2 * half, BLOCK, width), jnp.float32),
                pltpu.VMEM((half, BLOCK, width), send_type),
                pltpu.SemaphoreType.DMA,
                pltpu.SemaphoreType.DMA,
            ],
        ),
        compiler_params=pltpu.CompilerParams(vmem_limit_bytes=56 << 20),
        cost_estimate=pl.CostEstimate(
            flops=2 * pairs * rows * dom * width,
            bytes_accessed=2 * pairs * rows * (dom + width) + 6 * half * BLOCK * width,
            transcendentals=0,
        ),
        name="contract",
    )(cells, right, amplitude)


def reduce_owned(total_of, count):
    me = lax.axis_index("vb")
    result = total_of(me)
    arrivals = []
    for sign, hops in ((1, count // 2), (-1, (count - 1) // 2)):
        if hops == 0:
            continue
        ring = [(d, (d + sign) % count) for d in range(count)]
        running = total_of((me + sign * hops) % count).astype(jnp.bfloat16)
        for hop in range(1, hops + 1):
            running = lax.ppermute(running, "vb", ring)
            if hop < hops:
                mine = total_of((me + sign * (hops - hop)) % count)
                running = (mine + running.astype(jnp.float32)).astype(jnp.bfloat16)
        arrivals.append(running)
    for arrival in arrivals:
        result = result + arrival.astype(jnp.float32)
    return result


def shards(left_fit, right_fit, occ_energy, virt_energy, pair_list, domain_blocks):
    side = lax.axis_size("va")
    vb_count = lax.axis_size("vb")
    pair_count = lax.axis_size("pair")
    tile_rows = left_fit.shape[1]
    dom_blocks = domain_blocks.shape[1]
    va_index = lax.axis_index("va")
    vb_index = lax.axis_index("vb")
    pair_index = lax.axis_index("pair")
    energy_a = lax.dynamic_slice_in_dim(virt_energy, va_index * tile_rows, tile_rows)
    energy_b = lax.dynamic_slice_in_dim(virt_energy, vb_index * tile_rows, tile_rows)

    parts = max(1, tile_rows // 256)
    width = tile_rows // parts
    first_energy = pick_energy(occ_energy, pair_list[:, 0])
    second_energy = pick_energy(occ_energy, pair_list[:, 1])
    pair_energy = (first_energy + second_energy)[:, None, None]
    tiles = []
    for part in range(parts):
        columns = right_fit[:, part * width : (part + 1) * width]
        tile = jnp.einsum("pak,pbk->pab", left_fit, columns, preferred_element_type=jnp.float32)
        tiles.append(tile.astype(jnp.bfloat16))
    mirrored = [mirror(tile, side) for tile in tiles]

    def amplitude_of(part):
        rows = slice(part * width, (part + 1) * width)
        turned = jnp.einsum(
            "pbk,pak->pba", right_fit, left_fit[:, rows], preferred_element_type=jnp.float32
        ).astype(jnp.bfloat16)
        energy_gap = energy_a[None, None, rows] + energy_b[None, :, None] - pair_energy
        wide = 2.0 * turned.astype(jnp.float32) - mirrored[part].astype(jnp.float32)
        return (wide / energy_gap).astype(jnp.bfloat16)

    slab = AUX_BLK // (vb_count * pair_count)
    owner = domain_blocks // slab
    apart = (owner % pair_count - pair_index) % pair_count
    cells = ((apart * vb_count + owner // pair_count) * slab + domain_blocks % slab) * NOCC
    cells = (cells + pair_list[:, :1]).reshape(-1).astype(jnp.int32)

    send_type = jnp.bfloat16 if vb_count <= 4 else jnp.float32
    swap = [(c, (c + 1) % pair_count) for c in range(pair_count)]
    pieces = []
    for part in range(parts):
        keep, send = contract(cells, right_fit, amplitude_of(part), send_type)
        got = lax.ppermute(send, "pair", swap)
        shape = (vb_count, slab * NOCC, BLOCK, width)
        keep, got = keep.reshape(shape), got.reshape(shape)

        def total_of(owner, keep=keep, got=got):
            mine = lax.dynamic_index_in_dim(keep, owner, 0, False)
            return mine + lax.dynamic_index_in_dim(got, owner, 0, False).astype(jnp.float32)

        mine = reduce_owned(total_of, vb_count).reshape(slab, NOCC, BLOCK, width)
        pieces.append(mine.transpose(0, 2, 1, 3).reshape(slab * BLOCK, NOCC, width))
    return jnp.concatenate(pieces, axis=2)


def solution(mesh):
    return jax.shard_map(
        shards,
        mesh=mesh,
        in_specs=(
            P("pair", "va", None),
            P("pair", "vb", None),
            P(),
            P(),
            P("pair", None),
            P("pair", None),
        ),
        out_specs=P(("vb", "pair"), None, "va"),
        check_vma=False,
    )
```

time: 658 us -> 703 us (1.068)
  Pallas kernels: 303 us -> 57.5 us
  waiting for transfers between devices: 253 us -> 438 us
  matrix products: 22.9 us -> 73.4 us
  starting transfers between devices: 4.51 us -> 53.9 us
    pallas_call x1 -> x0, Pallas kernels: 245 us -> none  [mirror(): pl.pallas_call(functools.partial(mirror_kernel, side, batches), out_shape...]
    ppermute x0 -> x18, waiting for transfers between devices: none -> 185 us  [leg(): held.append(lax.ppermute(get(step), axis, partners(side, step)))]
    dot_general x1 -> x4, matrix products: 22.9 us -> 73.4 us  [the longest x2 40.8 us: amplitude_of(): jnp.einsum('pbk,pak->pba', right_fit, left_fit[:, rows], preferred_elemen...]
    ppermute x0 -> x18, starting transfers between devices: none -> 49 us  [leg(): held.append(lax.ppermute(get(step), axis, partners(side, step)))]
    another operation x0 -> x8, other arithmetic: none -> 13.3 us  [the longest x6 8.94 us: leg(): return jnp.stack(held)]
    reshape x1 -> x0, local copies, waits for them, and re-layouts: 10.7 us -> none  [mirror(): tile.reshape(pairs, side, strip, columns)]
    convert_element_type x1 -> x0, other arithmetic: 10.2 us -> none  [shards(): amplitude = ((2.0 * turned.astype(jnp.float32) - swapped.astype(jnp.float...]
    another operation x0 -> x4, local copies, waits for them, and re-layouts: none -> 9.31 us  [the longest x2 7.53 us: leg(): return jnp.stack(held)]
  transfers between devices with their start and end apart: 8 -> 26, of which waited for: 7 -> 17; matrix products, arithmetic and copies ran while one was open for 4% -> 12% of each run, Pallas kernels for 4% -> 4%
where the time goes in v2:
time: 703 us
  waiting for transfers between devices  438 us (62%)
  matrix products  73.4 us (10%)
  other arithmetic  58.2 us (8%)
  Pallas kernels  57.5 us (8%)
  starting transfers between devices  53.9 us (8%)
  local copies, waits for them, and re-layouts  21.5 us (3%)
    ppermute x6, waiting for transfers between devices, reduce_owned(): running = lax.ppermute(running, 'vb', ring)  247 us
    ppermute x18, waiting for transfers between devices, leg(): held.append(lax.ppermute(get(step), axis, partners(side, step)))  185 us
    pallas_call x2, Pallas kernels, contract(): pl.pallas_call(functools.partial(contract_kernel, dom // BLOCK), out_shap...  57.5 us
    ppermute x18, starting transfers between devices, leg(): held.append(lax.ppermute(get(step), axis, partners(side, step)))  49 us
    dot_general x2, matrix products, amplitude_of(): jnp.einsum('pbk,pak->pba', right_fit, left_fit[:, rows], preferred_elemen...  40.8 us
    dot_general x2, matrix products, shards(): jnp.einsum('pak,pbk->pab', left_fit, columns, preferred_element_type=jnp....  32.7 us
  transfers between devices with their start and end apart: 26, of which 17 were waited for; matrix products, arithmetic and copies ran while one was open for 12% of the time, Pallas kernels for 4%

profile of v2, /device:TPU:0, one launch (start us, length us, event | category | flops | bytes accessed | tf_op | source)
XLA Modules:
  0.0 702.6 jit_solution(6004613500180251836)
XLA Ops:
  0.0 16.3 %fusion.18 = bf16[15,512,256]{2,1,0:T(8,128)(2,1)} fusion(bf16[15,512,1536]{2,1,0:T(8,128)(2,1)} %param.6, bf16[15,512,1536]{2,1,0:T(8,128)(2,1)} %right.3), kind=kOutput, calls=%fused_computation.35 | convolution fusion | flops 6041763840 | bytes 39321600 | tf_op jit(solution)/shard_map/pak,pbk->pab/dot_general | solution.py:159
  24.6 16.3 %fusion.23 = bf16[15,512,256]{2,1,0:T(8,128)(2,1)} fusion(bf16[15,512,1536]{2,1,0:T(8,128)(2,1)} %param.6, bf16[15,512,1536]{2,1,0:T(8,128)(2,1)} %right.3), kind=kOutput, calls=%fused_computation.36 | convolution fusion | flops 6041763840 | bytes 39321600 | tf_op jit(solution)/shard_map/pak,pbk->pab/dot_general | solution.py:159
  49.0 19.1 %collective-permute-done.1 = bf16[15,128,256]{2,1,0:T(8,128)(2,1)} collective-permute-done((bf16[15,128,256]{2,1,0:T(8,128)(2,1)}, bf16[15,128,256]{2,1,0:T(8,128)(2,1)}, u32[]{:S(2)}, u32[]{:S(2)}) %collective-permute-start.1) | collective-permute-done | bytes 983072 | tf_op jit(solution)/shard_map/ppermute | solution.py:40
  74.8 14.3 %collective-permute-done.15 = bf16[15,128,256]{2,1,0:T(8,128)(2,1)} collective-permute-done((bf16[15,128,256]{2,1,0:T(8,128)(2,1)}, bf16[15,128,256]{2,1,0:T(8,128)(2,1)}, u32[]{:S(2)}, u32[]{:S(2)}) %collective-permute-start.15) | collective-permute-done | bytes 983072 | tf_op jit(solution)/shard_map/ppermute | solution.py:40
  91.2 18.0 %collective-permute-done.14 = bf16[15,128,256]{2,1,0:T(8,128)(2,1)} collective-permute-done((bf16[15,128,256]{2,1,0:T(8,128)(2,1)}, bf16[15,128,256]{2,1,0:T(8,128)(2,1)}, u32[]{:S(2)}, u32[]{:S(2)}) %collective-permute-start.14) | collective-permute-done | bytes 983072 | tf_op jit(solution)/shard_map/ppermute | solution.py:40
  116.6 23.8 %collective-permute-start.16 = (bf16[15,128,256]{2,1,0:T(8,128)(2,1)}, bf16[15,128,256]{2,1,0:T(8,128)(2,1)}, u32[]{:S(2)}, u32[]{:S(2)}) collective-permute-start(bf16[15,128,256]{2,1,0:T(8,128)(2,1)} %get-tuple-element.46), channel_id=1, source_target_pairs={{0,2},{2,0},{4,6},{6,4},{1,3},{3,1},{5,7},{7,5},{8,10},{10,8},{12,... | collective-permute-start | bytes 2949128 | tf_op jit(solution)/shard_map/ppermute | solution.py:40
  140.4 61.6 %collective-permute-done.4 = bf16[15,128,256]{2,1,0:T(8,128)(2,1)S(1)} collective-permute-done((bf16[15,128,256]{2,1,0:T(8,128)(2,1)S(1)}, bf16[15,128,256]{2,1,0:T(8,128)(2,1)S(1)}, u32[]{:S(2)}, u32[]{:S(2)}) %collective-permute-start.4) | collective-permute-done | bytes 983072 | tf_op jit(solution)/shard_map/ppermute | solution.py:40
  208.6 34.7 %collective-permute-done.17 = bf16[15,128,256]{2,1,0:T(8,128)(2,1)} collective-permute-done((bf16[15,128,256]{2,1,0:T(8,128)(2,1)}, bf16[15,128,256]{2,1,0:T(8,128)(2,1)}, u32[]{:S(2)}, u32[]{:S(2)}) %collective-permute-start.17) | collective-permute-done | bytes 983072 | tf_op jit(solution)/shard_map/ppermute | solution.py:40
  253.6 17.7 %collective-permute-done.21 = bf16[15,128,256]{2,1,0:T(8,128)(2,1)S(1)} collective-permute-done((bf16[15,128,256]{2,1,0:T(8,128)(2,1)S(1)}, bf16[15,128,256]{2,1,0:T(8,128)(2,1)S(1)}, u32[]{:S(2)}, u32[]{:S(2)}) %collective-permute-start.21) | collective-permute-done | bytes 983072 | tf_op jit(solution)/shard_map/ppermute | solution.py:40
  271.4 19.2 %collective-permute-done.20 = bf16[15,128,256]{2,1,0:T(8,128)(2,1)S(1)} collective-permute-done((bf16[15,128,256]{2,1,0:T(8,128)(2,1)S(1)}, bf16[15,128,256]{2,1,0:T(8,128)(2,1)S(1)}, u32[]{:S(2)}, u32[]{:S(2)}) %collective-permute-start.20) | collective-permute-done | bytes 983072 | tf_op jit(solution)/shard_map/ppermute | solution.py:40
  293.8 20.5 %fusion.9.amplitude = bf16[15,512,256]{2,1,0:T(8,128)(2,1)} fusion(bf16[15,4,128,256]{3,2,1,0:T(8,128)(2,1)} %pad_maximum_fusion.8, f32[512,256]{1,0:T(8,128)} %get-tuple-element.54, f32[15]{0:T(128)S(1)} %add.259, bf16[15,512,1536]{2,1,0:T(8,128)(2,1)} %right.3, bf16[15,512,1536]{2,1,0:T(8,128)(2,1)} %param.6), kind=kOutput, calls=%fused_computation.11 | convolution fusion | flops 6055526400 | bytes 43778108 | tf_op jit(solution)/shard_map/pbk,pak->pba/dot_general | solution.py:165
  314.3 29.1 %contract.3 = (f32[128,128,256]{2,1,0:T(8,128)}, bf16[128,128,256]{2,1,0:T(8,128)(2,1)}) custom-call(s32[180]{0:T(256)} %reshape.135.cells, bf16[15,512,1536]{2,1,0:T(8,128)(2,1)} %right.3, bf16[15,512,256]{2,1,0:T(8,128)(2,1)} %fusion.9.amplitude), custom_call_target="tpu_custom_call" | custom-call | flops 6039797760 | bytes 52690944 | tf_op jit(solution)/shard_map/contract/pallas_call | solution.py:88
  345.8 20.3 %fusion.11.amplitude = bf16[15,512,256]{2,1,0:T(8,128)(2,1)} fusion(bf16[15,4,128,256]{3,2,1,0:T(8,128)(2,1)} %pad_maximum_fusion.4, f32[15]{0:T(128)S(1)} %add.259, f32[512,256]{1,0:T(8,128)S(1)} %get-tuple-element.53, bf16[15,512,1536]{2,1,0:T(8,128)(2,1)} %right.3, bf16[15,512,1536]{2,1,0:T(8,128)(2,1)} %param.6), kind=kOutput, calls=%fused_computation.14 | convolution fusion | flops 6055526400 | bytes 43778108 | tf_op jit(solution)/shard_map/pbk,pak->pba/dot_general | solution.py:165
  366.0 28.3 %contract.2 = (f32[128,128,256]{2,1,0:T(8,128)}, bf16[128,128,256]{2,1,0:T(8,128)(2,1)}) custom-call(s32[180]{0:T(256)} %reshape.135.cells, bf16[15,512,1536]{2,1,0:T(8,128)(2,1)} %right.3, bf16[15,512,256]{2,1,0:T(8,128)(2,1)} %fusion.11.amplitude), custom_call_target="tpu_custom_call" | custom-call | flops 6039797760 | bytes 52690944 | tf_op jit(solution)/shard_map/contract/pallas_call | solution.py:88
  394.9 7.6 %fusion.28 = (bf16[32,128,256]{2,1,0:T(8,128)(2,1)}, bf16[32,128,256]{2,1,0:T(8,128)(2,1)S(1)}) fusion(f32[4,32,128,256]{3,2,1,0:T(8,128)} %bitcast.126, s32[]{:T(128)S(6)} %select_n.153, bf16[4,32,128,256]{3,2,1,0:T(8,128)(2,1)} %bitcast.62, s32[]{:T(128)S(6)} %select_n.155), kind=kLoop, calls=%fused_computation.39 | loop fusion | flops 6291456 | bytes 16777224 | tf_op jit(solution)/shard_map/convert_element_type | solution.py:127
  408.0 6.2 fusion.26
  418.5 34.8 %collective-permute-done.23 = bf16[32,128,256]{2,1,0:T(8,128)(2,1)} collective-permute-done((bf16[32,128,256]{2,1,0:T(8,128)(2,1)}, bf16[32,128,256]{2,1,0:T(8,128)(2,1)}, u32[]{:S(2)}, u32[]{:S(2)}) %collective-permute-start.23) | collective-permute-done | bytes 2097184 | tf_op jit(solution)/shard_map/ppermute | solution.py:129
  459.0 39.0 %collective-permute-done.10 = bf16[32,128,256]{2,1,0:T(8,128)(2,1)} collective-permute-done((bf16[32,128,256]{2,1,0:T(8,128)(2,1)}, bf16[32,128,256]{2,1,0:T(8,128)(2,1)}, u32[]{:S(2)}, u32[]{:S(2)}) %collective-permute-start.10) | collective-permute-done | bytes 2097184 | tf_op jit(solution)/shard_map/ppermute | solution.py:129
  498.1 5.8 fusion.14
  503.9 38.3 %collective-permute-done.25 = bf16[32,128,256]{2,1,0:T(8,128)(2,1)} collective-permute-done((bf16[32,128,256]{2,1,0:T(8,128)(2,1)S(1)}, bf16[32,128,256]{2,1,0:T(8,128)(2,1)}, u32[]{:S(2)}, u32[]{:S(2)}) %collective-permute-start.25) | collective-permute-done | bytes 2097184 | tf_op jit(solution)/shard_map/ppermute | solution.py:129
  542.1 45.7 %collective-permute-done.12 = bf16[32,128,256]{2,1,0:T(8,128)(2,1)} collective-permute-done((bf16[32,128,256]{2,1,0:T(8,128)(2,1)}, bf16[32,128,256]{2,1,0:T(8,128)(2,1)}, u32[]{:S(2)}, u32[]{:S(2)}) %collective-permute-start.12) | collective-permute-done | bytes 2097184 | tf_op jit(solution)/shard_map/ppermute | solution.py:129
  587.9 45.0 %collective-permute-done.24 = bf16[32,128,256]{2,1,0:T(8,128)(2,1)} collective-permute-done((bf16[32,128,256]{2,1,0:T(8,128)(2,1)}, bf16[32,128,256]{2,1,0:T(8,128)(2,1)}, u32[]{:S(2)}, u32[]{:S(2)}) %collective-permute-start.24) | collective-permute-done | bytes 2097184 | tf_op jit(solution)/shard_map/ppermute | solution.py:129
  632.9 44.1 %collective-permute-done.11 = bf16[32,128,256]{2,1,0:T(8,128)(2,1)} collective-permute-done((bf16[32,128,256]{2,1,0:T(8,128)(2,1)}, bf16[32,128,256]{2,1,0:T(8,128)(2,1)}, u32[]{:S(2)}, u32[]{:S(2)}) %collective-permute-start.11) | collective-permute-done | bytes 2097184 | tf_op jit(solution)/shard_map/ppermute | solution.py:129
  676.9 13.7 %fusion.13 = (f32[32,128,256]{2,1,0:T(8,128)}, f32[32,128,256]{2,1,0:T(8,128)}) fusion(bf16[32,128,256]{2,1,0:T(8,128)(2,1)} %collective-permute-done.25, bf16[32,128,256]{2,1,0:T(8,128)(2,1)} %collective-permute-done.24, f32[4,32,128,256]{3,2,1,0:T(8,128)} %bitcast.128, s32[]{:T(128)S(6)} %select_n.149, bf16[4,32,128,256]{3,2,1,0:T(8,128)(2,1)} %bitcast.62, ...), kind=kLoop, calls=%fused_computation.18 | loop fusion | flops 12582912 | bytes 29360132 | tf_op jit(solution)/shard_map/add | solution.py:135
  (80 shorter events, 83.0 us)
Async XLA Ops:
  20.1 28.0 %collective-permute-start.2 = (bf16[15,128,256]{2,1,0:T(8,128)(2,1)}, bf16[15,128,256]{2,1,0:T(8,128)(2,1)}, u32[]{:S(2)}, u32[]{:S(2)}) collective-permute-start(bf16[15,128,256]{2,1,0:T(8,128)(2,1)} %get-tuple-element.32), channel_id=1, source_target_pairs={{0,24},{8,16},{16,8},{24,0},{1,25},{9,17},{17,9},{25,1},{2,26},{10... | collective-permute-start | bytes 2949128 | tf_op jit(solution)/shard_map/ppermute | solution.py:40
  24.0 44.1 %collective-permute-start.1 = (bf16[15,128,256]{2,1,0:T(8,128)(2,1)}, bf16[15,128,256]{2,1,0:T(8,128)(2,1)}, u32[]{:S(2)}, u32[]{:S(2)}) collective-permute-start(bf16[15,128,256]{2,1,0:T(8,128)(2,1)} %get-tuple-element.33), channel_id=1, source_target_pairs={{0,16},{8,24},{16,0},{24,8},{1,17},{9,25},{17,1},{25,9},{2,18},{10... | collective-permute-start | bytes 2949128 | tf_op jit(solution)/shard_map/ppermute | solution.py:40
  24.5 44.1 %collective-permute-start = (bf16[15,128,256]{2,1,0:T(8,128)(2,1)}, bf16[15,128,256]{2,1,0:T(8,128)(2,1)}, u32[]{:S(2)}, u32[]{:S(2)}) collective-permute-start(bf16[15,128,256]{2,1,0:T(8,128)(2,1)} %get-tuple-element.34), channel_id=1, source_target_pairs={{0,8},{8,0},{16,24},{24,16},{1,9},{9,1},{17,25},{25,17},{2,10},{10... | collective-permute-start | bytes 2949128 | tf_op jit(solution)/shard_map/ppermute | solution.py:40
  44.7 44.5 %collective-permute-start.15 = (bf16[15,128,256]{2,1,0:T(8,128)(2,1)}, bf16[15,128,256]{2,1,0:T(8,128)(2,1)}, u32[]{:S(2)}, u32[]{:S(2)}) collective-permute-start(bf16[15,128,256]{2,1,0:T(8,128)(2,1)} %get-tuple-element.48), channel_id=1, source_target_pairs={{0,24},{8,16},{16,8},{24,0},{1,25},{9,17},{17,9},{25,1},{2,26},{10... | collective-permute-start | bytes 2949128 | tf_op jit(solution)/shard_map/ppermute | solution.py:40
  47.6 61.7 %collective-permute-start.14 = (bf16[15,128,256]{2,1,0:T(8,128)(2,1)}, bf16[15,128,256]{2,1,0:T(8,128)(2,1)}, u32[]{:S(2)}, u32[]{:S(2)}) collective-permute-start(bf16[15,128,256]{2,1,0:T(8,128)(2,1)} %get-tuple-element.49), channel_id=1, source_target_pairs={{0,16},{8,24},{16,0},{24,8},{1,17},{9,25},{17,1},{25,9},{2,18},{10... | collective-permute-start | bytes 2949128 | tf_op jit(solution)/shard_map/ppermute | solution.py:40
  48.1 61.4 %collective-permute-start.13 = (bf16[15,128,256]{2,1,0:T(8,128)(2,1)S(1)}, bf16[15,128,256]{2,1,0:T(8,128)(2,1)S(1)}, u32[]{:S(2)}, u32[]{:S(2)}) collective-permute-start(bf16[15,128,256]{2,1,0:T(8,128)(2,1)S(1)} %get-tuple-element.50), channel_id=1, source_target_pairs={{0,8},{8,0},{16,24},{24,16},{1,9},{9,1},{17,25},{25,17},{2,10},{10... | collective-permute-start | bytes 2949128 | tf_op jit(solution)/shard_map/ppermute | solution.py:40
  71.1 45.5 %collective-permute-start.5 = (bf16[15,128,256]{2,1,0:T(8,128)(2,1)S(1)}, bf16[15,128,256]{2,1,0:T(8,128)(2,1)S(1)}, u32[]{:S(2)}, u32[]{:S(2)}) collective-permute-start(bf16[15,128,256]{2,1,0:T(8,128)(2,1)S(1)} %get-tuple-element.28), channel_id=1, source_target_pairs={{0,6},{2,4},{4,2},{6,0},{1,7},{3,5},{5,3},{7,1},{8,14},{10,12},{12... | collective-permute-start | bytes 2949128 | tf_op jit(solution)/shard_map/ppermute | solution.py:40
  74.8 127.1 %collective-permute-start.4 = (bf16[15,128,256]{2,1,0:T(8,128)(2,1)S(1)}, bf16[15,128,256]{2,1,0:T(8,128)(2,1)S(1)}, u32[]{:S(2)}, u32[]{:S(2)}) collective-permute-start(bf16[15,128,256]{2,1,0:T(8,128)(2,1)S(1)} %get-tuple-element.29), channel_id=1, source_target_pairs={{0,4},{2,6},{4,0},{6,2},{1,5},{3,7},{5,1},{7,3},{8,12},{10,14},{12... | collective-permute-start | bytes 2949128 | tf_op jit(solution)/shard_map/ppermute | solution.py:40
  89.1 112.8 %collective-permute-start.3 = (bf16[15,128,256]{2,1,0:T(8,128)(2,1)S(1)}, bf16[15,128,256]{2,1,0:T(8,128)(2,1)S(1)}, u32[]{:S(2)}, u32[]{:S(2)}) collective-permute-start(bf16[15,128,256]{2,1,0:T(8,128)(2,1)S(1)} %get-tuple-element.30), channel_id=1, source_target_pairs={{0,2},{2,0},{4,6},{6,4},{1,3},{3,1},{5,7},{7,5},{8,10},{10,8},{12,... | collective-permute-start | bytes 2949128 | tf_op jit(solution)/shard_map/ppermute | solution.py:40
  113.0 94.3 %collective-permute-start.18 = (bf16[15,128,256]{2,1,0:T(8,128)(2,1)}, bf16[15,128,256]{2,1,0:T(8,128)(2,1)}, u32[]{:S(2)}, u32[]{:S(2)}) collective-permute-start(bf16[15,128,256]{2,1,0:T(8,128)(2,1)} %get-tuple-element.44), channel_id=1, source_target_pairs={{0,6},{2,4},{4,2},{6,0},{1,7},{3,5},{5,3},{7,1},{8,14},{10,12},{12... | collective-permute-start | bytes 2949128 | tf_op jit(solution)/shard_map/ppermute | solution.py:40
  116.6 126.6 %collective-permute-start.17 = (bf16[15,128,256]{2,1,0:T(8,128)(2,1)}, bf16[15,128,256]{2,1,0:T(8,128)(2,1)}, u32[]{:S(2)}, u32[]{:S(2)}) collective-permute-start(bf16[15,128,256]{2,1,0:T(8,128)(2,1)} %get-tuple-element.45), channel_id=1, source_target_pairs={{0,4},{2,6},{4,0},{6,2},{1,5},{3,7},{5,1},{7,3},{8,12},{10,14},{12... | collective-permute-start | bytes 2949128 | tf_op jit(solution)/shard_map/ppermute | solution.py:40
  116.6 126.6 %collective-permute-start.16 = (bf16[15,128,256]{2,1,0:T(8,128)(2,1)}, bf16[15,128,256]{2,1,0:T(8,128)(2,1)}, u32[]{:S(2)}, u32[]{:S(2)}) collective-permute-start(bf16[15,128,256]{2,1,0:T(8,128)(2,1)} %get-tuple-element.46), channel_id=1, source_target_pairs={{0,2},{2,0},{4,6},{6,4},{1,3},{3,1},{5,7},{7,5},{8,10},{10,8},{12,... | collective-permute-start | bytes 2949128 | tf_op jit(solution)/shard_map/ppermute | solution.py:40
  204.2 44.6 %collective-permute-start.8 = (bf16[15,128,256]{2,1,0:T(8,128)(2,1)}, bf16[15,128,256]{2,1,0:T(8,128)(2,1)}, u32[]{:S(2)}, u32[]{:S(2)}) collective-permute-start(bf16[15,128,256]{2,1,0:T(8,128)(2,1)} %get-tuple-element.24), channel_id=1, source_target_pairs={{0,24},{8,16},{16,8},{24,0},{1,25},{9,17},{17,9},{25,1},{2,26},{10... | collective-permute-start | bytes 2949128 | tf_op jit(solution)/shard_map/ppermute | solution.py:40
  204.9 45.4 %collective-permute-start.7 = (bf16[15,128,256]{2,1,0:T(8,128)(2,1)}, bf16[15,128,256]{2,1,0:T(8,128)(2,1)}, u32[]{:S(2)}, u32[]{:S(2)}) collective-permute-start(bf16[15,128,256]{2,1,0:T(8,128)(2,1)} %get-tuple-element.25), channel_id=1, source_target_pairs={{0,16},{8,24},{16,0},{24,8},{1,17},{9,25},{17,1},{25,9},{2,18},{10... | collective-permute-start | bytes 2949128 | tf_op jit(solution)/shard_map/ppermute | solution.py:40
  207.3 42.9 %collective-permute-start.6 = (bf16[15,128,256]{2,1,0:T(8,128)(2,1)S(1)}, bf16[15,128,256]{2,1,0:T(8,128)(2,1)}, u32[]{:S(2)}, u32[]{:S(2)}) collective-permute-start(bf16[15,128,256]{2,1,0:T(8,128)(2,1)S(1)} %get-tuple-element.26), channel_id=1, source_target_pairs={{0,8},{8,0},{16,24},{24,16},{1,9},{9,1},{17,25},{25,17},{2,10},{10... | collective-permute-start | bytes 2949128 | tf_op jit(solution)/shard_map/ppermute | solution.py:40
  245.8 44.7 %collective-permute-start.20 = (bf16[15,128,256]{2,1,0:T(8,128)(2,1)S(1)}, bf16[15,128,256]{2,1,0:T(8,128)(2,1)S(1)}, u32[]{:S(2)}, u32[]{:S(2)}) collective-permute-start(bf16[15,128,256]{2,1,0:T(8,128)(2,1)S(1)} %get-tuple-element.41), channel_id=1, source_target_pairs={{0,16},{8,24},{16,0},{24,8},{1,17},{9,25},{17,1},{25,9},{2,18},{10... | collective-permute-start | bytes 2949128 | tf_op jit(solution)/shard_map/ppermute | solution.py:40
  248.7 41.9 %collective-permute-start.19 = (bf16[15,128,256]{2,1,0:T(8,128)(2,1)S(1)}, bf16[15,128,256]{2,1,0:T(8,128)(2,1)S(1)}, u32[]{:S(2)}, u32[]{:S(2)}) collective-permute-start(bf16[15,128,256]{2,1,0:T(8,128)(2,1)S(1)} %get-tuple-element.42), channel_id=1, source_target_pairs={{0,8},{8,0},{16,24},{24,16},{1,9},{9,1},{17,25},{25,17},{2,10},{10... | collective-permute-start | bytes 2949128 | tf_op jit(solution)/shard_map/ppermute | solution.py:40
  343.5 51.4 %collective-permute-start.22 = (bf16[128,128,256]{2,1,0:T(8,128)(2,1)}, bf16[128,128,256]{2,1,0:T(8,128)(2,1)}, u32[]{:S(2)}, u32[]{:S(2)}) collective-permute-start(bf16[128,128,256]{2,1,0:T(8,128)(2,1)} %get-tuple-element.12), channel_id=1, source_target_pairs={{0,1},{1,0},{2,3},{3,2},{4,5},{5,4},{6,7},{7,6},{8,9},{9,8},{10,11... | collective-permute-start | bytes 25165832 | tf_op jit(solution)/shard_map/ppermute | solution.py:183
  402.5 50.8 %collective-permute-start.23 = (bf16[32,128,256]{2,1,0:T(8,128)(2,1)}, bf16[32,128,256]{2,1,0:T(8,128)(2,1)}, u32[]{:S(2)}, u32[]{:S(2)}) collective-permute-start(bf16[32,128,256]{2,1,0:T(8,128)(2,1)} %get-tuple-element.17), channel_id=1, source_target_pairs={{0,2},{2,4},{4,6},{6,0},{1,3},{3,5},{5,7},{7,1},{8,10},{10,12},{12... | collective-permute-start | bytes 6291464 | tf_op jit(solution)/shard_map/ppermute | solution.py:129
  414.2 83.9 %collective-permute-start.10 = (bf16[32,128,256]{2,1,0:T(8,128)(2,1)}, bf16[32,128,256]{2,1,0:T(8,128)(2,1)}, u32[]{:S(2)}, u32[]{:S(2)}) collective-permute-start(bf16[32,128,256]{2,1,0:T(8,128)(2,1)} %get-tuple-element.15), channel_id=1, source_target_pairs={{0,2},{2,4},{4,6},{6,0},{1,3},{3,5},{5,7},{7,1},{8,10},{10,12},{12... | collective-permute-start | bytes 6291464 | tf_op jit(solution)/shard_map/ppermute | solution.py:129
  414.2 127.9 %collective-permute-start.25 = (bf16[32,128,256]{2,1,0:T(8,128)(2,1)S(1)}, bf16[32,128,256]{2,1,0:T(8,128)(2,1)}, u32[]{:S(2)}, u32[]{:S(2)}) collective-permute-start(bf16[32,128,256]{2,1,0:T(8,128)(2,1)S(1)} %get-tuple-element.18), channel_id=1, source_target_pairs={{0,6},{2,0},{4,2},{6,4},{1,7},{3,1},{5,3},{7,5},{8,14},{10,8},{12,... | collective-permute-start | bytes 6291464 | tf_op jit(solution)/shard_map/ppermute | solution.py:129
  418.0 169.8 %collective-permute-start.12 = (bf16[32,128,256]{2,1,0:T(8,128)(2,1)}, bf16[32,128,256]{2,1,0:T(8,128)(2,1)}, u32[]{:S(2)}, u32[]{:S(2)}) collective-permute-start(bf16[32,128,256]{2,1,0:T(8,128)(2,1)} %get-tuple-element.16), channel_id=1, source_target_pairs={{0,6},{2,0},{4,2},{6,4},{1,7},{3,1},{5,3},{7,5},{8,14},{10,8},{12,... | collective-permute-start | bytes 6291464 | tf_op jit(solution)/shard_map/ppermute | solution.py:129
  459.0 173.9 %collective-permute-start.24 = (bf16[32,128,256]{2,1,0:T(8,128)(2,1)}, bf16[32,128,256]{2,1,0:T(8,128)(2,1)}, u32[]{:S(2)}, u32[]{:S(2)}) collective-permute-start(bf16[32,128,256]{2,1,0:T(8,128)(2,1)} %fusion.12), channel_id=1, source_target_pairs={{0,2},{2,4},{4,6},{6,0},{1,3},{3,5},{5,7},{7,1},{8,10},{10,12},{12... | collective-permute-start | bytes 6291464 | tf_op jit(solution)/shard_map/ppermute | solution.py:129
  503.9 173.1 %collective-permute-start.11 = (bf16[32,128,256]{2,1,0:T(8,128)(2,1)}, bf16[32,128,256]{2,1,0:T(8,128)(2,1)}, u32[]{:S(2)}, u32[]{:S(2)}) collective-permute-start(bf16[32,128,256]{2,1,0:T(8,128)(2,1)} %fusion.14), channel_id=1, source_target_pairs={{0,2},{2,4},{4,6},{6,0},{1,3},{3,5},{5,7},{7,1},{8,10},{10,12},{12... | collective-permute-start | bytes 6291464 | tf_op jit(solution)/shard_map/ppermute | solution.py:129
  (9 other events, 98.6 us)

commit v3 on v2

--- a/solution.py
+++ b/solution.py
@@ -25,26 +25,34 @@
     return [(d, d ^ step) for d in range(side)]
 
 
-def mirror(tile, side):
+def leg(get, side, axis):
+    held = [get(0)]
+    for step in range(1, side):
+        held.append(lax.ppermute(get(step), axis, partners(side, step)))
+    return held
+
+
+def first_leg(tile, side):
     pairs, rows, columns = tile.shape
     me_a = lax.axis_index("va")
-    me_b = lax.axis_index("vb")
     strips = tile.reshape(pairs, side, rows // side, columns)
-
-    def strip(index):
-        return lax.dynamic_index_in_dim(strips, index, 1, False)
-
-    def leg(get, axis):
-        held = [get(0)]
-        for step in range(1, side):
-            held.append(lax.ppermute(get(step), axis, partners(side, step)))
-        return jnp.stack(held)
-
-    plane = leg(lambda step: strip(me_a ^ step), "va")
-    column = leg(lambda step: pick(plane, me_a ^ me_b ^ step), "vb")
-    back = leg(lambda step: pick(column, me_a ^ me_b ^ step), "va")
-    ordered = [pick(back, me_a ^ c) for c in range(side)]
-    return jnp.stack(ordered, axis=1).reshape(pairs, rows, columns)
+    return leg(
+        lambda step: lax.dynamic_index_in_dim(strips, me_a ^ step, 1, False), side, "va"
+    )
+
+
+def next_leg(held, axis):
+    apart = lax.axis_index("va") ^ lax.axis_index("vb")
+    stack = jnp.stack(held)
+    return leg(lambda step: pick(stack, apart ^ step), len(held), axis)
+
+
+def assemble(held):
+    pairs, strip, columns = held[0].shape
+    me_a = lax.axis_index("va")
+    stack = jnp.stack(held)
+    ordered = [pick(stack, me_a ^ c) for c in range(len(held))]
+    return jnp.stack(ordered, axis=1).reshape(pairs, len(held) * strip, columns)
 
 
 def contract_kernel(dom_blocks, cells, right, amplitude, keep, send, total, staged, keep_sem, send_sem):
@@ -116,24 +124,33 @@
     )(cells, right, amplitude)
 
 
-def reduce_owned(total_of, count):
+def ring(count, sign):
+    return [(d, (d + sign) % count) for d in range(count)]
+
+
+def ways(count):
+    return [(sign, hops) for sign, hops in ((1, count // 2), (-1, (count - 1) // 2)) if hops]
+
+
+def first_sums(total_of, count):
     me = lax.axis_index("vb")
-    result = total_of(me)
-    arrivals = []
-    for sign, hops in ((1, count // 2), (-1, (count - 1) // 2)):
-        if hops == 0:
-            continue
-        ring = [(d, (d + sign) % count) for d in range(count)]
-        running = total_of((me + sign * hops) % count).astype(jnp.bfloat16)
-        for hop in range(1, hops + 1):
-            running = lax.ppermute(running, "vb", ring)
-            if hop < hops:
-                mine = total_of((me + sign * (hops - hop)) % count)
-                running = (mine + running.astype(jnp.float32)).astype(jnp.bfloat16)
-        arrivals.append(running)
-    for arrival in arrivals:
-        result = result + arrival.astype(jnp.float32)
-    return result
+    return [total_of((me + sign * hops) % count).astype(jnp.bfloat16) for sign, hops in ways(count)]
+
+
+def first_hops(sums, count):
+    return [lax.ppermute(x, "vb", ring(count, sign)) for x, (sign, _) in zip(sums, ways(count))]
+
+
+def last_hops(total_of, arrivals, count):
+    me = lax.axis_index("vb")
+    arrived = []
+    for running, (sign, hops) in zip(arrivals, ways(count)):
+        for hop in range(1, hops):
+            mine = total_of((me + sign * (hops - hop)) % count)
+            running = (mine + running.astype(jnp.float32)).astype(jnp.bfloat16)
+            running = lax.ppermute(running, "vb", ring(count, sign))
+        arrived.append(running)
+    return arrived
 
 
 def shards(left_fit, right_fit, occ_energy, virt_energy, pair_list, domain_blocks):
@@ -158,15 +175,30 @@
         columns = right_fit[:, part * width : (part + 1) * width]
         tile = jnp.einsum("pak,pbk->pab", left_fit, columns, preferred_element_type=jnp.float32)
         tiles.append(tile.astype(jnp.bfloat16))
-    mirrored = [mirror(tile, side) for tile in tiles]
+    turned = []
+    for part in range(parts):
+        rows = left_fit[:, part * width : (part + 1) * width]
+        tile = jnp.einsum("pbk,pak->pba", right_fit, rows, preferred_element_type=jnp.float32)
+        turned.append(tile.astype(jnp.bfloat16))
+
+    plane, column = [], []
+    for part in range(parts):
+        tile = tiles[part]
+        if part:
+            tile, plane[-1], turned[0] = lax.optimization_barrier((tile, plane[-1], turned[0]))
+        plane.append(first_leg(tile, side))
+    for part in range(parts):
+        if part:
+            plane[part], column[-1], turned[part] = lax.optimization_barrier(
+                (plane[part], column[-1], turned[part])
+            )
+        column.append(next_leg(plane[part], "vb"))
 
     def amplitude_of(part):
+        mirrored = assemble(next_leg(column[part], "va"))
         rows = slice(part * width, (part + 1) * width)
-        turned = jnp.einsum(
-            "pbk,pak->pba", right_fit, left_fit[:, rows], preferred_element_type=jnp.float32
-        ).astype(jnp.bfloat16)
         energy_gap = energy_a[None, None, rows] + energy_b[None, :, None] - pair_energy
-        wide = 2.0 * turned.astype(jnp.float32) - mirrored[part].astype(jnp.float32)
+        wide = 2.0 * turned[part].astype(jnp.float32) - mirrored.astype(jnp.float32)
         return (wide / energy_gap).astype(jnp.bfloat16)
 
     slab = AUX_BLK // (vb_count * pair_count)
@@ -177,18 +209,32 @@
 
     send_type = jnp.bfloat16 if vb_count <= 4 else jnp.float32
     swap = [(c, (c + 1) % pair_count) for c in range(pair_count)]
+    shape = (vb_count, slab * NOCC, BLOCK, width)
+    totals, hops = [], []
+    for part in range(parts):
+        keep, send = contract(cells, right_fit, amplitude_of(part), send_type)
+        if part:
+            send, hops[-1] = lax.optimization_barrier((send, hops[-1]))
+        got = lax.ppermute(send, "pair", swap)
+        keep, got = keep.reshape(shape), got.reshape(shape)
+
+        def total_of(owner, keep=keep, got=got):
+            return pick(keep, owner) + pick(got, owner).astype(jnp.float32)
+
+        totals.append(total_of)
+        sums = first_sums(total_of, vb_count)
+        if part + 1 < parts:
+            sums, column[part + 1] = lax.optimization_barrier((sums, column[part + 1]))
+        hops.append(first_hops(sums, vb_count))
     pieces = []
     for part in range(parts):
-        keep, send = contract(cells, right_fit, amplitude_of(part), send_type)
-        got = lax.ppermute(send, "pair", swap)
-        shape = (vb_count, slab * NOCC, BLOCK, width)
-        keep, got = keep.reshape(shape), got.reshape(shape)
-
-        def total_of(owner, keep=keep, got=got):
-            mine = lax.dynamic_index_in_dim(keep, owner, 0, False)
-            return mine + lax.dynamic_index_in_dim(got, owner, 0, False).astype(jnp.float32)
-
-        mine = reduce_owned(total_of, vb_count).reshape(slab, NOCC, BLOCK, width)
+        arrived = last_hops(totals[part], hops[part], vb_count)
+        if part:
+            arrived, pieces[-1] = lax.optimization_barrier((arrived, pieces[-1]))
+        mine = totals[part](vb_index)
+        for arrival in arrived:
+            mine = mine + arrival.astype(jnp.float32)
+        mine = mine.reshape(slab, NOCC, BLOCK, width)
         pieces.append(mine.transpose(0, 2, 1, 3).reshape(slab * BLOCK, NOCC, width))
     return jnp.concatenate(pieces, axis=2)
 

time: 703 us -> 660 us (0.939)
  waiting for transfers between devices: 438 us -> 417 us
  starting transfers between devices: 53.9 us -> 33.8 us
  matrix products: 73.4 us -> 65.4 us
    ppermute x6, waiting for transfers between devices: 247 us -> 174 us  [the longest x4 91 us: first_hops(): lax.ppermute(x, 'vb', ring(count, sign))]
    ppermute x18, waiting for transfers between devices: 185 us -> 224 us  [leg(): held.append(lax.ppermute(get(step), axis, partners(side, step)))]
    ppermute x18, starting transfers between devices: 49 us -> 24.8 us  [leg(): held.append(lax.ppermute(get(step), axis, partners(side, step)))]
    ppermute x2, waiting for transfers between devices: 5.55 us -> 19 us  [shards(): got = lax.ppermute(send, 'pair', swap)]
    squeeze x0 -> x4, local copies, waits for them, and re-layouts: none -> 11 us  [the longest x2 7.57 us: first_leg(): lax.dynamic_index_in_dim(strips, me_a ^ step, 1, False)]
    convert_element_type x4 -> x6, other arithmetic: 25.3 us -> 34.5 us  [the longest x2 15.8 us: first_sums(): total_of((me + sign * hops) % count).astype(jnp.bfloat16)]
    another operation x4 -> x2, local copies, waits for them, and re-layouts: 9.31 us -> 0.53 us  [assemble(): return jnp.stack(ordered, axis=1).reshape(pairs, len(held) * strip, columns)]
    dot_general x2, matrix products: 40.8 us -> 32.7 us  [shards(): jnp.einsum('pbk,pak->pba', right_fit, rows, preferred_element_type=jnp.fl...]
  transfers between devices with their start and end apart: 26 -> 26, of which waited for: 17 -> 19; matrix products, arithmetic and copies ran while one was open for 12% -> 13% of each run, Pallas kernels for 4% -> 4%
where the time goes in v3:
time: 660 us; the launch traced here: 659 us
  waiting for transfers between devices  417 us (63%)
  matrix products  65.4 us (10%)
  other arithmetic  61.8 us (9%)
  Pallas kernels  58 us (9%)
  starting transfers between devices  33.8 us (5%)
  local copies, waits for them, and re-layouts  22.5 us (3%)
    ppermute x18, waiting for transfers between devices, leg(): held.append(lax.ppermute(get(step), axis, partners(side, step)))  224 us
    ppermute x4, waiting for transfers between devices, first_hops(): lax.ppermute(x, 'vb', ring(count, sign))  91 us
    ppermute x2, waiting for transfers between devices, last_hops(): running = lax.ppermute(running, 'vb', ring(count, sign))  83.2 us
    pallas_call x2, Pallas kernels, contract(): pl.pallas_call(functools.partial(contract_kernel, dom // BLOCK), out_shap...  58 us
    dot_general x2, matrix products, shards(): jnp.einsum('pbk,pak->pba', right_fit, rows, preferred_element_type=jnp.fl...  32.7 us
    dot_general x2, matrix products, shards(): jnp.einsum('pak,pbk->pab', left_fit, columns, preferred_element_type=jnp....  32.7 us
    ppermute x18, starting transfers between devices, leg(): held.append(lax.ppermute(get(step), axis, partners(side, step)))  24.8 us
    ppermute x2, waiting for transfers between devices, shards(): got = lax.ppermute(send, 'pair', swap)  19 us
  transfers between devices with their start and end apart: 26, of which 19 were waited for; matrix products, arithmetic and copies ran while one was open for 13% of the time, Pallas kernels for 4%

profile of v3, /device:TPU:0, one launch (start us, length us, event | category | flops | bytes accessed | tf_op | source)
XLA Modules:
  0.0 659.1 jit_solution(14607332583177990800)
XLA Ops:
  0.0 16.3 %fusion.19 = bf16[15,512,256]{2,1,0:T(8,128)(2,1)} fusion(bf16[15,512,1536]{2,1,0:T(8,128)(2,1)} %param.6, bf16[15,512,1536]{2,1,0:T(8,128)(2,1)} %right.3), kind=kOutput, calls=%fused_computation.36 | convolution fusion | flops 6041763840 | bytes 39321600 | tf_op jit(solution)/shard_map/pak,pbk->pab/dot_general | solution.py:176
  24.6 16.3 %fusion.16 = bf16[15,512,256]{2,1,0:T(8,128)(2,1)} fusion(bf16[15,512,1536]{2,1,0:T(8,128)(2,1)} %param.6, bf16[15,512,1536]{2,1,0:T(8,128)(2,1)} %right.3), kind=kOutput, calls=%fused_computation.35 | convolution fusion | flops 6041763840 | bytes 39321600 | tf_op jit(solution)/shard_map/pak,pbk->pab/dot_general | solution.py:176
  40.9 16.4 %fusion.22 = bf16[15,512,256]{2,1,0:T(8,128)(2,1)} fusion(bf16[15,512,1536]{2,1,0:T(8,128)(2,1)} %right.3, bf16[15,512,1536]{2,1,0:T(8,128)(2,1)} %param.6), kind=kOutput, calls=%fused_computation.37 | convolution fusion | flops 6041763840 | bytes 39321600 | tf_op jit(solution)/shard_map/pbk,pak->pba/dot_general | solution.py:181
  57.3 9.8 %collective-permute-done.1 = bf16[15,128,256]{2,1,0:T(8,128)(2,1)S(1)} collective-permute-done((bf16[15,128,256]{2,1,0:T(8,128)(2,1)}, bf16[15,128,256]{2,1,0:T(8,128)(2,1)S(1)}, u32[]{:S(2)}, u32[]{:S(2)}) %collective-permute-start.1) | collective-permute-done | bytes 983072 | tf_op jit(solution)/shard_map/ppermute | solution.py:31
  82.3 14.8 %collective-permute-done.5 = bf16[15,128,256]{2,1,0:T(8,128)(2,1)S(1)} collective-permute-done((bf16[15,128,256]{2,1,0:T(8,128)(2,1)}, bf16[15,128,256]{2,1,0:T(8,128)(2,1)S(1)}, u32[]{:S(2)}, u32[]{:S(2)}) %collective-permute-start.5) | collective-permute-done | bytes 983072 | tf_op jit(solution)/shard_map/ppermute | solution.py:31
  98.7 16.3 %fusion.25 = bf16[15,512,256]{2,1,0:T(8,128)(2,1)} fusion(bf16[15,512,1536]{2,1,0:T(8,128)(2,1)} %right.3, bf16[15,512,1536]{2,1,0:T(8,128)(2,1)} %param.6), kind=kOutput, calls=%fused_computation.38 | convolution fusion | flops 6041763840 | bytes 39321600 | tf_op jit(solution)/shard_map/pbk,pak->pba/dot_general | solution.py:181
  117.5 48.7 %collective-permute-done.7 = bf16[15,128,256]{2,1,0:T(8,128)(2,1)} collective-permute-done((bf16[15,128,256]{2,1,0:T(8,128)(2,1)}, bf16[15,128,256]{2,1,0:T(8,128)(2,1)}, u32[]{:S(2)}, u32[]{:S(2)}) %collective-permute-start.7) | collective-permute-done | bytes 983072 | tf_op jit(solution)/shard_map/ppermute | solution.py:31
  174.6 21.3 %collective-permute-done.11 = bf16[15,128,256]{2,1,0:T(8,128)(2,1)} collective-permute-done((bf16[15,128,256]{2,1,0:T(8,128)(2,1)}, bf16[15,128,256]{2,1,0:T(8,128)(2,1)}, u32[]{:S(2)}, u32[]{:S(2)}) %collective-permute-start.11) | collective-permute-done | bytes 983072 | tf_op jit(solution)/shard_map/ppermute | solution.py:31
  195.9 19.2 %collective-permute-done.10 = bf16[15,128,256]{2,1,0:T(8,128)(2,1)} collective-permute-done((bf16[15,128,256]{2,1,0:T(8,128)(2,1)}, bf16[15,128,256]{2,1,0:T(8,128)(2,1)}, u32[]{:S(2)}, u32[]{:S(2)}) %collective-permute-start.10) | collective-permute-done | bytes 983072 | tf_op jit(solution)/shard_map/ppermute | solution.py:31
  223.3 29.0 %contract.2 = (f32[128,128,256]{2,1,0:T(8,128)}, bf16[128,128,256]{2,1,0:T(8,128)(2,1)}) custom-call(s32[180]{0:T(256)} %reshape.133.cells, bf16[15,512,1536]{2,1,0:T(8,128)(2,1)} %right.3, bf16[15,512,256]{2,1,0:T(8,128)(2,1)} %fusion.11.amplitude), custom_call_target="tpu_custom_call" | custom-call | flops 6039797760 | bytes 52690944 | tf_op jit(solution)/shard_map/contract/pallas_call | solution.py:96
  265.8 6.2 fusion.29
  272.1 10.4 %collective-permute-done.15 = bf16[15,128,256]{2,1,0:T(8,128)(2,1)S(1)} collective-permute-done((bf16[15,128,256]{2,1,0:T(8,128)(2,1)}, bf16[15,128,256]{2,1,0:T(8,128)(2,1)S(1)}, u32[]{:S(2)}, u32[]{:S(2)}) %collective-permute-start.15) | collective-permute-done | bytes 983072 | tf_op jit(solution)/shard_map/ppermute | solution.py:31
  282.5 59.3 %collective-permute-done.14 = bf16[15,128,256]{2,1,0:T(8,128)(2,1)} collective-permute-done((bf16[15,128,256]{2,1,0:T(8,128)(2,1)}, bf16[15,128,256]{2,1,0:T(8,128)(2,1)}, u32[]{:S(2)}, u32[]{:S(2)}) %collective-permute-start.14) | collective-permute-done | bytes 983072 | tf_op jit(solution)/shard_map/ppermute | solution.py:31
  351.4 18.3 %collective-permute-done.18 = bf16[15,128,256]{2,1,0:T(8,128)(2,1)S(1)} collective-permute-done((bf16[15,128,256]{2,1,0:T(8,128)(2,1)S(1)}, bf16[15,128,256]{2,1,0:T(8,128)(2,1)S(1)}, u32[]{:S(2)}, u32[]{:S(2)}) %collective-permute-start.18) | collective-permute-done | bytes 983072 | tf_op jit(solution)/shard_map/ppermute | solution.py:31
  369.7 19.7 %collective-permute-done.17 = bf16[15,128,256]{2,1,0:T(8,128)(2,1)S(1)} collective-permute-done((bf16[15,128,256]{2,1,0:T(8,128)(2,1)S(1)}, bf16[15,128,256]{2,1,0:T(8,128)(2,1)S(1)}, u32[]{:S(2)}, u32[]{:S(2)}) %collective-permute-start.17) | collective-permute-done | bytes 983072 | tf_op jit(solution)/shard_map/ppermute | solution.py:31
  395.8 29.0 %contract.3 = (f32[128,128,256]{2,1,0:T(8,128)}, bf16[128,128,256]{2,1,0:T(8,128)(2,1)}) custom-call(s32[180]{0:T(256)} %reshape.133.cells, bf16[15,512,1536]{2,1,0:T(8,128)(2,1)} %right.3, bf16[15,512,256]{2,1,0:T(8,128)(2,1)} %fusion.9.amplitude), custom_call_target="tpu_custom_call" | custom-call | flops 6039797760 | bytes 52690944 | tf_op jit(solution)/shard_map/contract/pallas_call | solution.py:96
  424.9 14.0 %collective-permute-done.20 = bf16[32,128,256]{2,1,0:T(8,128)(2,1)S(1)} collective-permute-done((bf16[32,128,256]{2,1,0:T(8,128)(2,1)S(1)}, bf16[32,128,256]{2,1,0:T(8,128)(2,1)S(1)}, u32[]{:S(2)}, u32[]{:S(2)}) %collective-permute-start.20) | collective-permute-done | bytes 2097184 | tf_op jit(solution)/shard_map/ppermute | solution.py:141
  438.9 13.4 %collective-permute-done.21 = bf16[128,128,256]{2,1,0:T(8,128)(2,1)S(1)} collective-permute-done((bf16[128,128,256]{2,1,0:T(8,128)(2,1)}, bf16[128,128,256]{2,1,0:T(8,128)(2,1)S(1)}, u32[]{:S(2)}, u32[]{:S(2)}) %collective-permute-start.21) | collective-permute-done | bytes 8388640 | tf_op jit(solution)/shard_map/ppermute | solution.py:218
  452.3 9.6 %fusion.31 = (bf16[32,128,256]{2,1,0:T(8,128)(2,1)S(1)}, bf16[32,128,256]{2,1,0:T(8,128)(2,1)}) fusion(f32[4,32,128,256]{3,2,1,0:T(8,128)} %bitcast.139, s32[]{:T(128)S(6)} %select_n.152, bf16[4,32,128,256]{3,2,1,0:T(8,128)(2,1)S(1)} %bitcast.144, s32[]{:T(128)S(6)} %select_n.150), kind=kLoop, calls=%fused_computation.42 | loop fusion | flops 6291456 | bytes 16777224 | tf_op jit(solution)/shard_map/convert_element_type | solution.py:137
  463.1 5.8 fusion.13
  472.7 39.9 %collective-permute-done.22 = bf16[32,128,256]{2,1,0:T(8,128)(2,1)} collective-permute-done((bf16[32,128,256]{2,1,0:T(8,128)(2,1)}, bf16[32,128,256]{2,1,0:T(8,128)(2,1)}, u32[]{:S(2)}, u32[]{:S(2)}) %collective-permute-start.22) | collective-permute-done | bytes 2097184 | tf_op jit(solution)/shard_map/ppermute | solution.py:141
  518.4 39.0 %collective-permute-done.25 = bf16[32,128,256]{2,1,0:T(8,128)(2,1)} collective-permute-done((bf16[32,128,256]{2,1,0:T(8,128)(2,1)}, bf16[32,128,256]{2,1,0:T(8,128)(2,1)}, u32[]{:S(2)}, u32[]{:S(2)}) %collective-permute-start.25) | collective-permute-done | bytes 2097184 | tf_op jit(solution)/shard_map/ppermute | solution.py:151
  565.3 37.0 %collective-permute-done.24 = bf16[32,128,256]{2,1,0:T(8,128)(2,1)} collective-permute-done((bf16[32,128,256]{2,1,0:T(8,128)(2,1)S(1)}, bf16[32,128,256]{2,1,0:T(8,128)(2,1)}, u32[]{:S(2)}, u32[]{:S(2)}) %collective-permute-start.24) | collective-permute-done | bytes 2097184 | tf_op jit(solution)/shard_map/ppermute | solution.py:141
  602.3 44.2 %collective-permute-done.23 = bf16[32,128,256]{2,1,0:T(8,128)(2,1)} collective-permute-done((bf16[32,128,256]{2,1,0:T(8,128)(2,1)}, bf16[32,128,256]{2,1,0:T(8,128)(2,1)}, u32[]{:S(2)}, u32[]{:S(2)}) %collective-permute-start.23) | collective-permute-done | bytes 2097184 | tf_op jit(solution)/shard_map/ppermute | solution.py:151
  (89 shorter events, 104.9 us)
Async XLA Ops:
  20.1 37.2 %collective-permute-start.2 = (bf16[15,128,256]{2,1,0:T(8,128)(2,1)}, bf16[15,128,256]{2,1,0:T(8,128)(2,1)S(1)}, u32[]{:S(2)}, u32[]{:S(2)}) collective-permute-start(bf16[15,128,256]{2,1,0:T(8,128)(2,1)} %get-tuple-element.101), channel_id=1, source_target_pairs={{0,24},{8,16},{16,8},{24,0},{1,25},{9,17},{17,9},{25,1},{2,26},{10... | collective-permute-start | bytes 2949128 | tf_op jit(solution)/shard_map/ppermute | solution.py:31
  24.0 43.0 %collective-permute-start.1 = (bf16[15,128,256]{2,1,0:T(8,128)(2,1)}, bf16[15,128,256]{2,1,0:T(8,128)(2,1)S(1)}, u32[]{:S(2)}, u32[]{:S(2)}) collective-permute-start(bf16[15,128,256]{2,1,0:T(8,128)(2,1)} %get-tuple-element.102), channel_id=1, source_target_pairs={{0,16},{8,24},{16,0},{24,8},{1,17},{9,25},{17,1},{25,9},{2,18},{10... | collective-permute-start | bytes 2949128 | tf_op jit(solution)/shard_map/ppermute | solution.py:31
  24.5 42.9 %collective-permute-start = (bf16[15,128,256]{2,1,0:T(8,128)(2,1)}, bf16[15,128,256]{2,1,0:T(8,128)(2,1)}, u32[]{:S(2)}, u32[]{:S(2)}) collective-permute-start(bf16[15,128,256]{2,1,0:T(8,128)(2,1)} %get-tuple-element.103), channel_id=1, source_target_pairs={{0,8},{8,0},{16,24},{24,16},{1,9},{9,1},{17,25},{25,17},{2,10},{10... | collective-permute-start | bytes 2949128 | tf_op jit(solution)/shard_map/ppermute | solution.py:31
  71.3 25.8 %collective-permute-start.5 = (bf16[15,128,256]{2,1,0:T(8,128)(2,1)}, bf16[15,128,256]{2,1,0:T(8,128)(2,1)S(1)}, u32[]{:S(2)}, u32[]{:S(2)}) collective-permute-start(bf16[15,128,256]{2,1,0:T(8,128)(2,1)} %get-tuple-element.97), channel_id=1, source_target_pairs={{0,24},{8,16},{16,8},{24,0},{1,25},{9,17},{17,9},{25,1},{2,26},{10... | collective-permute-start | bytes 2949128 | tf_op jit(solution)/shard_map/ppermute | solution.py:31
  73.0 44.3 %collective-permute-start.4 = (bf16[15,128,256]{2,1,0:T(8,128)(2,1)}, bf16[15,128,256]{2,1,0:T(8,128)(2,1)}, u32[]{:S(2)}, u32[]{:S(2)}) collective-permute-start(bf16[15,128,256]{2,1,0:T(8,128)(2,1)} %get-tuple-element.98), channel_id=1, source_target_pairs={{0,16},{8,24},{16,0},{24,8},{1,17},{9,25},{17,1},{25,9},{2,18},{10... | collective-permute-start | bytes 2949128 | tf_op jit(solution)/shard_map/ppermute | solution.py:31
  74.4 43.1 %collective-permute-start.3 = (bf16[15,128,256]{2,1,0:T(8,128)(2,1)}, bf16[15,128,256]{2,1,0:T(8,128)(2,1)}, u32[]{:S(2)}, u32[]{:S(2)}) collective-permute-start(bf16[15,128,256]{2,1,0:T(8,128)(2,1)} %get-tuple-element.99), channel_id=1, source_target_pairs={{0,8},{8,0},{16,24},{24,16},{1,9},{9,1},{17,25},{25,17},{2,10},{10... | collective-permute-start | bytes 2949128 | tf_op jit(solution)/shard_map/ppermute | solution.py:31
  78.5 38.9 %collective-permute-start.8 = (bf16[15,128,256]{2,1,0:T(8,128)(2,1)}, bf16[15,128,256]{2,1,0:T(8,128)(2,1)}, u32[]{:S(2)}, u32[]{:S(2)}) collective-permute-start(bf16[15,128,256]{2,1,0:T(8,128)(2,1)} %get-tuple-element.93), channel_id=1, source_target_pairs={{0,6},{2,4},{4,2},{6,0},{1,7},{3,5},{5,3},{7,1},{8,14},{10,12},{12... | collective-permute-start | bytes 2949128 | tf_op jit(solution)/shard_map/ppermute | solution.py:31
  82.3 83.9 %collective-permute-start.7 = (bf16[15,128,256]{2,1,0:T(8,128)(2,1)}, bf16[15,128,256]{2,1,0:T(8,128)(2,1)}, u32[]{:S(2)}, u32[]{:S(2)}) collective-permute-start(bf16[15,128,256]{2,1,0:T(8,128)(2,1)} %get-tuple-element.94), channel_id=1, source_target_pairs={{0,4},{2,6},{4,0},{6,2},{1,5},{3,7},{5,1},{7,3},{8,12},{10,14},{12... | collective-permute-start | bytes 2949128 | tf_op jit(solution)/shard_map/ppermute | solution.py:31
  97.0 69.2 %collective-permute-start.6 = (bf16[15,128,256]{2,1,0:T(8,128)(2,1)}, bf16[15,128,256]{2,1,0:T(8,128)(2,1)}, u32[]{:S(2)}, u32[]{:S(2)}) collective-permute-start(bf16[15,128,256]{2,1,0:T(8,128)(2,1)} %get-tuple-element.95), channel_id=1, source_target_pairs={{0,2},{2,0},{4,6},{6,4},{1,3},{3,1},{5,7},{7,5},{8,10},{10,8},{12,... | collective-permute-start | bytes 2949128 | tf_op jit(solution)/shard_map/ppermute | solution.py:31
  170.0 25.9 %collective-permute-start.11 = (bf16[15,128,256]{2,1,0:T(8,128)(2,1)}, bf16[15,128,256]{2,1,0:T(8,128)(2,1)}, u32[]{:S(2)}, u32[]{:S(2)}) collective-permute-start(bf16[15,128,256]{2,1,0:T(8,128)(2,1)} %get-tuple-element.90), channel_id=1, source_target_pairs={{0,24},{8,16},{16,8},{24,0},{1,25},{9,17},{17,9},{25,1},{2,26},{10... | collective-permute-start | bytes 2949128 | tf_op jit(solution)/shard_map/ppermute | solution.py:31
  171.2 43.9 %collective-permute-start.10 = (bf16[15,128,256]{2,1,0:T(8,128)(2,1)}, bf16[15,128,256]{2,1,0:T(8,128)(2,1)}, u32[]{:S(2)}, u32[]{:S(2)}) collective-permute-start(bf16[15,128,256]{2,1,0:T(8,128)(2,1)} %get-tuple-element.91), channel_id=1, source_target_pairs={{0,16},{8,24},{16,0},{24,8},{1,17},{9,25},{17,1},{25,9},{2,18},{10... | collective-permute-start | bytes 2949128 | tf_op jit(solution)/shard_map/ppermute | solution.py:31
  173.0 42.1 %collective-permute-start.9 = (bf16[15,128,256]{2,1,0:T(8,128)(2,1)}, bf16[15,128,256]{2,1,0:T(8,128)(2,1)}, u32[]{:S(2)}, u32[]{:S(2)}) collective-permute-start(bf16[15,128,256]{2,1,0:T(8,128)(2,1)} %get-tuple-element.92), channel_id=1, source_target_pairs={{0,8},{8,0},{16,24},{24,16},{1,9},{9,1},{17,25},{25,17},{2,10},{10... | collective-permute-start | bytes 2949128 | tf_op jit(solution)/shard_map/ppermute | solution.py:31
  255.8 26.7 %collective-permute-start.15 = (bf16[15,128,256]{2,1,0:T(8,128)(2,1)}, bf16[15,128,256]{2,1,0:T(8,128)(2,1)S(1)}, u32[]{:S(2)}, u32[]{:S(2)}) collective-permute-start(bf16[15,128,256]{2,1,0:T(8,128)(2,1)} %get-tuple-element.81), channel_id=1, source_target_pairs={{0,6},{2,4},{4,2},{6,0},{1,7},{3,5},{5,3},{7,1},{8,14},{10,12},{12... | collective-permute-start | bytes 2949128 | tf_op jit(solution)/shard_map/ppermute | solution.py:31
  257.5 84.3 %collective-permute-start.14 = (bf16[15,128,256]{2,1,0:T(8,128)(2,1)}, bf16[15,128,256]{2,1,0:T(8,128)(2,1)}, u32[]{:S(2)}, u32[]{:S(2)}) collective-permute-start(bf16[15,128,256]{2,1,0:T(8,128)(2,1)} %get-tuple-element.82), channel_id=1, source_target_pairs={{0,4},{2,6},{4,0},{6,2},{1,5},{3,7},{5,1},{7,3},{8,12},{10,14},{12... | collective-permute-start | bytes 2949128 | tf_op jit(solution)/shard_map/ppermute | solution.py:31
  257.5 84.3 %collective-permute-start.13 = (bf16[15,128,256]{2,1,0:T(8,128)(2,1)S(1)}, bf16[15,128,256]{2,1,0:T(8,128)(2,1)}, u32[]{:S(2)}, u32[]{:S(2)}) collective-permute-start(bf16[15,128,256]{2,1,0:T(8,128)(2,1)S(1)} %get-tuple-element.83), channel_id=1, source_target_pairs={{0,2},{2,0},{4,6},{6,4},{1,3},{3,1},{5,7},{7,5},{8,10},{10,8},{12,... | collective-permute-start | bytes 2949128 | tf_op jit(solution)/shard_map/ppermute | solution.py:31
  344.0 25.7 %collective-permute-start.18 = (bf16[15,128,256]{2,1,0:T(8,128)(2,1)S(1)}, bf16[15,128,256]{2,1,0:T(8,128)(2,1)S(1)}, u32[]{:S(2)}, u32[]{:S(2)}) collective-permute-start(bf16[15,128,256]{2,1,0:T(8,128)(2,1)S(1)} %get-tuple-element.78), channel_id=1, source_target_pairs={{0,24},{8,16},{16,8},{24,0},{1,25},{9,17},{17,9},{25,1},{2,26},{10... | collective-permute-start | bytes 2949128 | tf_op jit(solution)/shard_map/ppermute | solution.py:31
  345.6 43.8 %collective-permute-start.17 = (bf16[15,128,256]{2,1,0:T(8,128)(2,1)S(1)}, bf16[15,128,256]{2,1,0:T(8,128)(2,1)S(1)}, u32[]{:S(2)}, u32[]{:S(2)}) collective-permute-start(bf16[15,128,256]{2,1,0:T(8,128)(2,1)S(1)} %get-tuple-element.79), channel_id=1, source_target_pairs={{0,16},{8,24},{16,0},{24,8},{1,17},{9,25},{17,1},{25,9},{2,18},{10... | collective-permute-start | bytes 2949128 | tf_op jit(solution)/shard_map/ppermute | solution.py:31
  347.0 42.4 %collective-permute-start.16 = (bf16[15,128,256]{2,1,0:T(8,128)(2,1)S(1)}, bf16[15,128,256]{2,1,0:T(8,128)(2,1)S(1)}, u32[]{:S(2)}, u32[]{:S(2)}) collective-permute-start(bf16[15,128,256]{2,1,0:T(8,128)(2,1)S(1)} %get-tuple-element.80), channel_id=1, source_target_pairs={{0,8},{8,0},{16,24},{24,16},{1,9},{9,1},{17,25},{25,17},{2,10},{10... | collective-permute-start | bytes 2949128 | tf_op jit(solution)/shard_map/ppermute | solution.py:31
  347.6 77.3 %collective-permute-start.19 = (bf16[32,128,256]{2,1,0:T(8,128)(2,1)S(1)}, bf16[32,128,256]{2,1,0:T(8,128)(2,1)}, u32[]{:S(2)}, u32[]{:S(2)}) collective-permute-start(bf16[32,128,256]{2,1,0:T(8,128)(2,1)S(1)} %get-tuple-element.59), channel_id=1, source_target_pairs={{0,2},{2,4},{4,6},{6,0},{1,3},{3,5},{5,7},{7,1},{8,10},{10,12},{12... | collective-permute-start | bytes 6291464 | tf_op jit(solution)/shard_map/ppermute | solution.py:141
  347.6 91.3 %collective-permute-start.20 = (bf16[32,128,256]{2,1,0:T(8,128)(2,1)S(1)}, bf16[32,128,256]{2,1,0:T(8,128)(2,1)S(1)}, u32[]{:S(2)}, u32[]{:S(2)}) collective-permute-start(bf16[32,128,256]{2,1,0:T(8,128)(2,1)S(1)} %get-tuple-element.60), channel_id=1, source_target_pairs={{0,6},{2,0},{4,2},{6,4},{1,7},{3,1},{5,3},{7,5},{8,14},{10,8},{12,... | collective-permute-start | bytes 6291464 | tf_op jit(solution)/shard_map/ppermute | solution.py:141
  461.9 50.7 %collective-permute-start.22 = (bf16[32,128,256]{2,1,0:T(8,128)(2,1)}, bf16[32,128,256]{2,1,0:T(8,128)(2,1)}, u32[]{:S(2)}, u32[]{:S(2)}) collective-permute-start(bf16[32,128,256]{2,1,0:T(8,128)(2,1)} %get-tuple-element.70), channel_id=1, source_target_pairs={{0,2},{2,4},{4,6},{6,0},{1,3},{3,5},{5,7},{7,1},{8,10},{10,12},{12... | collective-permute-start | bytes 6291464 | tf_op jit(solution)/shard_map/ppermute | solution.py:141
  468.9 88.5 %collective-permute-start.25 = (bf16[32,128,256]{2,1,0:T(8,128)(2,1)}, bf16[32,128,256]{2,1,0:T(8,128)(2,1)}, u32[]{:S(2)}, u32[]{:S(2)}) collective-permute-start(bf16[32,128,256]{2,1,0:T(8,128)(2,1)} %fusion.13), channel_id=1, source_target_pairs={{0,2},{2,4},{4,6},{6,0},{1,3},{3,5},{5,7},{7,1},{8,10},{10,12},{12... | collective-permute-start | bytes 6291464 | tf_op jit(solution)/shard_map/ppermute | solution.py:151
  470.7 131.7 %collective-permute-start.24 = (bf16[32,128,256]{2,1,0:T(8,128)(2,1)S(1)}, bf16[32,128,256]{2,1,0:T(8,128)(2,1)}, u32[]{:S(2)}, u32[]{:S(2)}) collective-permute-start(bf16[32,128,256]{2,1,0:T(8,128)(2,1)S(1)} %get-tuple-element.69), channel_id=1, source_target_pairs={{0,6},{2,0},{4,2},{6,4},{1,7},{3,1},{5,3},{7,5},{8,14},{10,8},{12,... | collective-permute-start | bytes 6291464 | tf_op jit(solution)/shard_map/ppermute | solution.py:141
  518.4 128.1 %collective-permute-start.23 = (bf16[32,128,256]{2,1,0:T(8,128)(2,1)}, bf16[32,128,256]{2,1,0:T(8,128)(2,1)}, u32[]{:S(2)}, u32[]{:S(2)}) collective-permute-start(bf16[32,128,256]{2,1,0:T(8,128)(2,1)} %fusion.15), channel_id=1, source_target_pairs={{0,2},{2,4},{4,6},{6,0},{1,3},{3,5},{5,7},{7,1},{8,10},{10,12},{12... | collective-permute-start | bytes 6291464 | tf_op jit(solution)/shard_map/ppermute | solution.py:151
  (12 other events, 91.2 us)

commit v4 on v3

--- a/solution.py
+++ b/solution.py
@@ -195,7 +195,10 @@
         column.append(next_leg(plane[part], "vb"))
 
     def amplitude_of(part):
-        mirrored = assemble(next_leg(column[part], "va"))
+        back = next_leg(column[part], "va")
+        if part + 1 < parts:
+            back, column[part + 1][:-1] = lax.optimization_barrier((back, column[part + 1][:-1]))
+        mirrored = assemble(back)
         rows = slice(part * width, (part + 1) * width)
         energy_gap = energy_a[None, None, rows] + energy_b[None, :, None] - pair_energy
         wide = 2.0 * turned[part].astype(jnp.float32) - mirrored.astype(jnp.float32)
@@ -215,6 +218,8 @@
         keep, send = contract(cells, right_fit, amplitude_of(part), send_type)
         if part:
             send, hops[-1] = lax.optimization_barrier((send, hops[-1]))
+        if part + 1 < parts:
+            send, column[part + 1][-1] = lax.optimization_barrier((send, column[part + 1][-1]))
         got = lax.ppermute(send, "pair", swap)
         keep, got = keep.reshape(shape), got.reshape(shape)
 

time: 660 us -> 617 us (0.935)
  waiting for transfers between devices: 417 us -> 374 us
    ppermute x18, waiting for transfers between devices: 224 us -> 173 us  [leg(): held.append(lax.ppermute(get(step), axis, partners(side, step)))]
    ppermute x2, waiting for transfers between devices: 19 us -> 26.8 us  [shards(): got = lax.ppermute(send, 'pair', swap)]
  transfers between devices with their start and end apart: 26 -> 26, of which waited for: 19 -> 19; matrix products, arithmetic and copies ran while one was open for 13% -> 14% of each run, Pallas kernels for 4% -> 9%
where the time goes in v4:
time: 617 us; the launch traced here: 616 us
  waiting for transfers between devices  374 us (61%)
  matrix products  65.4 us (11%)
  other arithmetic  61.8 us (10%)
  Pallas kernels  58 us (9%)
  starting transfers between devices  34.9 us (6%)
  local copies, waits for them, and re-layouts  22.6 us (4%)
    ppermute x18, waiting for transfers between devices, leg(): held.append(lax.ppermute(get(step), axis, partners(side, step)))  173 us
    ppermute x4, waiting for transfers between devices, first_hops(): lax.ppermute(x, 'vb', ring(count, sign))  91 us
    ppermute x2, waiting for transfers between devices, last_hops(): running = lax.ppermute(running, 'vb', ring(count, sign))  83.2 us
    pallas_call x2, Pallas kernels, contract(): pl.pallas_call(functools.partial(contract_kernel, dom // BLOCK), out_shap...  58 us
    dot_general x2, matrix products, shards(): jnp.einsum('pbk,pak->pba', right_fit, rows, preferred_element_type=jnp.fl...  32.7 us
    dot_general x2, matrix products, shards(): jnp.einsum('pak,pbk->pab', left_fit, columns, preferred_element_type=jnp....  32.7 us
    ppermute x2, waiting for transfers between devices, shards(): got = lax.ppermute(send, 'pair', swap)  26.8 us
    ppermute x18, starting transfers between devices, leg(): held.append(lax.ppermute(get(step), axis, partners(side, step)))  25.9 us
  transfers between devices with their start and end apart: 26, of which 19 were waited for; matrix products, arithmetic and copies ran while one was open for 14% of the time, Pallas kernels for 9%

profile of v4, /device:TPU:0, one launch (start us, length us, event | category | flops | bytes accessed | tf_op | source)
XLA Modules:
  0.0 616.5 jit_solution(6712926583959307982)
XLA Ops:
  0.0 16.3 %fusion.19 = bf16[15,512,256]{2,1,0:T(8,128)(2,1)} fusion(bf16[15,512,1536]{2,1,0:T(8,128)(2,1)} %param.6, bf16[15,512,1536]{2,1,0:T(8,128)(2,1)} %right.3), kind=kOutput, calls=%fused_computation.36 | convolution fusion | flops 6041763840 | bytes 39321600 | tf_op jit(solution)/shard_map/pak,pbk->pab/dot_general | solution.py:176
  24.6 16.3 %fusion.16 = bf16[15,512,256]{2,1,0:T(8,128)(2,1)} fusion(bf16[15,512,1536]{2,1,0:T(8,128)(2,1)} %param.6, bf16[15,512,1536]{2,1,0:T(8,128)(2,1)} %right.3), kind=kOutput, calls=%fused_computation.35 | convolution fusion | flops 6041763840 | bytes 39321600 | tf_op jit(solution)/shard_map/pak,pbk->pab/dot_general | solution.py:176
  40.9 16.4 %fusion.22 = bf16[15,512,256]{2,1,0:T(8,128)(2,1)} fusion(bf16[15,512,1536]{2,1,0:T(8,128)(2,1)} %right.3, bf16[15,512,1536]{2,1,0:T(8,128)(2,1)} %param.6), kind=kOutput, calls=%fused_computation.37 | convolution fusion | flops 6041763840 | bytes 39321600 | tf_op jit(solution)/shard_map/pbk,pak->pba/dot_general | solution.py:181
  57.3 9.8 %collective-permute-done.1 = bf16[15,128,256]{2,1,0:T(8,128)(2,1)S(1)} collective-permute-done((bf16[15,128,256]{2,1,0:T(8,128)(2,1)}, bf16[15,128,256]{2,1,0:T(8,128)(2,1)S(1)}, u32[]{:S(2)}, u32[]{:S(2)}) %collective-permute-start.1) | collective-permute-done | bytes 983072 | tf_op jit(solution)/shard_map/ppermute | solution.py:31
  82.3 14.8 %collective-permute-done.5 = bf16[15,128,256]{2,1,0:T(8,128)(2,1)S(1)} collective-permute-done((bf16[15,128,256]{2,1,0:T(8,128)(2,1)}, bf16[15,128,256]{2,1,0:T(8,128)(2,1)S(1)}, u32[]{:S(2)}, u32[]{:S(2)}) %collective-permute-start.5) | collective-permute-done | bytes 983072 | tf_op jit(solution)/shard_map/ppermute | solution.py:31
  98.8 16.3 %fusion.25 = bf16[15,512,256]{2,1,0:T(8,128)(2,1)} fusion(bf16[15,512,1536]{2,1,0:T(8,128)(2,1)} %right.3, bf16[15,512,1536]{2,1,0:T(8,128)(2,1)} %param.6), kind=kOutput, calls=%fused_computation.38 | convolution fusion | flops 6041763840 | bytes 39321600 | tf_op jit(solution)/shard_map/pbk,pak->pba/dot_general | solution.py:181
  117.5 48.7 %collective-permute-done.7 = bf16[15,128,256]{2,1,0:T(8,128)(2,1)} collective-permute-done((bf16[15,128,256]{2,1,0:T(8,128)(2,1)}, bf16[15,128,256]{2,1,0:T(8,128)(2,1)}, u32[]{:S(2)}, u32[]{:S(2)}) %collective-permute-start.7) | collective-permute-done | bytes 983072 | tf_op jit(solution)/shard_map/ppermute | solution.py:31
  181.4 14.6 %collective-permute-done.11 = bf16[15,128,256]{2,1,0:T(8,128)(2,1)} collective-permute-done((bf16[15,128,256]{2,1,0:T(8,128)(2,1)}, bf16[15,128,256]{2,1,0:T(8,128)(2,1)}, u32[]{:S(2)}, u32[]{:S(2)}) %collective-permute-start.11) | collective-permute-done | bytes 983072 | tf_op jit(solution)/shard_map/ppermute | solution.py:31
  198.4 16.7 %collective-permute-done.10 = bf16[15,128,256]{2,1,0:T(8,128)(2,1)} collective-permute-done((bf16[15,128,256]{2,1,0:T(8,128)(2,1)}, bf16[15,128,256]{2,1,0:T(8,128)(2,1)}, u32[]{:S(2)}, u32[]{:S(2)}) %collective-permute-start.10) | collective-permute-done | bytes 983072 | tf_op jit(solution)/shard_map/ppermute | solution.py:31
  215.1 8.7 %collective-permute-done.13 = bf16[15,128,256]{2,1,0:T(8,128)(2,1)S(1)} collective-permute-done((bf16[15,128,256]{2,1,0:T(8,128)(2,1)}, bf16[15,128,256]{2,1,0:T(8,128)(2,1)S(1)}, u32[]{:S(2)}, u32[]{:S(2)}) %collective-permute-start.13) | collective-permute-done | bytes 983072 | tf_op jit(solution)/shard_map/ppermute | solution.py:31
  223.8 18.1 %collective-permute-done.12 = bf16[15,128,256]{2,1,0:T(8,128)(2,1)} collective-permute-done((bf16[15,128,256]{2,1,0:T(8,128)(2,1)}, bf16[15,128,256]{2,1,0:T(8,128)(2,1)}, u32[]{:S(2)}, u32[]{:S(2)}) %collective-permute-start.12) | collective-permute-done | bytes 983072 | tf_op jit(solution)/shard_map/ppermute | solution.py:31
  249.9 29.0 %contract.2 = (f32[128,128,256]{2,1,0:T(8,128)}, bf16[128,128,256]{2,1,0:T(8,128)(2,1)}) custom-call(s32[180]{0:T(256)} %reshape.133.cells, bf16[15,512,1536]{2,1,0:T(8,128)(2,1)} %right.3, bf16[15,512,256]{2,1,0:T(8,128)(2,1)} %fusion.11.amplitude), custom_call_target="tpu_custom_call" | custom-call | flops 6039797760 | bytes 52690944 | tf_op jit(solution)/shard_map/contract/pallas_call | solution.py:96
  279.0 13.4 %collective-permute-done.15 = bf16[128,128,256]{2,1,0:T(8,128)(2,1)} collective-permute-done((bf16[128,128,256]{2,1,0:T(8,128)(2,1)}, bf16[128,128,256]{2,1,0:T(8,128)(2,1)}, u32[]{:S(2)}, u32[]{:S(2)}) %collective-permute-start.15) | collective-permute-done | bytes 8388640 | tf_op jit(solution)/shard_map/ppermute | solution.py:223
  292.5 6.2 %fusion.29 = (bf16[32,128,256]{2,1,0:T(8,128)(2,1)S(1)}, bf16[32,128,256]{2,1,0:T(8,128)(2,1)S(1)}) fusion(f32[4,32,128,256]{3,2,1,0:T(8,128)} %bitcast.139, s32[]{:T(128)S(6)} %select_n.152, bf16[4,32,128,256]{3,2,1,0:T(8,128)(2,1)} %bitcast.46, s32[]{:T(128)S(6)} %select_n.150), kind=kLoop, calls=%fused_computation.40 | loop fusion | flops 6291456 | bytes 16777224 | tf_op jit(solution)/shard_map/convert_element_type | solution.py:137
  308.3 18.2 %collective-permute-done.18 = bf16[15,128,256]{2,1,0:T(8,128)(2,1)S(1)} collective-permute-done((bf16[15,128,256]{2,1,0:T(8,128)(2,1)S(1)}, bf16[15,128,256]{2,1,0:T(8,128)(2,1)S(1)}, u32[]{:S(2)}, u32[]{:S(2)}) %collective-permute-start.18) | collective-permute-done | bytes 983072 | tf_op jit(solution)/shard_map/ppermute | solution.py:31
  326.5 20.2 %collective-permute-done.17 = bf16[15,128,256]{2,1,0:T(8,128)(2,1)S(1)} collective-permute-done((bf16[15,128,256]{2,1,0:T(8,128)(2,1)S(1)}, bf16[15,128,256]{2,1,0:T(8,128)(2,1)S(1)}, u32[]{:S(2)}, u32[]{:S(2)}) %collective-permute-start.17) | collective-permute-done | bytes 983072 | tf_op jit(solution)/shard_map/ppermute | solution.py:31
  353.2 29.0 %contract.3 = (f32[128,128,256]{2,1,0:T(8,128)}, bf16[128,128,256]{2,1,0:T(8,128)(2,1)}) custom-call(s32[180]{0:T(256)} %reshape.133.cells, bf16[15,512,1536]{2,1,0:T(8,128)(2,1)} %right.3, bf16[15,512,256]{2,1,0:T(8,128)(2,1)} %fusion.9.amplitude), custom_call_target="tpu_custom_call" | custom-call | flops 6039797760 | bytes 52690944 | tf_op jit(solution)/shard_map/contract/pallas_call | solution.py:96
  382.2 14.0 %collective-permute-done.20 = bf16[32,128,256]{2,1,0:T(8,128)(2,1)S(1)} collective-permute-done((bf16[32,128,256]{2,1,0:T(8,128)(2,1)S(1)}, bf16[32,128,256]{2,1,0:T(8,128)(2,1)S(1)}, u32[]{:S(2)}, u32[]{:S(2)}) %collective-permute-start.20) | collective-permute-done | bytes 2097184 | tf_op jit(solution)/shard_map/ppermute | solution.py:141
  396.3 13.4 %collective-permute-done.21 = bf16[128,128,256]{2,1,0:T(8,128)(2,1)S(1)} collective-permute-done((bf16[128,128,256]{2,1,0:T(8,128)(2,1)}, bf16[128,128,256]{2,1,0:T(8,128)(2,1)S(1)}, u32[]{:S(2)}, u32[]{:S(2)}) %collective-permute-start.21) | collective-permute-done | bytes 8388640 | tf_op jit(solution)/shard_map/ppermute | solution.py:223
  409.6 9.6 %fusion.31 = (bf16[32,128,256]{2,1,0:T(8,128)(2,1)S(1)}, bf16[32,128,256]{2,1,0:T(8,128)(2,1)}) fusion(f32[4,32,128,256]{3,2,1,0:T(8,128)} %bitcast.142, s32[]{:T(128)S(6)} %select_n.152, bf16[4,32,128,256]{3,2,1,0:T(8,128)(2,1)S(1)} %bitcast.147, s32[]{:T(128)S(6)} %select_n.150), kind=kLoop, calls=%fused_computation.42 | loop fusion | flops 6291456 | bytes 16777224 | tf_op jit(solution)/shard_map/convert_element_type | solution.py:137
  430.1 39.9 %collective-permute-done.22 = bf16[32,128,256]{2,1,0:T(8,128)(2,1)} collective-permute-done((bf16[32,128,256]{2,1,0:T(8,128)(2,1)}, bf16[32,128,256]{2,1,0:T(8,128)(2,1)}, u32[]{:S(2)}, u32[]{:S(2)}) %collective-permute-start.22) | collective-permute-done | bytes 2097184 | tf_op jit(solution)/shard_map/ppermute | solution.py:141
  475.8 39.0 %collective-permute-done.25 = bf16[32,128,256]{2,1,0:T(8,128)(2,1)} collective-permute-done((bf16[32,128,256]{2,1,0:T(8,128)(2,1)}, bf16[32,128,256]{2,1,0:T(8,128)(2,1)}, u32[]{:S(2)}, u32[]{:S(2)}) %collective-permute-start.25) | collective-permute-done | bytes 2097184 | tf_op jit(solution)/shard_map/ppermute | solution.py:151
  522.7 37.0 %collective-permute-done.24 = bf16[32,128,256]{2,1,0:T(8,128)(2,1)} collective-permute-done((bf16[32,128,256]{2,1,0:T(8,128)(2,1)S(1)}, bf16[32,128,256]{2,1,0:T(8,128)(2,1)}, u32[]{:S(2)}, u32[]{:S(2)}) %collective-permute-start.24) | collective-permute-done | bytes 2097184 | tf_op jit(solution)/shard_map/ppermute | solution.py:141
  559.7 44.2 %collective-permute-done.23 = bf16[32,128,256]{2,1,0:T(8,128)(2,1)} collective-permute-done((bf16[32,128,256]{2,1,0:T(8,128)(2,1)}, bf16[32,128,256]{2,1,0:T(8,128)(2,1)}, u32[]{:S(2)}, u32[]{:S(2)}) %collective-permute-start.23) | collective-permute-done | bytes 2097184 | tf_op jit(solution)/shard_map/ppermute | solution.py:151
  (89 shorter events, 106.3 us)
Async XLA Ops:
  20.1 37.2 %collective-permute-start.2 = (bf16[15,128,256]{2,1,0:T(8,128)(2,1)}, bf16[15,128,256]{2,1,0:T(8,128)(2,1)S(1)}, u32[]{:S(2)}, u32[]{:S(2)}) collective-permute-start(bf16[15,128,256]{2,1,0:T(8,128)(2,1)} %get-tuple-element.119), channel_id=1, source_target_pairs={{0,24},{8,16},{16,8},{24,0},{1,25},{9,17},{17,9},{25,1},{2,26},{10... | collective-permute-start | bytes 2949128 | tf_op jit(solution)/shard_map/ppermute | solution.py:31
  24.0 43.0 %collective-permute-start.1 = (bf16[15,128,256]{2,1,0:T(8,128)(2,1)}, bf16[15,128,256]{2,1,0:T(8,128)(2,1)S(1)}, u32[]{:S(2)}, u32[]{:S(2)}) collective-permute-start(bf16[15,128,256]{2,1,0:T(8,128)(2,1)} %get-tuple-element.120), channel_id=1, source_target_pairs={{0,16},{8,24},{16,0},{24,8},{1,17},{9,25},{17,1},{25,9},{2,18},{10... | collective-permute-start | bytes 2949128 | tf_op jit(solution)/shard_map/ppermute | solution.py:31
  24.5 42.9 %collective-permute-start = (bf16[15,128,256]{2,1,0:T(8,128)(2,1)}, bf16[15,128,256]{2,1,0:T(8,128)(2,1)}, u32[]{:S(2)}, u32[]{:S(2)}) collective-permute-start(bf16[15,128,256]{2,1,0:T(8,128)(2,1)} %get-tuple-element.121), channel_id=1, source_target_pairs={{0,8},{8,0},{16,24},{24,16},{1,9},{9,1},{17,25},{25,17},{2,10},{10... | collective-permute-start | bytes 2949128 | tf_op jit(solution)/shard_map/ppermute | solution.py:31
  71.3 25.8 %collective-permute-start.5 = (bf16[15,128,256]{2,1,0:T(8,128)(2,1)}, bf16[15,128,256]{2,1,0:T(8,128)(2,1)S(1)}, u32[]{:S(2)}, u32[]{:S(2)}) collective-permute-start(bf16[15,128,256]{2,1,0:T(8,128)(2,1)} %get-tuple-element.115), channel_id=1, source_target_pairs={{0,24},{8,16},{16,8},{24,0},{1,25},{9,17},{17,9},{25,1},{2,26},{10... | collective-permute-start | bytes 2949128 | tf_op jit(solution)/shard_map/ppermute | solution.py:31
  73.0 44.3 %collective-permute-start.4 = (bf16[15,128,256]{2,1,0:T(8,128)(2,1)}, bf16[15,128,256]{2,1,0:T(8,128)(2,1)}, u32[]{:S(2)}, u32[]{:S(2)}) collective-permute-start(bf16[15,128,256]{2,1,0:T(8,128)(2,1)} %get-tuple-element.116), channel_id=1, source_target_pairs={{0,16},{8,24},{16,0},{24,8},{1,17},{9,25},{17,1},{25,9},{2,18},{10... | collective-permute-start | bytes 2949128 | tf_op jit(solution)/shard_map/ppermute | solution.py:31
  74.4 43.1 %collective-permute-start.3 = (bf16[15,128,256]{2,1,0:T(8,128)(2,1)}, bf16[15,128,256]{2,1,0:T(8,128)(2,1)}, u32[]{:S(2)}, u32[]{:S(2)}) collective-permute-start(bf16[15,128,256]{2,1,0:T(8,128)(2,1)} %get-tuple-element.117), channel_id=1, source_target_pairs={{0,8},{8,0},{16,24},{24,16},{1,9},{9,1},{17,25},{25,17},{2,10},{10... | collective-permute-start | bytes 2949128 | tf_op jit(solution)/shard_map/ppermute | solution.py:31
  78.5 39.0 %collective-permute-start.8 = (bf16[15,128,256]{2,1,0:T(8,128)(2,1)}, bf16[15,128,256]{2,1,0:T(8,128)(2,1)}, u32[]{:S(2)}, u32[]{:S(2)}) collective-permute-start(bf16[15,128,256]{2,1,0:T(8,128)(2,1)} %get-tuple-element.111), channel_id=1, source_target_pairs={{0,6},{2,4},{4,2},{6,0},{1,7},{3,5},{5,3},{7,1},{8,14},{10,12},{12... | collective-permute-start | bytes 2949128 | tf_op jit(solution)/shard_map/ppermute | solution.py:31
  82.3 83.9 %collective-permute-start.7 = (bf16[15,128,256]{2,1,0:T(8,128)(2,1)}, bf16[15,128,256]{2,1,0:T(8,128)(2,1)}, u32[]{:S(2)}, u32[]{:S(2)}) collective-permute-start(bf16[15,128,256]{2,1,0:T(8,128)(2,1)} %get-tuple-element.112), channel_id=1, source_target_pairs={{0,4},{2,6},{4,0},{6,2},{1,5},{3,7},{5,1},{7,3},{8,12},{10,14},{12... | collective-permute-start | bytes 2949128 | tf_op jit(solution)/shard_map/ppermute | solution.py:31
  97.0 69.1 %collective-permute-start.6 = (bf16[15,128,256]{2,1,0:T(8,128)(2,1)}, bf16[15,128,256]{2,1,0:T(8,128)(2,1)}, u32[]{:S(2)}, u32[]{:S(2)}) collective-permute-start(bf16[15,128,256]{2,1,0:T(8,128)(2,1)} %get-tuple-element.113), channel_id=1, source_target_pairs={{0,2},{2,0},{4,6},{6,4},{1,3},{3,1},{5,7},{7,5},{8,10},{10,8},{12,... | collective-permute-start | bytes 2949128 | tf_op jit(solution)/shard_map/ppermute | solution.py:31
  170.0 25.9 %collective-permute-start.11 = (bf16[15,128,256]{2,1,0:T(8,128)(2,1)}, bf16[15,128,256]{2,1,0:T(8,128)(2,1)}, u32[]{:S(2)}, u32[]{:S(2)}) collective-permute-start(bf16[15,128,256]{2,1,0:T(8,128)(2,1)} %get-tuple-element.107), channel_id=1, source_target_pairs={{0,24},{8,16},{16,8},{24,0},{1,25},{9,17},{17,9},{25,1},{2,26},{10... | collective-permute-start | bytes 2949128 | tf_op jit(solution)/shard_map/ppermute | solution.py:31
  171.2 43.9 %collective-permute-start.10 = (bf16[15,128,256]{2,1,0:T(8,128)(2,1)}, bf16[15,128,256]{2,1,0:T(8,128)(2,1)}, u32[]{:S(2)}, u32[]{:S(2)}) collective-permute-start(bf16[15,128,256]{2,1,0:T(8,128)(2,1)} %get-tuple-element.108), channel_id=1, source_target_pairs={{0,16},{8,24},{16,0},{24,8},{1,17},{9,25},{17,1},{25,9},{2,18},{10... | collective-permute-start | bytes 2949128 | tf_op jit(solution)/shard_map/ppermute | solution.py:31
  173.0 42.1 %collective-permute-start.9 = (bf16[15,128,256]{2,1,0:T(8,128)(2,1)}, bf16[15,128,256]{2,1,0:T(8,128)(2,1)}, u32[]{:S(2)}, u32[]{:S(2)}) collective-permute-start(bf16[15,128,256]{2,1,0:T(8,128)(2,1)} %get-tuple-element.109), channel_id=1, source_target_pairs={{0,8},{8,0},{16,24},{24,16},{1,9},{9,1},{17,25},{25,17},{2,10},{10... | collective-permute-start | bytes 2949128 | tf_op jit(solution)/shard_map/ppermute | solution.py:31
  177.2 46.5 %collective-permute-start.13 = (bf16[15,128,256]{2,1,0:T(8,128)(2,1)}, bf16[15,128,256]{2,1,0:T(8,128)(2,1)S(1)}, u32[]{:S(2)}, u32[]{:S(2)}) collective-permute-start(bf16[15,128,256]{2,1,0:T(8,128)(2,1)} %get-tuple-element.100), channel_id=1, source_target_pairs={{0,4},{2,6},{4,0},{6,2},{1,5},{3,7},{5,1},{7,3},{8,12},{10,14},{12... | collective-permute-start | bytes 2949128 | tf_op jit(solution)/shard_map/ppermute | solution.py:31
  177.2 64.7 %collective-permute-start.12 = (bf16[15,128,256]{2,1,0:T(8,128)(2,1)}, bf16[15,128,256]{2,1,0:T(8,128)(2,1)}, u32[]{:S(2)}, u32[]{:S(2)}) collective-permute-start(bf16[15,128,256]{2,1,0:T(8,128)(2,1)} %get-tuple-element.101), channel_id=1, source_target_pairs={{0,2},{2,0},{4,6},{6,4},{1,3},{3,1},{5,7},{7,5},{8,10},{10,8},{12,... | collective-permute-start | bytes 2949128 | tf_op jit(solution)/shard_map/ppermute | solution.py:31
  195.9 83.0 %collective-permute-start.14 = (bf16[15,128,256]{2,1,0:T(8,128)(2,1)}, bf16[15,128,256]{2,1,0:T(8,128)(2,1)}, u32[]{:S(2)}, u32[]{:S(2)}) collective-permute-start(bf16[15,128,256]{2,1,0:T(8,128)(2,1)} %get-tuple-element.99), channel_id=1, source_target_pairs={{0,6},{2,4},{4,2},{6,0},{1,7},{3,5},{5,3},{7,1},{8,14},{10,12},{12... | collective-permute-start | bytes 2949128 | tf_op jit(solution)/shard_map/ppermute | solution.py:31
  300.9 25.6 %collective-permute-start.18 = (bf16[15,128,256]{2,1,0:T(8,128)(2,1)S(1)}, bf16[15,128,256]{2,1,0:T(8,128)(2,1)S(1)}, u32[]{:S(2)}, u32[]{:S(2)}) collective-permute-start(bf16[15,128,256]{2,1,0:T(8,128)(2,1)S(1)} %get-tuple-element.96), channel_id=1, source_target_pairs={{0,24},{8,16},{16,8},{24,0},{1,25},{9,17},{17,9},{25,1},{2,26},{10... | collective-permute-start | bytes 2949128 | tf_op jit(solution)/shard_map/ppermute | solution.py:31
  302.2 44.6 %collective-permute-start.17 = (bf16[15,128,256]{2,1,0:T(8,128)(2,1)S(1)}, bf16[15,128,256]{2,1,0:T(8,128)(2,1)S(1)}, u32[]{:S(2)}, u32[]{:S(2)}) collective-permute-start(bf16[15,128,256]{2,1,0:T(8,128)(2,1)S(1)} %get-tuple-element.97), channel_id=1, source_target_pairs={{0,16},{8,24},{16,0},{24,8},{1,17},{9,25},{17,1},{25,9},{2,18},{10... | collective-permute-start | bytes 2949128 | tf_op jit(solution)/shard_map/ppermute | solution.py:31
  303.9 42.8 %collective-permute-start.16 = (bf16[15,128,256]{2,1,0:T(8,128)(2,1)S(1)}, bf16[15,128,256]{2,1,0:T(8,128)(2,1)S(1)}, u32[]{:S(2)}, u32[]{:S(2)}) collective-permute-start(bf16[15,128,256]{2,1,0:T(8,128)(2,1)S(1)} %get-tuple-element.98), channel_id=1, source_target_pairs={{0,8},{8,0},{16,24},{24,16},{1,9},{9,1},{17,25},{25,17},{2,10},{10... | collective-permute-start | bytes 2949128 | tf_op jit(solution)/shard_map/ppermute | solution.py:31
  304.5 77.7 %collective-permute-start.19 = (bf16[32,128,256]{2,1,0:T(8,128)(2,1)S(1)}, bf16[32,128,256]{2,1,0:T(8,128)(2,1)}, u32[]{:S(2)}, u32[]{:S(2)}) collective-permute-start(bf16[32,128,256]{2,1,0:T(8,128)(2,1)S(1)} %get-tuple-element.77), channel_id=1, source_target_pairs={{0,2},{2,4},{4,6},{6,0},{1,3},{3,5},{5,7},{7,1},{8,10},{10,12},{12... | collective-permute-start | bytes 6291464 | tf_op jit(solution)/shard_map/ppermute | solution.py:141
  304.5 91.8 %collective-permute-start.20 = (bf16[32,128,256]{2,1,0:T(8,128)(2,1)S(1)}, bf16[32,128,256]{2,1,0:T(8,128)(2,1)S(1)}, u32[]{:S(2)}, u32[]{:S(2)}) collective-permute-start(bf16[32,128,256]{2,1,0:T(8,128)(2,1)S(1)} %get-tuple-element.78), channel_id=1, source_target_pairs={{0,6},{2,0},{4,2},{6,4},{1,7},{3,1},{5,3},{7,5},{8,14},{10,8},{12,... | collective-permute-start | bytes 6291464 | tf_op jit(solution)/shard_map/ppermute | solution.py:141
  419.2 50.7 %collective-permute-start.22 = (bf16[32,128,256]{2,1,0:T(8,128)(2,1)}, bf16[32,128,256]{2,1,0:T(8,128)(2,1)}, u32[]{:S(2)}, u32[]{:S(2)}) collective-permute-start(bf16[32,128,256]{2,1,0:T(8,128)(2,1)} %get-tuple-element.88), channel_id=1, source_target_pairs={{0,2},{2,4},{4,6},{6,0},{1,3},{3,5},{5,7},{7,1},{8,10},{10,12},{12... | collective-permute-start | bytes 6291464 | tf_op jit(solution)/shard_map/ppermute | solution.py:141
  426.3 88.5 %collective-permute-start.25 = (bf16[32,128,256]{2,1,0:T(8,128)(2,1)}, bf16[32,128,256]{2,1,0:T(8,128)(2,1)}, u32[]{:S(2)}, u32[]{:S(2)}) collective-permute-start(bf16[32,128,256]{2,1,0:T(8,128)(2,1)} %fusion.13), channel_id=1, source_target_pairs={{0,2},{2,4},{4,6},{6,0},{1,3},{3,5},{5,7},{7,1},{8,10},{10,12},{12... | collective-permute-start | bytes 6291464 | tf_op jit(solution)/shard_map/ppermute | solution.py:151
  428.0 131.7 %collective-permute-start.24 = (bf16[32,128,256]{2,1,0:T(8,128)(2,1)S(1)}, bf16[32,128,256]{2,1,0:T(8,128)(2,1)}, u32[]{:S(2)}, u32[]{:S(2)}) collective-permute-start(bf16[32,128,256]{2,1,0:T(8,128)(2,1)S(1)} %get-tuple-element.87), channel_id=1, source_target_pairs={{0,6},{2,0},{4,2},{6,4},{1,7},{3,1},{5,3},{7,5},{8,14},{10,8},{12,... | collective-permute-start | bytes 6291464 | tf_op jit(solution)/shard_map/ppermute | solution.py:141
  475.8 128.1 %collective-permute-start.23 = (bf16[32,128,256]{2,1,0:T(8,128)(2,1)}, bf16[32,128,256]{2,1,0:T(8,128)(2,1)}, u32[]{:S(2)}, u32[]{:S(2)}) collective-permute-start(bf16[32,128,256]{2,1,0:T(8,128)(2,1)} %fusion.15), channel_id=1, source_target_pairs={{0,2},{2,4},{4,6},{6,0},{1,3},{3,5},{5,7},{7,1},{8,10},{10,12},{12... | collective-permute-start | bytes 6291464 | tf_op jit(solution)/shard_map/ppermute | solution.py:151
  (12 other events, 89.4 us)

commit v5 on v4

--- a/solution.py
+++ b/solution.py
@@ -132,25 +132,26 @@
     return [(sign, hops) for sign, hops in ((1, count // 2), (-1, (count - 1) // 2)) if hops]
 
 
-def first_sums(total_of, count):
+def hop_sums(total_of, arrivals, hop, count):
     me = lax.axis_index("vb")
-    return [total_of((me + sign * hops) % count).astype(jnp.bfloat16) for sign, hops in ways(count)]
-
-
-def first_hops(sums, count):
-    return [lax.ppermute(x, "vb", ring(count, sign)) for x, (sign, _) in zip(sums, ways(count))]
-
-
-def last_hops(total_of, arrivals, count):
-    me = lax.axis_index("vb")
-    arrived = []
-    for running, (sign, hops) in zip(arrivals, ways(count)):
-        for hop in range(1, hops):
-            mine = total_of((me + sign * (hops - hop)) % count)
-            running = (mine + running.astype(jnp.float32)).astype(jnp.bfloat16)
-            running = lax.ppermute(running, "vb", ring(count, sign))
-        arrived.append(running)
-    return arrived
+    sums = []
+    for way, (sign, hops) in enumerate(ways(count)):
+        if hop >= hops:
+            sums.append(None)
+            continue
+        mine = total_of((me + sign * (hops - hop)) % count)
+        if hop:
+            mine = mine + arrivals[way].astype(jnp.float32)
+        sums.append(mine.astype(jnp.bfloat16))
+    return sums
+
+
+def make_hop(sums, arrivals, count):
+    made = []
+    for way, (sign, _) in enumerate(ways(count)):
+        going = sums[way]
+        made.append(arrivals[way] if going is None else lax.ppermute(going, "vb", ring(count, sign)))
+    return made
 
 
 def shards(left_fit, right_fit, occ_energy, virt_energy, pair_list, domain_blocks):
@@ -197,7 +198,7 @@
     def amplitude_of(part):
         back = next_leg(column[part], "va")
         if part + 1 < parts:
-            back, column[part + 1][:-1] = lax.optimization_barrier((back, column[part + 1][:-1]))
+            back, column[part + 1][:2] = lax.optimization_barrier((back, column[part + 1][:2]))
         mirrored = assemble(back)
         rows = slice(part * width, (part + 1) * width)
         energy_gap = energy_a[None, None, rows] + energy_b[None, :, None] - pair_energy
@@ -218,8 +219,11 @@
         keep, send = contract(cells, right_fit, amplitude_of(part), send_type)
         if part:
             send, hops[-1] = lax.optimization_barrier((send, hops[-1]))
+            sums = hop_sums(totals[-1], hops[-1], 1, vb_count)
+            send, sums = lax.optimization_barrier((send, sums))
+            hops[-1] = make_hop(sums, hops[-1], vb_count)
         if part + 1 < parts:
-            send, column[part + 1][-1] = lax.optimization_barrier((send, column[part + 1][-1]))
+            send, column[part + 1][2:] = lax.optimization_barrier((send, column[part + 1][2:]))
         got = lax.ppermute(send, "pair", swap)
         keep, got = keep.reshape(shape), got.reshape(shape)
 
@@ -227,13 +231,17 @@
             return pick(keep, owner) + pick(got, owner).astype(jnp.float32)
 
         totals.append(total_of)
-        sums = first_sums(total_of, vb_count)
+        sums = hop_sums(total_of, None, 0, vb_count)
+        if part:
+            sums, hops[-1] = lax.optimization_barrier((sums, hops[-1]))
         if part + 1 < parts:
             sums, column[part + 1] = lax.optimization_barrier((sums, column[part + 1]))
-        hops.append(first_hops(sums, vb_count))
+        hops.append(make_hop(sums, None, vb_count))
     pieces = []
     for part in range(parts):
-        arrived = last_hops(totals[part], hops[part], vb_count)
+        arrived = hops[part]
+        for hop in range(2 if part + 1 < parts else 1, vb_count // 2):
+            arrived = make_hop(hop_sums(totals[part], arrived, hop, vb_count), arrived, vb_count)
         if part:
             arrived, pieces[-1] = lax.optimization_barrier((arrived, pieces[-1]))
         mine = totals[part](vb_index)

time: 617 us -> 595 us (0.964)
  waiting for transfers between devices: 374 us -> 351 us
    ppermute x18, waiting for transfers between devices: 173 us -> 162 us  [leg(): held.append(lax.ppermute(get(step), axis, partners(side, step)))]
    ppermute x6, waiting for transfers between devices: 174 us -> 163 us  [make_hop(): lax.ppermute(going, 'vb', ring(count, sign))]
  transfers between devices with their start and end apart: 26 -> 26, of which waited for: 19 -> 18; matrix products, arithmetic and copies ran while one was open for 14% -> 16% of each run, Pallas kernels for 9% -> 10%
where the time goes in v5:
time: 595 us; the launch traced here: 594 us
  waiting for transfers between devices  351 us (59%)
  matrix products  65.4 us (11%)
  other arithmetic  63.6 us (11%)
  Pallas kernels  58 us (10%)
  starting transfers between devices  31.3 us (5%)
  local copies, waits for them, and re-layouts  24.7 us (4%)
    ppermute x6, waiting for transfers between devices, make_hop(): lax.ppermute(going, 'vb', ring(count, sign))  163 us
    ppermute x18, waiting for transfers between devices, leg(): held.append(lax.ppermute(get(step), axis, partners(side, step)))  162 us
    pallas_call x2, Pallas kernels, contract(): pl.pallas_call(functools.partial(contract_kernel, dom // BLOCK), out_shap...  58 us
    dot_general x2, matrix products, shards(): jnp.einsum('pbk,pak->pba', right_fit, rows, preferred_element_type=jnp.fl...  32.7 us
    dot_general x2, matrix products, shards(): jnp.einsum('pak,pbk->pab', left_fit, columns, preferred_element_type=jnp....  32.7 us
    convert_element_type x4, other arithmetic, hop_sums(): sums.append(mine.astype(jnp.bfloat16))  26.5 us
    ppermute x2, waiting for transfers between devices, shards(): got = lax.ppermute(send, 'pair', swap)  25.8 us
    ppermute x18, starting transfers between devices, leg(): held.append(lax.ppermute(get(step), axis, partners(side, step)))  22.9 us
  transfers between devices with their start and end apart: 26, of which 18 were waited for; matrix products, arithmetic and copies ran while one was open for 16% of the time, Pallas kernels for 10%

profile of v5, /device:TPU:0, one launch (start us, length us, event | category | flops | bytes accessed | tf_op | source)
XLA Modules:
  0.0 594.0 jit_solution(8439553152571306252)
XLA Ops:
  0.0 16.3 %fusion.19 = bf16[15,512,256]{2,1,0:T(8,128)(2,1)} fusion(bf16[15,512,1536]{2,1,0:T(8,128)(2,1)} %param.6, bf16[15,512,1536]{2,1,0:T(8,128)(2,1)} %right.3), kind=kOutput, calls=%fused_computation.36 | convolution fusion | flops 6041763840 | bytes 39321600 | tf_op jit(solution)/shard_map/pak,pbk->pab/dot_general | solution.py:177
  24.6 16.3 %fusion.16 = bf16[15,512,256]{2,1,0:T(8,128)(2,1)} fusion(bf16[15,512,1536]{2,1,0:T(8,128)(2,1)} %param.6, bf16[15,512,1536]{2,1,0:T(8,128)(2,1)} %right.3), kind=kOutput, calls=%fused_computation.35 | convolution fusion | flops 6041763840 | bytes 39321600 | tf_op jit(solution)/shard_map/pak,pbk->pab/dot_general | solution.py:177
  40.9 16.4 %fusion.22 = bf16[15,512,256]{2,1,0:T(8,128)(2,1)} fusion(bf16[15,512,1536]{2,1,0:T(8,128)(2,1)} %right.3, bf16[15,512,1536]{2,1,0:T(8,128)(2,1)} %param.6), kind=kOutput, calls=%fused_computation.37 | convolution fusion | flops 6041763840 | bytes 39321600 | tf_op jit(solution)/shard_map/pbk,pak->pba/dot_general | solution.py:182
  57.3 9.7 %collective-permute-done.1 = bf16[15,128,256]{2,1,0:T(8,128)(2,1)S(1)} collective-permute-done((bf16[15,128,256]{2,1,0:T(8,128)(2,1)}, bf16[15,128,256]{2,1,0:T(8,128)(2,1)S(1)}, u32[]{:S(2)}, u32[]{:S(2)}) %collective-permute-start.1) | collective-permute-done | bytes 983072 | tf_op jit(solution)/shard_map/ppermute | solution.py:31
  82.3 14.8 %collective-permute-done.5 = bf16[15,128,256]{2,1,0:T(8,128)(2,1)S(1)} collective-permute-done((bf16[15,128,256]{2,1,0:T(8,128)(2,1)}, bf16[15,128,256]{2,1,0:T(8,128)(2,1)S(1)}, u32[]{:S(2)}, u32[]{:S(2)}) %collective-permute-start.5) | collective-permute-done | bytes 983072 | tf_op jit(solution)/shard_map/ppermute | solution.py:31
  98.8 16.4 %fusion.25 = bf16[15,512,256]{2,1,0:T(8,128)(2,1)} fusion(bf16[15,512,1536]{2,1,0:T(8,128)(2,1)} %right.3, bf16[15,512,1536]{2,1,0:T(8,128)(2,1)} %param.6), kind=kOutput, calls=%fused_computation.38 | convolution fusion | flops 6041763840 | bytes 39321600 | tf_op jit(solution)/shard_map/pbk,pak->pba/dot_general | solution.py:182
  117.5 48.7 %collective-permute-done.7 = bf16[15,128,256]{2,1,0:T(8,128)(2,1)} collective-permute-done((bf16[15,128,256]{2,1,0:T(8,128)(2,1)}, bf16[15,128,256]{2,1,0:T(8,128)(2,1)}, u32[]{:S(2)}, u32[]{:S(2)}) %collective-permute-start.7) | collective-permute-done | bytes 983072 | tf_op jit(solution)/shard_map/ppermute | solution.py:31
  181.6 14.4 %collective-permute-done.11 = bf16[15,128,256]{2,1,0:T(8,128)(2,1)} collective-permute-done((bf16[15,128,256]{2,1,0:T(8,128)(2,1)}, bf16[15,128,256]{2,1,0:T(8,128)(2,1)}, u32[]{:S(2)}, u32[]{:S(2)}) %collective-permute-start.11) | collective-permute-done | bytes 983072 | tf_op jit(solution)/shard_map/ppermute | solution.py:31
  195.9 19.2 %collective-permute-done.10 = bf16[15,128,256]{2,1,0:T(8,128)(2,1)} collective-permute-done((bf16[15,128,256]{2,1,0:T(8,128)(2,1)}, bf16[15,128,256]{2,1,0:T(8,128)(2,1)}, u32[]{:S(2)}, u32[]{:S(2)}) %collective-permute-start.10) | collective-permute-done | bytes 983072 | tf_op jit(solution)/shard_map/ppermute | solution.py:31
  223.5 29.0 %contract.2 = (f32[128,128,256]{2,1,0:T(8,128)}, bf16[128,128,256]{2,1,0:T(8,128)(2,1)}) custom-call(s32[180]{0:T(256)} %reshape.133.cells, bf16[15,512,1536]{2,1,0:T(8,128)(2,1)} %right.3, bf16[15,512,256]{2,1,0:T(8,128)(2,1)} %fusion.11.amplitude), custom_call_target="tpu_custom_call" | custom-call | flops 6039797760 | bytes 52690944 | tf_op jit(solution)/shard_map/contract/pallas_call | solution.py:96
  252.5 13.2 %collective-permute-done.13 = bf16[15,128,256]{2,1,0:T(8,128)(2,1)} collective-permute-done((bf16[15,128,256]{2,1,0:T(8,128)(2,1)}, bf16[15,128,256]{2,1,0:T(8,128)(2,1)}, u32[]{:S(2)}, u32[]{:S(2)}) %collective-permute-start.13) | collective-permute-done | bytes 983072 | tf_op jit(solution)/shard_map/ppermute | solution.py:31
  265.7 13.5 %collective-permute-done.15 = bf16[128,128,256]{2,1,0:T(8,128)(2,1)} collective-permute-done((bf16[128,128,256]{2,1,0:T(8,128)(2,1)}, bf16[128,128,256]{2,1,0:T(8,128)(2,1)}, u32[]{:S(2)}, u32[]{:S(2)}) %collective-permute-start.15) | collective-permute-done | bytes 8388640 | tf_op jit(solution)/shard_map/ppermute | solution.py:227
  279.2 7.6 %fusion.29 = (bf16[32,128,256]{2,1,0:T(8,128)(2,1)S(1)}, bf16[32,128,256]{2,1,0:T(8,128)(2,1)}) fusion(f32[4,32,128,256]{3,2,1,0:T(8,128)} %bitcast.139, s32[]{:T(128)S(6)} %select_n.152, bf16[4,32,128,256]{3,2,1,0:T(8,128)(2,1)} %bitcast.46, s32[]{:T(128)S(6)} %select_n.150), kind=kLoop, calls=%fused_computation.40 | loop fusion | flops 6291456 | bytes 16777224 | tf_op jit(solution)/shard_map/convert_element_type | solution.py:145
  297.6 18.5 %collective-permute-done.18 = bf16[15,128,256]{2,1,0:T(8,128)(2,1)} collective-permute-done((bf16[15,128,256]{2,1,0:T(8,128)(2,1)}, bf16[15,128,256]{2,1,0:T(8,128)(2,1)}, u32[]{:S(2)}, u32[]{:S(2)}) %collective-permute-start.18) | collective-permute-done | bytes 983072 | tf_op jit(solution)/shard_map/ppermute | solution.py:31
  316.1 20.2 %collective-permute-done.17 = bf16[15,128,256]{2,1,0:T(8,128)(2,1)} collective-permute-done((bf16[15,128,256]{2,1,0:T(8,128)(2,1)}, bf16[15,128,256]{2,1,0:T(8,128)(2,1)}, u32[]{:S(2)}, u32[]{:S(2)}) %collective-permute-start.17) | collective-permute-done | bytes 983072 | tf_op jit(solution)/shard_map/ppermute | solution.py:31
  344.5 29.0 %contract.3 = (f32[128,128,256]{2,1,0:T(8,128)}, bf16[128,128,256]{2,1,0:T(8,128)(2,1)}) custom-call(s32[180]{0:T(256)} %reshape.133.cells, bf16[15,512,1536]{2,1,0:T(8,128)(2,1)} %right.3, bf16[15,512,256]{2,1,0:T(8,128)(2,1)} %fusion.9.amplitude), custom_call_target="tpu_custom_call" | custom-call | flops 6039797760 | bytes 52690944 | tf_op jit(solution)/shard_map/contract/pallas_call | solution.py:96
  373.5 12.1 %collective-permute-done.20 = bf16[32,128,256]{2,1,0:T(8,128)(2,1)S(1)} collective-permute-done((bf16[32,128,256]{2,1,0:T(8,128)(2,1)S(1)}, bf16[32,128,256]{2,1,0:T(8,128)(2,1)S(1)}, u32[]{:S(2)}, u32[]{:S(2)}) %collective-permute-start.20) | collective-permute-done | bytes 2097184 | tf_op jit(solution)/shard_map/ppermute | solution.py:153
  385.6 6.0 %fusion.15 = bf16[32,128,256]{2,1,0:T(8,128)(2,1)} fusion(bf16[32,128,256]{2,1,0:T(8,128)(2,1)S(1)} %collective-permute-done.19, f32[4,32,128,256]{3,2,1,0:T(8,128)} %bitcast.140, s32[]{:T(128)S(6)} %select_n.154, bf16[4,32,128,256]{3,2,1,0:T(8,128)(2,1)} %bitcast.46), kind=kLoop, calls=%fused_computation.22 | loop fusion | flops 5242880 | bytes 10485764 | tf_op jit(solution)/shard_map/convert_element_type | solution.py:145
  393.1 12.3 %collective-permute-done.21 = bf16[128,128,256]{2,1,0:T(8,128)(2,1)S(1)} collective-permute-done((bf16[128,128,256]{2,1,0:T(8,128)(2,1)S(1)}, bf16[128,128,256]{2,1,0:T(8,128)(2,1)S(1)}, u32[]{:S(2)}, u32[]{:S(2)}) %collective-permute-start.21) | collective-permute-done | bytes 8388640 | tf_op jit(solution)/shard_map/ppermute | solution.py:227
  405.5 8.2 %fusion.31 = (bf16[32,128,256]{2,1,0:T(8,128)(2,1)S(1)}, bf16[32,128,256]{2,1,0:T(8,128)(2,1)S(1)}) fusion(f32[4,32,128,256]{3,2,1,0:T(8,128)} %bitcast.142, s32[]{:T(128)S(6)} %select_n.152, bf16[4,32,128,256]{3,2,1,0:T(8,128)(2,1)S(1)} %bitcast.147, s32[]{:T(128)S(6)} %select_n.150), kind=kLoop, calls=%fused_computation.42 | loop fusion | flops 6291456 | bytes 16777224 | tf_op jit(solution)/shard_map/convert_element_type | solution.py:145
  413.7 28.6 %collective-permute-done.22 = bf16[32,128,256]{2,1,0:T(8,128)(2,1)S(1)} collective-permute-done((bf16[32,128,256]{2,1,0:T(8,128)(2,1)}, bf16[32,128,256]{2,1,0:T(8,128)(2,1)S(1)}, u32[]{:S(2)}, u32[]{:S(2)}) %collective-permute-start.22) | collective-permute-done | bytes 2097184 | tf_op jit(solution)/shard_map/ppermute | solution.py:153
  446.2 46.5 %collective-permute-done.23 = bf16[32,128,256]{2,1,0:T(8,128)(2,1)S(1)} collective-permute-done((bf16[32,128,256]{2,1,0:T(8,128)(2,1)S(1)}, bf16[32,128,256]{2,1,0:T(8,128)(2,1)S(1)}, u32[]{:S(2)}, u32[]{:S(2)}) %collective-permute-start.23) | collective-permute-done | bytes 2097184 | tf_op jit(solution)/shard_map/ppermute | solution.py:153
  505.2 29.5 %collective-permute-done.25 = bf16[32,128,256]{2,1,0:T(8,128)(2,1)} collective-permute-done((bf16[32,128,256]{2,1,0:T(8,128)(2,1)S(1)}, bf16[32,128,256]{2,1,0:T(8,128)(2,1)}, u32[]{:S(2)}, u32[]{:S(2)}) %collective-permute-start.25) | collective-permute-done | bytes 2097184 | tf_op jit(solution)/shard_map/ppermute | solution.py:153
  534.7 46.8 %collective-permute-done.24 = bf16[32,128,256]{2,1,0:T(8,128)(2,1)} collective-permute-done((bf16[32,128,256]{2,1,0:T(8,128)(2,1)}, bf16[32,128,256]{2,1,0:T(8,128)(2,1)}, u32[]{:S(2)}, u32[]{:S(2)}) %collective-permute-start.24) | collective-permute-done | bytes 2097184 | tf_op jit(solution)/shard_map/ppermute | solution.py:153
  (99 shorter events, 100.6 us)
Async XLA Ops:
  20.1 37.2 %collective-permute-start.2 = (bf16[15,128,256]{2,1,0:T(8,128)(2,1)}, bf16[15,128,256]{2,1,0:T(8,128)(2,1)S(1)}, u32[]{:S(2)}, u32[]{:S(2)}) collective-permute-start(bf16[15,128,256]{2,1,0:T(8,128)(2,1)} %get-tuple-element.131), channel_id=1, source_target_pairs={{0,24},{8,16},{16,8},{24,0},{1,25},{9,17},{17,9},{25,1},{2,26},{10... | collective-permute-start | bytes 2949128 | tf_op jit(solution)/shard_map/ppermute | solution.py:31
  24.0 43.0 %collective-permute-start.1 = (bf16[15,128,256]{2,1,0:T(8,128)(2,1)}, bf16[15,128,256]{2,1,0:T(8,128)(2,1)S(1)}, u32[]{:S(2)}, u32[]{:S(2)}) collective-permute-start(bf16[15,128,256]{2,1,0:T(8,128)(2,1)} %get-tuple-element.132), channel_id=1, source_target_pairs={{0,16},{8,24},{16,0},{24,8},{1,17},{9,25},{17,1},{25,9},{2,18},{10... | collective-permute-start | bytes 2949128 | tf_op jit(solution)/shard_map/ppermute | solution.py:31
  24.5 42.9 %collective-permute-start = (bf16[15,128,256]{2,1,0:T(8,128)(2,1)}, bf16[15,128,256]{2,1,0:T(8,128)(2,1)}, u32[]{:S(2)}, u32[]{:S(2)}) collective-permute-start(bf16[15,128,256]{2,1,0:T(8,128)(2,1)} %get-tuple-element.133), channel_id=1, source_target_pairs={{0,8},{8,0},{16,24},{24,16},{1,9},{9,1},{17,25},{25,17},{2,10},{10... | collective-permute-start | bytes 2949128 | tf_op jit(solution)/shard_map/ppermute | solution.py:31
  71.3 25.8 %collective-permute-start.5 = (bf16[15,128,256]{2,1,0:T(8,128)(2,1)}, bf16[15,128,256]{2,1,0:T(8,128)(2,1)S(1)}, u32[]{:S(2)}, u32[]{:S(2)}) collective-permute-start(bf16[15,128,256]{2,1,0:T(8,128)(2,1)} %get-tuple-element.127), channel_id=1, source_target_pairs={{0,24},{8,16},{16,8},{24,0},{1,25},{9,17},{17,9},{25,1},{2,26},{10... | collective-permute-start | bytes 2949128 | tf_op jit(solution)/shard_map/ppermute | solution.py:31
  73.0 44.3 %collective-permute-start.4 = (bf16[15,128,256]{2,1,0:T(8,128)(2,1)}, bf16[15,128,256]{2,1,0:T(8,128)(2,1)}, u32[]{:S(2)}, u32[]{:S(2)}) collective-permute-start(bf16[15,128,256]{2,1,0:T(8,128)(2,1)} %get-tuple-element.128), channel_id=1, source_target_pairs={{0,16},{8,24},{16,0},{24,8},{1,17},{9,25},{17,1},{25,9},{2,18},{10... | collective-permute-start | bytes 2949128 | tf_op jit(solution)/shard_map/ppermute | solution.py:31
  74.4 43.1 %collective-permute-start.3 = (bf16[15,128,256]{2,1,0:T(8,128)(2,1)}, bf16[15,128,256]{2,1,0:T(8,128)(2,1)}, u32[]{:S(2)}, u32[]{:S(2)}) collective-permute-start(bf16[15,128,256]{2,1,0:T(8,128)(2,1)} %get-tuple-element.129), channel_id=1, source_target_pairs={{0,8},{8,0},{16,24},{24,16},{1,9},{9,1},{17,25},{25,17},{2,10},{10... | collective-permute-start | bytes 2949128 | tf_op jit(solution)/shard_map/ppermute | solution.py:31
  78.6 39.0 %collective-permute-start.8 = (bf16[15,128,256]{2,1,0:T(8,128)(2,1)}, bf16[15,128,256]{2,1,0:T(8,128)(2,1)}, u32[]{:S(2)}, u32[]{:S(2)}) collective-permute-start(bf16[15,128,256]{2,1,0:T(8,128)(2,1)} %get-tuple-element.123), channel_id=1, source_target_pairs={{0,6},{2,4},{4,2},{6,0},{1,7},{3,5},{5,3},{7,1},{8,14},{10,12},{12... | collective-permute-start | bytes 2949128 | tf_op jit(solution)/shard_map/ppermute | solution.py:31
  82.3 83.9 %collective-permute-start.7 = (bf16[15,128,256]{2,1,0:T(8,128)(2,1)}, bf16[15,128,256]{2,1,0:T(8,128)(2,1)}, u32[]{:S(2)}, u32[]{:S(2)}) collective-permute-start(bf16[15,128,256]{2,1,0:T(8,128)(2,1)} %get-tuple-element.124), channel_id=1, source_target_pairs={{0,4},{2,6},{4,0},{6,2},{1,5},{3,7},{5,1},{7,3},{8,12},{10,14},{12... | collective-permute-start | bytes 2949128 | tf_op jit(solution)/shard_map/ppermute | solution.py:31
  97.1 69.1 %collective-permute-start.6 = (bf16[15,128,256]{2,1,0:T(8,128)(2,1)}, bf16[15,128,256]{2,1,0:T(8,128)(2,1)}, u32[]{:S(2)}, u32[]{:S(2)}) collective-permute-start(bf16[15,128,256]{2,1,0:T(8,128)(2,1)} %get-tuple-element.125), channel_id=1, source_target_pairs={{0,2},{2,0},{4,6},{6,4},{1,3},{3,1},{5,7},{7,5},{8,10},{10,8},{12,... | collective-permute-start | bytes 2949128 | tf_op jit(solution)/shard_map/ppermute | solution.py:31
  170.0 25.9 %collective-permute-start.11 = (bf16[15,128,256]{2,1,0:T(8,128)(2,1)}, bf16[15,128,256]{2,1,0:T(8,128)(2,1)}, u32[]{:S(2)}, u32[]{:S(2)}) collective-permute-start(bf16[15,128,256]{2,1,0:T(8,128)(2,1)} %get-tuple-element.119), channel_id=1, source_target_pairs={{0,24},{8,16},{16,8},{24,0},{1,25},{9,17},{17,9},{25,1},{2,26},{10... | collective-permute-start | bytes 2949128 | tf_op jit(solution)/shard_map/ppermute | solution.py:31
  171.2 43.9 %collective-permute-start.10 = (bf16[15,128,256]{2,1,0:T(8,128)(2,1)}, bf16[15,128,256]{2,1,0:T(8,128)(2,1)}, u32[]{:S(2)}, u32[]{:S(2)}) collective-permute-start(bf16[15,128,256]{2,1,0:T(8,128)(2,1)} %get-tuple-element.120), channel_id=1, source_target_pairs={{0,16},{8,24},{16,0},{24,8},{1,17},{9,25},{17,1},{25,9},{2,18},{10... | collective-permute-start | bytes 2949128 | tf_op jit(solution)/shard_map/ppermute | solution.py:31
  173.0 42.1 %collective-permute-start.9 = (bf16[15,128,256]{2,1,0:T(8,128)(2,1)}, bf16[15,128,256]{2,1,0:T(8,128)(2,1)}, u32[]{:S(2)}, u32[]{:S(2)}) collective-permute-start(bf16[15,128,256]{2,1,0:T(8,128)(2,1)} %get-tuple-element.121), channel_id=1, source_target_pairs={{0,8},{8,0},{16,24},{24,16},{1,9},{9,1},{17,25},{25,17},{2,10},{10... | collective-permute-start | bytes 2949128 | tf_op jit(solution)/shard_map/ppermute | solution.py:31
  177.2 37.9 %collective-permute-start.12 = (bf16[15,128,256]{2,1,0:T(8,128)(2,1)}, bf16[15,128,256]{2,1,0:T(8,128)(2,1)S(1)}, u32[]{:S(2)}, u32[]{:S(2)}) collective-permute-start(bf16[15,128,256]{2,1,0:T(8,128)(2,1)} %get-tuple-element.113), channel_id=1, source_target_pairs={{0,2},{2,0},{4,6},{6,4},{1,3},{3,1},{5,7},{7,5},{8,10},{10,8},{12,... | collective-permute-start | bytes 2949128 | tf_op jit(solution)/shard_map/ppermute | solution.py:31
  179.1 73.4 %collective-permute-start.14 = (bf16[15,128,256]{2,1,0:T(8,128)(2,1)}, bf16[15,128,256]{2,1,0:T(8,128)(2,1)}, u32[]{:S(2)}, u32[]{:S(2)}) collective-permute-start(bf16[15,128,256]{2,1,0:T(8,128)(2,1)} %get-tuple-element.111), channel_id=1, source_target_pairs={{0,6},{2,4},{4,2},{6,0},{1,7},{3,5},{5,3},{7,1},{8,14},{10,12},{12... | collective-permute-start | bytes 2949128 | tf_op jit(solution)/shard_map/ppermute | solution.py:31
  195.9 69.8 %collective-permute-start.13 = (bf16[15,128,256]{2,1,0:T(8,128)(2,1)}, bf16[15,128,256]{2,1,0:T(8,128)(2,1)}, u32[]{:S(2)}, u32[]{:S(2)}) collective-permute-start(bf16[15,128,256]{2,1,0:T(8,128)(2,1)} %get-tuple-element.112), channel_id=1, source_target_pairs={{0,4},{2,6},{4,0},{6,2},{1,5},{3,7},{5,1},{7,3},{8,12},{10,14},{12... | collective-permute-start | bytes 2949128 | tf_op jit(solution)/shard_map/ppermute | solution.py:31
  290.3 25.9 %collective-permute-start.18 = (bf16[15,128,256]{2,1,0:T(8,128)(2,1)}, bf16[15,128,256]{2,1,0:T(8,128)(2,1)}, u32[]{:S(2)}, u32[]{:S(2)}) collective-permute-start(bf16[15,128,256]{2,1,0:T(8,128)(2,1)} %get-tuple-element.108), channel_id=1, source_target_pairs={{0,24},{8,16},{16,8},{24,0},{1,25},{9,17},{17,9},{25,1},{2,26},{10... | collective-permute-start | bytes 2949128 | tf_op jit(solution)/shard_map/ppermute | solution.py:31
  291.5 44.9 %collective-permute-start.17 = (bf16[15,128,256]{2,1,0:T(8,128)(2,1)}, bf16[15,128,256]{2,1,0:T(8,128)(2,1)}, u32[]{:S(2)}, u32[]{:S(2)}) collective-permute-start(bf16[15,128,256]{2,1,0:T(8,128)(2,1)} %get-tuple-element.109), channel_id=1, source_target_pairs={{0,16},{8,24},{16,0},{24,8},{1,17},{9,25},{17,1},{25,9},{2,18},{10... | collective-permute-start | bytes 2949128 | tf_op jit(solution)/shard_map/ppermute | solution.py:31
  293.2 43.2 %collective-permute-start.16 = (bf16[15,128,256]{2,1,0:T(8,128)(2,1)}, bf16[15,128,256]{2,1,0:T(8,128)(2,1)}, u32[]{:S(2)}, u32[]{:S(2)}) collective-permute-start(bf16[15,128,256]{2,1,0:T(8,128)(2,1)} %get-tuple-element.110), channel_id=1, source_target_pairs={{0,8},{8,0},{16,24},{24,16},{1,9},{9,1},{17,25},{25,17},{2,10},{10... | collective-permute-start | bytes 2949128 | tf_op jit(solution)/shard_map/ppermute | solution.py:31
  293.8 79.7 %collective-permute-start.19 = (bf16[32,128,256]{2,1,0:T(8,128)(2,1)}, bf16[32,128,256]{2,1,0:T(8,128)(2,1)S(1)}, u32[]{:S(2)}, u32[]{:S(2)}) collective-permute-start(bf16[32,128,256]{2,1,0:T(8,128)(2,1)} %get-tuple-element.83), channel_id=1, source_target_pairs={{0,2},{2,4},{4,6},{6,0},{1,3},{3,5},{5,7},{7,1},{8,10},{10,12},{12... | collective-permute-start | bytes 6291464 | tf_op jit(solution)/shard_map/ppermute | solution.py:153
  293.8 91.8 %collective-permute-start.20 = (bf16[32,128,256]{2,1,0:T(8,128)(2,1)S(1)}, bf16[32,128,256]{2,1,0:T(8,128)(2,1)S(1)}, u32[]{:S(2)}, u32[]{:S(2)}) collective-permute-start(bf16[32,128,256]{2,1,0:T(8,128)(2,1)S(1)} %get-tuple-element.84), channel_id=1, source_target_pairs={{0,6},{2,0},{4,2},{6,4},{1,7},{3,1},{5,3},{7,5},{8,14},{10,8},{12,... | collective-permute-start | bytes 6291464 | tf_op jit(solution)/shard_map/ppermute | solution.py:153
  392.3 50.1 %collective-permute-start.22 = (bf16[32,128,256]{2,1,0:T(8,128)(2,1)}, bf16[32,128,256]{2,1,0:T(8,128)(2,1)S(1)}, u32[]{:S(2)}, u32[]{:S(2)}) collective-permute-start(bf16[32,128,256]{2,1,0:T(8,128)(2,1)} %fusion.15), channel_id=1, source_target_pairs={{0,2},{2,4},{4,6},{6,0},{1,3},{3,5},{5,7},{7,1},{8,10},{10,12},{12... | collective-permute-start | bytes 6291464 | tf_op jit(solution)/shard_map/ppermute | solution.py:153
  442.4 50.3 %collective-permute-start.23 = (bf16[32,128,256]{2,1,0:T(8,128)(2,1)S(1)}, bf16[32,128,256]{2,1,0:T(8,128)(2,1)S(1)}, u32[]{:S(2)}, u32[]{:S(2)}) collective-permute-start(bf16[32,128,256]{2,1,0:T(8,128)(2,1)S(1)} %get-tuple-element.90), channel_id=1, source_target_pairs={{0,2},{2,4},{4,6},{6,0},{1,3},{3,5},{5,7},{7,1},{8,10},{10,12},{12... | collective-permute-start | bytes 6291464 | tf_op jit(solution)/shard_map/ppermute | solution.py:153
  442.4 92.3 %collective-permute-start.25 = (bf16[32,128,256]{2,1,0:T(8,128)(2,1)S(1)}, bf16[32,128,256]{2,1,0:T(8,128)(2,1)}, u32[]{:S(2)}, u32[]{:S(2)}) collective-permute-start(bf16[32,128,256]{2,1,0:T(8,128)(2,1)S(1)} %get-tuple-element.91), channel_id=1, source_target_pairs={{0,6},{2,0},{4,2},{6,4},{1,7},{3,1},{5,3},{7,5},{8,14},{10,8},{12,... | collective-permute-start | bytes 6291464 | tf_op jit(solution)/shard_map/ppermute | solution.py:153
  497.4 84.1 %collective-permute-start.24 = (bf16[32,128,256]{2,1,0:T(8,128)(2,1)}, bf16[32,128,256]{2,1,0:T(8,128)(2,1)}, u32[]{:S(2)}, u32[]{:S(2)}) collective-permute-start(bf16[32,128,256]{2,1,0:T(8,128)(2,1)} %fusion.14), channel_id=1, source_target_pairs={{0,2},{2,4},{4,6},{6,0},{1,3},{3,5},{5,7},{7,1},{8,10},{10,12},{12... | collective-permute-start | bytes 6291464 | tf_op jit(solution)/shard_map/ppermute | solution.py:153
  (17 other events, 221.2 us)

commit v6 on v5

--- a/solution.py
+++ b/solution.py
@@ -166,19 +166,22 @@
     energy_a = lax.dynamic_slice_in_dim(virt_energy, va_index * tile_rows, tile_rows)
     energy_b = lax.dynamic_slice_in_dim(virt_energy, vb_index * tile_rows, tile_rows)
 
-    parts = max(1, tile_rows // 256)
-    width = tile_rows // parts
+    widths = [min(128, tile_rows)]
+    while sum(widths) < tile_rows:
+        widths.append(min(256, tile_rows - sum(widths)))
+    parts = len(widths)
+    spans = [slice(sum(widths[:part]), sum(widths[: part + 1])) for part in range(parts)]
     first_energy = pick_energy(occ_energy, pair_list[:, 0])
     second_energy = pick_energy(occ_energy, pair_list[:, 1])
     pair_energy = (first_energy + second_energy)[:, None, None]
     tiles = []
     for part in range(parts):
-        columns = right_fit[:, part * width : (part + 1) * width]
+        columns = right_fit[:, spans[part]]
         tile = jnp.einsum("pak,pbk->pab", left_fit, columns, preferred_element_type=jnp.float32)
         tiles.append(tile.astype(jnp.bfloat16))
     turned = []
     for part in range(parts):
-        rows = left_fit[:, part * width : (part + 1) * width]
+        rows = left_fit[:, spans[part]]
         tile = jnp.einsum("pbk,pak->pba", right_fit, rows, preferred_element_type=jnp.float32)
         turned.append(tile.astype(jnp.bfloat16))
 
@@ -200,7 +203,7 @@
         if part + 1 < parts:
             back, column[part + 1][:2] = lax.optimization_barrier((back, column[part + 1][:2]))
         mirrored = assemble(back)
-        rows = slice(part * width, (part + 1) * width)
+        rows = spans[part]
         energy_gap = energy_a[None, None, rows] + energy_b[None, :, None] - pair_energy
         wide = 2.0 * turned[part].astype(jnp.float32) - mirrored.astype(jnp.float32)
         return (wide / energy_gap).astype(jnp.bfloat16)
@@ -213,7 +216,6 @@
 
     send_type = jnp.bfloat16 if vb_count <= 4 else jnp.float32
     swap = [(c, (c + 1) % pair_count) for c in range(pair_count)]
-    shape = (vb_count, slab * NOCC, BLOCK, width)
     totals, hops = [], []
     for part in range(parts):
         keep, send = contract(cells, right_fit, amplitude_of(part), send_type)
@@ -225,6 +227,7 @@
         if part + 1 < parts:
             send, column[part + 1][2:] = lax.optimization_barrier((send, column[part + 1][2:]))
         got = lax.ppermute(send, "pair", swap)
+        shape = (vb_count, slab * NOCC, BLOCK, widths[part])
         keep, got = keep.reshape(shape), got.reshape(shape)
 
         def total_of(owner, keep=keep, got=got):
@@ -247,8 +250,8 @@
         mine = totals[part](vb_index)
         for arrival in arrived:
             mine = mine + arrival.astype(jnp.float32)
-        mine = mine.reshape(slab, NOCC, BLOCK, width)
-        pieces.append(mine.transpose(0, 2, 1, 3).reshape(slab * BLOCK, NOCC, width))
+        mine = mine.reshape(slab, NOCC, BLOCK, widths[part])
+        pieces.append(mine.transpose(0, 2, 1, 3).reshape(slab * BLOCK, NOCC, widths[part]))
     return jnp.concatenate(pieces, axis=2)
 
 

time: 595 us -> 613 us (1.030); the launches traced: 594 us -> 604 us
  waiting for transfers between devices: 351 us -> 299 us
  starting transfers between devices: 31.3 us -> 60.6 us
  matrix products: 65.4 us -> 84.8 us
  Pallas kernels: 58 us -> 76.2 us
    ppermute x18 -> x27, waiting for transfers between devices: 162 us -> 124 us  [leg(): held.append(lax.ppermute(get(step), axis, partners(side, step)))]
    ppermute x18 -> x27, starting transfers between devices: 22.9 us -> 45.1 us  [leg(): held.append(lax.ppermute(get(step), axis, partners(side, step)))]
    pallas_call x2 -> x3, Pallas kernels: 58 us -> 76.2 us  [contract(): pl.pallas_call(functools.partial(contract_kernel, dom // BLOCK), out_shap...]
    ppermute x6 -> x9, waiting for transfers between devices: 163 us -> 149 us  [make_hop(): lax.ppermute(going, 'vb', ring(count, sign))]
    dot_general x2 -> x3, matrix products: 32.7 us -> 43 us  [shards(): jnp.einsum('pbk,pak->pba', right_fit, rows, preferred_element_type=jnp.fl...]
    dot_general x2 -> x3, matrix products: 32.7 us -> 41.8 us  [shards(): jnp.einsum('pak,pbk->pab', left_fit, columns, preferred_element_type=jnp....]
    ppermute x6 -> x9, starting transfers between devices: 8.48 us -> 15.3 us  [make_hop(): lax.ppermute(going, 'vb', ring(count, sign))]
    convert_element_type x4 -> x6, other arithmetic: 26.5 us -> 22.3 us  [hop_sums(): sums.append(mine.astype(jnp.bfloat16))]
  transfers between devices with their start and end apart: 26 -> 39, of which waited for: 18 -> 20; matrix products, arithmetic and copies ran while one was open for 16% -> 20% of each run, Pallas kernels for 10% -> 9%
where the time goes in v6:
time: 613 us; the launch traced here: 604 us
  waiting for transfers between devices  299 us (49%)
  matrix products  84.8 us (14%)
  Pallas kernels  76.2 us (12%)
  starting transfers between devices  60.6 us (10%)
  other arithmetic  59.8 us (10%)
  local copies, waits for them, and re-layouts  22.9 us (4%)
    ppermute x9, waiting for transfers between devices, make_hop(): lax.ppermute(going, 'vb', ring(count, sign))  149 us
    ppermute x27, waiting for transfers between devices, leg(): held.append(lax.ppermute(get(step), axis, partners(side, step)))  124 us
    pallas_call x3, Pallas kernels, contract(): pl.pallas_call(functools.partial(contract_kernel, dom // BLOCK), out_shap...  76.2 us
    ppermute x27, starting transfers between devices, leg(): held.append(lax.ppermute(get(step), axis, partners(side, step)))  45.1 us
    dot_general x3, matrix products, shards(): jnp.einsum('pbk,pak->pba', right_fit, rows, preferred_element_type=jnp.fl...  43 us
    dot_general x3, matrix products, shards(): jnp.einsum('pak,pbk->pab', left_fit, columns, preferred_element_type=jnp....  41.8 us
    ppermute x3, waiting for transfers between devices, shards(): got = lax.ppermute(send, 'pair', swap)  26 us
    convert_element_type x6, other arithmetic, hop_sums(): sums.append(mine.astype(jnp.bfloat16))  22.3 us
  transfers between devices with their start and end apart: 39, of which 20 were waited for; matrix products, arithmetic and copies ran while one was open for 20% of the time, Pallas kernels for 9%

profile of v6, /device:TPU:0, one launch (start us, length us, event | category | flops | bytes accessed | tf_op | source)
XLA Modules:
  0.0 604.1 jit_solution(7401925187651142003)
XLA Ops:
  0.0 12.9 %fusion.35 = bf16[15,512,128]{2,1,0:T(8,128)(2,1)S(1)} fusion(bf16[15,512,1536]{2,1,0:T(8,128)(2,1)} %param.6, bf16[15,512,1536]{2,1,0:T(8,128)(2,1)} %right.5), kind=kOutput, calls=%fused_computation.57 | convolution fusion | flops 3020881920 | bytes 31457280 | tf_op jit(solution)/shard_map/pak,pbk->pab/dot_general | solution.py:180
  18.6 16.3 %fusion.20 = bf16[15,512,256]{2,1,0:T(8,128)(2,1)} fusion(bf16[15,512,1536]{2,1,0:T(8,128)(2,1)} %param.6, bf16[15,512,1536]{2,1,0:T(8,128)(2,1)} %right.5), kind=kOutput, calls=%fused_computation.32 | convolution fusion | flops 6041763840 | bytes 39321600 | tf_op jit(solution)/shard_map/pak,pbk->pab/dot_general | solution.py:180
  34.9 12.8 %fusion.38 = bf16[15,512,128]{2,1,0:T(8,128)(2,1)S(1)} fusion(bf16[15,512,1536]{2,1,0:T(8,128)(2,1)} %right.5, bf16[15,512,1536]{2,1,0:T(8,128)(2,1)} %param.6), kind=kOutput, calls=%fused_computation.58 | convolution fusion | flops 3020881920 | bytes 31457280 | tf_op jit(solution)/shard_map/pbk,pak->pba/dot_general | solution.py:185
  53.3 16.5 %fusion.23 = bf16[15,512,256]{2,1,0:T(8,128)(2,1)} fusion(bf16[15,512,1536]{2,1,0:T(8,128)(2,1)} %right.5, bf16[15,512,1536]{2,1,0:T(8,128)(2,1)} %param.6), kind=kOutput, calls=%fused_computation.33 | convolution fusion | flops 6041763840 | bytes 39321600 | tf_op jit(solution)/shard_map/pbk,pak->pba/dot_general | solution.py:185
  78.3 12.6 %fusion.32 = bf16[15,512,128]{2,1,0:T(8,128)(2,1)S(1)} fusion(bf16[15,512,1536]{2,1,0:T(8,128)(2,1)} %param.6, bf16[15,512,1536]{2,1,0:T(8,128)(2,1)} %right.5), kind=kOutput, calls=%fused_computation.56 | convolution fusion | flops 3020881920 | bytes 31457280 | tf_op jit(solution)/shard_map/pak,pbk->pab/dot_general | solution.py:180
  99.4 18.5 %collective-permute-done.10 = bf16[15,128,128]{2,1,0:T(8,128)(2,1)} collective-permute-done((bf16[15,128,128]{2,1,0:T(8,128)(2,1)}, bf16[15,128,128]{2,1,0:T(8,128)(2,1)}, u32[]{:S(2)}, u32[]{:S(2)}) %collective-permute-start.10) | collective-permute-done | bytes 491552 | tf_op jit(solution)/shard_map/ppermute | solution.py:31
  123.7 13.7 %fusion.41 = bf16[15,512,128]{2,1,0:T(8,128)(2,1)} fusion(bf16[15,512,1536]{2,1,0:T(8,128)(2,1)} %right.5, bf16[15,512,1536]{2,1,0:T(8,128)(2,1)} %param.6), kind=kOutput, calls=%fused_computation.59 | convolution fusion | flops 3020881920 | bytes 31457280 | tf_op jit(solution)/shard_map/pbk,pak->pba/dot_general | solution.py:185
  154.0 51.5 %collective-permute-done.13 = bf16[15,128,256]{2,1,0:T(8,128)(2,1)} collective-permute-done((bf16[15,128,256]{2,1,0:T(8,128)(2,1)}, bf16[15,128,256]{2,1,0:T(8,128)(2,1)}, u32[]{:S(2)}, u32[]{:S(2)}) %collective-permute-start.13) | collective-permute-done | bytes 983072 | tf_op jit(solution)/shard_map/ppermute | solution.py:31
  210.2 23.6 %contract.3 = (f32[128,128,128]{2,1,0:T(8,128)}, bf16[128,128,128]{2,1,0:T(8,128)(2,1)}) custom-call(s32[180]{0:T(256)} %reshape.197.cells, bf16[15,512,1536]{2,1,0:T(8,128)(2,1)} %right.5, bf16[15,512,128]{2,1,0:T(8,128)(2,1)} %fusion.19.amplitude), custom_call_target="tpu_custom_call" | custom-call | flops 3019898880 | bytes 38141952 | tf_op jit(solution)/shard_map/contract/pallas_call | solution.py:96
  233.9 7.4 %collective-permute-done.18 = bf16[128,128,128]{2,1,0:T(8,128)(2,1)} collective-permute-done((bf16[128,128,128]{2,1,0:T(8,128)(2,1)}, bf16[128,128,128]{2,1,0:T(8,128)(2,1)}, u32[]{:S(2)}, u32[]{:S(2)}) %collective-permute-start.18) | collective-permute-done | bytes 4194336 | tf_op jit(solution)/shard_map/ppermute | solution.py:229
  258.5 10.8 %collective-permute-done.22 = bf16[15,128,128]{2,1,0:T(8,128)(2,1)S(1)} collective-permute-done((bf16[15,128,128]{2,1,0:T(8,128)(2,1)}, bf16[15,128,128]{2,1,0:T(8,128)(2,1)S(1)}, u32[]{:S(2)}, u32[]{:S(2)}) %collective-permute-start.22) | collective-permute-done | bytes 491552 | tf_op jit(solution)/shard_map/ppermute | solution.py:31
  269.2 9.0 %collective-permute-start.25 = (bf16[15,128,128]{2,1,0:T(8,128)(2,1)}, bf16[15,128,128]{2,1,0:T(8,128)(2,1)S(1)}, u32[]{:S(2)}, u32[]{:S(2)}) collective-permute-start(bf16[15,128,128]{2,1,0:T(8,128)(2,1)} %get-tuple-element.218), channel_id=1, source_target_pairs={{0,4},{2,6},{4,0},{6,2},{1,5},{3,7},{5,1},{7,3},{8,12},{10,14},{12... | collective-permute-start | bytes 1474568 | tf_op jit(solution)/shard_map/ppermute | solution.py:31
  281.0 14.7 %collective-permute-done.20 = bf16[15,128,256]{2,1,0:T(8,128)(2,1)} collective-permute-done((bf16[15,128,256]{2,1,0:T(8,128)(2,1)}, bf16[15,128,256]{2,1,0:T(8,128)(2,1)}, u32[]{:S(2)}, u32[]{:S(2)}) %collective-permute-start.20) | collective-permute-done | bytes 983072 | tf_op jit(solution)/shard_map/ppermute | solution.py:31
  306.2 29.0 %contract.4 = (f32[128,128,256]{2,1,0:T(8,128)}, bf16[128,128,256]{2,1,0:T(8,128)(2,1)}) custom-call(s32[180]{0:T(256)} %reshape.197.cells, bf16[15,512,1536]{2,1,0:T(8,128)(2,1)} %right.5, bf16[15,512,256]{2,1,0:T(8,128)(2,1)} %fusion.5.amplitude), custom_call_target="tpu_custom_call" | custom-call | flops 6039797760 | bytes 52690944 | tf_op jit(solution)/shard_map/contract/pallas_call | solution.py:96
  335.3 10.5 %collective-permute-done.24 = bf16[32,128,128]{2,1,0:T(8,128)(2,1)S(1)} collective-permute-done((bf16[32,128,128]{2,1,0:T(8,128)(2,1)S(1)}, bf16[32,128,128]{2,1,0:T(8,128)(2,1)S(1)}, u32[]{:S(2)}, u32[]{:S(2)}) %collective-permute-start.24) | collective-permute-done | bytes 1048608 | tf_op jit(solution)/shard_map/ppermute | solution.py:153
  350.1 11.9 %collective-permute-done.27 = bf16[128,128,256]{2,1,0:T(8,128)(2,1)S(1)} collective-permute-done((bf16[128,128,256]{2,1,0:T(8,128)(2,1)}, bf16[128,128,256]{2,1,0:T(8,128)(2,1)S(1)}, u32[]{:S(2)}, u32[]{:S(2)}) %collective-permute-start.27) | collective-permute-done | bytes 8388640 | tf_op jit(solution)/shard_map/ppermute | solution.py:229
  362.0 8.3 %fusion.27 = (bf16[32,128,256]{2,1,0:T(8,128)(2,1)S(1)}, bf16[32,128,256]{2,1,0:T(8,128)(2,1)S(1)}) fusion(f32[4,32,128,256]{3,2,1,0:T(8,128)} %bitcast.206, s32[]{:T(128)S(6)} %select_n.186, bf16[4,32,128,256]{3,2,1,0:T(8,128)(2,1)S(1)} %bitcast.218, s32[]{:T(128)S(6)} %select_n.184), kind=kLoop, calls=%fused_computation.35 | loop fusion | flops 6291456 | bytes 16777224 | tf_op jit(solution)/shard_map/convert_element_type | solution.py:145
  385.1 11.6 %collective-permute-done.31 = bf16[15,128,128]{2,1,0:T(8,128)(2,1)S(1)} collective-permute-done((bf16[15,128,128]{2,1,0:T(8,128)(2,1)S(1)}, bf16[15,128,128]{2,1,0:T(8,128)(2,1)S(1)}, u32[]{:S(2)}, u32[]{:S(2)}) %collective-permute-start.31) | collective-permute-done | bytes 491552 | tf_op jit(solution)/shard_map/ppermute | solution.py:31
  396.7 8.5 %collective-permute-done.30 = bf16[15,128,128]{2,1,0:T(8,128)(2,1)S(1)} collective-permute-done((bf16[15,128,128]{2,1,0:T(8,128)(2,1)S(1)}, bf16[15,128,128]{2,1,0:T(8,128)(2,1)S(1)}, u32[]{:S(2)}, u32[]{:S(2)}) %collective-permute-start.30) | collective-permute-done | bytes 491552 | tf_op jit(solution)/shard_map/ppermute | solution.py:31
  409.6 23.6 %contract.5 = (f32[128,128,128]{2,1,0:T(8,128)}, bf16[128,128,128]{2,1,0:T(8,128)(2,1)}) custom-call(s32[180]{0:T(256)} %reshape.197.cells, bf16[15,512,1536]{2,1,0:T(8,128)(2,1)} %right.5, bf16[15,512,128]{2,1,0:T(8,128)(2,1)} %fusion.17.amplitude), custom_call_target="tpu_custom_call" | custom-call | flops 3019898880 | bytes 38141952 | tf_op jit(solution)/shard_map/contract/pallas_call | solution.py:96
  433.2 36.2 %collective-permute-done.33 = bf16[32,128,256]{2,1,0:T(8,128)(2,1)S(1)} collective-permute-done((bf16[32,128,256]{2,1,0:T(8,128)(2,1)S(1)}, bf16[32,128,256]{2,1,0:T(8,128)(2,1)S(1)}, u32[]{:S(2)}, u32[]{:S(2)}) %collective-permute-start.33) | collective-permute-done | bytes 2097184 | tf_op jit(solution)/shard_map/ppermute | solution.py:153
  482.1 41.8 %collective-permute-done.35 = bf16[32,128,256]{2,1,0:T(8,128)(2,1)S(1)} collective-permute-done((bf16[32,128,256]{2,1,0:T(8,128)(2,1)S(1)}, bf16[32,128,256]{2,1,0:T(8,128)(2,1)S(1)}, u32[]{:S(2)}, u32[]{:S(2)}) %collective-permute-start.35) | collective-permute-done | bytes 2097184 | tf_op jit(solution)/shard_map/ppermute | solution.py:153
  527.7 24.0 %collective-permute-done.36 = bf16[32,128,128]{2,1,0:T(8,128)(2,1)S(1)} collective-permute-done((bf16[32,128,128]{2,1,0:T(8,128)(2,1)S(1)}, bf16[32,128,128]{2,1,0:T(8,128)(2,1)S(1)}, u32[]{:S(2)}, u32[]{:S(2)}) %collective-permute-start.36) | collective-permute-done | bytes 1048608 | tf_op jit(solution)/shard_map/ppermute | solution.py:153
  571.2 24.3 %collective-permute-done.37 = bf16[32,128,128]{2,1,0:T(8,128)(2,1)} collective-permute-done((bf16[32,128,128]{2,1,0:T(8,128)(2,1)}, bf16[32,128,128]{2,1,0:T(8,128)(2,1)}, u32[]{:S(2)}, u32[]{:S(2)}) %collective-permute-start.37) | collective-permute-done | bytes 1048608 | tf_op jit(solution)/shard_map/ppermute | solution.py:153
  (157 shorter events, 153.0 us)
Async XLA Ops:
  14.1 33.6 %collective-permute-start.2 = (bf16[15,128,128]{2,1,0:T(8,128)(2,1)}, bf16[15,128,128]{2,1,0:T(8,128)(2,1)S(1)}, u32[]{:S(2)}, u32[]{:S(2)}) collective-permute-start(bf16[15,128,128]{2,1,0:T(8,128)(2,1)} %get-tuple-element.237), channel_id=1, source_target_pairs={{0,24},{8,16},{16,8},{24,0},{1,25},{9,17},{17,9},{25,1},{2,26},{10... | collective-permute-start | bytes 1474568 | tf_op jit(solution)/shard_map/ppermute | solution.py:31
  18.0 29.7 %collective-permute-start.1 = (bf16[15,128,128]{2,1,0:T(8,128)(2,1)}, bf16[15,128,128]{2,1,0:T(8,128)(2,1)S(1)}, u32[]{:S(2)}, u32[]{:S(2)}) collective-permute-start(bf16[15,128,128]{2,1,0:T(8,128)(2,1)} %get-tuple-element.238), channel_id=1, source_target_pairs={{0,16},{8,24},{16,0},{24,8},{1,17},{9,25},{17,1},{25,9},{2,18},{10... | collective-permute-start | bytes 1474568 | tf_op jit(solution)/shard_map/ppermute | solution.py:31
  18.5 29.2 %collective-permute-start = (bf16[15,128,128]{2,1,0:T(8,128)(2,1)}, bf16[15,128,128]{2,1,0:T(8,128)(2,1)}, u32[]{:S(2)}, u32[]{:S(2)}) collective-permute-start(bf16[15,128,128]{2,1,0:T(8,128)(2,1)} %get-tuple-element.239), channel_id=1, source_target_pairs={{0,8},{8,0},{16,24},{24,16},{1,9},{9,1},{17,25},{25,17},{2,10},{10... | collective-permute-start | bytes 1474568 | tf_op jit(solution)/shard_map/ppermute | solution.py:31
  77.3 40.6 %collective-permute-start.10 = (bf16[15,128,128]{2,1,0:T(8,128)(2,1)}, bf16[15,128,128]{2,1,0:T(8,128)(2,1)}, u32[]{:S(2)}, u32[]{:S(2)}) collective-permute-start(bf16[15,128,128]{2,1,0:T(8,128)(2,1)} %get-tuple-element.230), channel_id=1, source_target_pairs={{0,4},{2,6},{4,0},{6,2},{1,5},{3,7},{5,1},{7,3},{8,12},{10,14},{12... | collective-permute-start | bytes 1474568 | tf_op jit(solution)/shard_map/ppermute | solution.py:31
  77.3 40.6 %collective-permute-start.9 = (bf16[15,128,128]{2,1,0:T(8,128)(2,1)}, bf16[15,128,128]{2,1,0:T(8,128)(2,1)}, u32[]{:S(2)}, u32[]{:S(2)}) collective-permute-start(bf16[15,128,128]{2,1,0:T(8,128)(2,1)} %get-tuple-element.231), channel_id=1, source_target_pairs={{0,2},{2,0},{4,6},{6,4},{1,3},{3,1},{5,7},{7,5},{8,10},{10,8},{12,... | collective-permute-start | bytes 1474568 | tf_op jit(solution)/shard_map/ppermute | solution.py:31
  97.0 43.6 %collective-permute-start.8 = (bf16[15,128,128]{2,1,0:T(8,128)(2,1)}, bf16[15,128,128]{2,1,0:T(8,128)(2,1)}, u32[]{:S(2)}, u32[]{:S(2)}) collective-permute-start(bf16[15,128,128]{2,1,0:T(8,128)(2,1)} %get-tuple-element.233), channel_id=1, source_target_pairs={{0,24},{8,16},{16,8},{24,0},{1,25},{9,17},{17,9},{25,1},{2,26},{10... | collective-permute-start | bytes 1474568 | tf_op jit(solution)/shard_map/ppermute | solution.py:31
  121.2 30.5 %collective-permute-start.14 = (bf16[15,128,256]{2,1,0:T(8,128)(2,1)}, bf16[15,128,256]{2,1,0:T(8,128)(2,1)}, u32[]{:S(2)}, u32[]{:S(2)}) collective-permute-start(bf16[15,128,256]{2,1,0:T(8,128)(2,1)} %get-tuple-element.201), channel_id=1, source_target_pairs={{0,6},{2,4},{4,2},{6,0},{1,7},{3,5},{5,3},{7,1},{8,14},{10,12},{12... | collective-permute-start | bytes 2949128 | tf_op jit(solution)/shard_map/ppermute | solution.py:31
  140.6 65.0 %collective-permute-start.13 = (bf16[15,128,256]{2,1,0:T(8,128)(2,1)}, bf16[15,128,256]{2,1,0:T(8,128)(2,1)}, u32[]{:S(2)}, u32[]{:S(2)}) collective-permute-start(bf16[15,128,256]{2,1,0:T(8,128)(2,1)} %get-tuple-element.202), channel_id=1, source_target_pairs={{0,4},{2,6},{4,0},{6,2},{1,5},{3,7},{5,1},{7,3},{8,12},{10,14},{12... | collective-permute-start | bytes 2949128 | tf_op jit(solution)/shard_map/ppermute | solution.py:31
  140.6 64.9 %collective-permute-start.12 = (bf16[15,128,256]{2,1,0:T(8,128)(2,1)}, bf16[15,128,256]{2,1,0:T(8,128)(2,1)}, u32[]{:S(2)}, u32[]{:S(2)}) collective-permute-start(bf16[15,128,256]{2,1,0:T(8,128)(2,1)} %get-tuple-element.203), channel_id=1, source_target_pairs={{0,2},{2,0},{4,6},{6,4},{1,3},{3,1},{5,7},{7,5},{8,10},{10,8},{12,... | collective-permute-start | bytes 2949128 | tf_op jit(solution)/shard_map/ppermute | solution.py:31
  148.7 56.8 %collective-permute-start.17 = (bf16[15,128,128]{2,1,0:T(8,128)(2,1)}, bf16[15,128,128]{2,1,0:T(8,128)(2,1)}, u32[]{:S(2)}, u32[]{:S(2)}) collective-permute-start(bf16[15,128,128]{2,1,0:T(8,128)(2,1)} %get-tuple-element.225), channel_id=1, source_target_pairs={{0,24},{8,16},{16,8},{24,0},{1,25},{9,17},{17,9},{25,1},{2,26},{10... | collective-permute-start | bytes 1474568 | tf_op jit(solution)/shard_map/ppermute | solution.py:31
  151.1 54.5 %collective-permute-start.16 = (bf16[15,128,128]{2,1,0:T(8,128)(2,1)}, bf16[15,128,128]{2,1,0:T(8,128)(2,1)}, u32[]{:S(2)}, u32[]{:S(2)}) collective-permute-start(bf16[15,128,128]{2,1,0:T(8,128)(2,1)} %get-tuple-element.226), channel_id=1, source_target_pairs={{0,16},{8,24},{16,0},{24,8},{1,17},{9,25},{17,1},{25,9},{2,18},{10... | collective-permute-start | bytes 1474568 | tf_op jit(solution)/shard_map/ppermute | solution.py:31
  151.7 53.8 %collective-permute-start.15 = (bf16[15,128,128]{2,1,0:T(8,128)(2,1)}, bf16[15,128,128]{2,1,0:T(8,128)(2,1)}, u32[]{:S(2)}, u32[]{:S(2)}) collective-permute-start(bf16[15,128,128]{2,1,0:T(8,128)(2,1)} %get-tuple-element.227), channel_id=1, source_target_pairs={{0,8},{8,0},{16,24},{24,16},{1,9},{9,1},{17,25},{25,17},{2,10},{10... | collective-permute-start | bytes 1474568 | tf_op jit(solution)/shard_map/ppermute | solution.py:31
  249.6 28.6 %collective-permute-start.21 = (bf16[15,128,256]{2,1,0:T(8,128)(2,1)}, bf16[15,128,256]{2,1,0:T(8,128)(2,1)}, u32[]{:S(2)}, u32[]{:S(2)}) collective-permute-start(bf16[15,128,256]{2,1,0:T(8,128)(2,1)} %get-tuple-element.197), channel_id=1, source_target_pairs={{0,24},{8,16},{16,8},{24,0},{1,25},{9,17},{17,9},{25,1},{2,26},{10... | collective-permute-start | bytes 2949128 | tf_op jit(solution)/shard_map/ppermute | solution.py:31
  252.0 43.7 %collective-permute-start.20 = (bf16[15,128,256]{2,1,0:T(8,128)(2,1)}, bf16[15,128,256]{2,1,0:T(8,128)(2,1)}, u32[]{:S(2)}, u32[]{:S(2)}) collective-permute-start(bf16[15,128,256]{2,1,0:T(8,128)(2,1)} %get-tuple-element.198), channel_id=1, source_target_pairs={{0,16},{8,24},{16,0},{24,8},{1,17},{9,25},{17,1},{25,9},{2,18},{10... | collective-permute-start | bytes 2949128 | tf_op jit(solution)/shard_map/ppermute | solution.py:31
  252.6 45.5 %collective-permute-start.19 = (bf16[15,128,256]{2,1,0:T(8,128)(2,1)}, bf16[15,128,256]{2,1,0:T(8,128)(2,1)}, u32[]{:S(2)}, u32[]{:S(2)}) collective-permute-start(bf16[15,128,256]{2,1,0:T(8,128)(2,1)} %get-tuple-element.199), channel_id=1, source_target_pairs={{0,8},{8,0},{16,24},{24,16},{1,9},{9,1},{17,25},{25,17},{2,10},{10... | collective-permute-start | bytes 2949128 | tf_op jit(solution)/shard_map/ppermute | solution.py:31
  256.0 92.6 %collective-permute-start.26 = (bf16[15,128,128]{2,1,0:T(8,128)(2,1)}, bf16[15,128,128]{2,1,0:T(8,128)(2,1)S(1)}, u32[]{:S(2)}, u32[]{:S(2)}) collective-permute-start(bf16[15,128,128]{2,1,0:T(8,128)(2,1)} %get-tuple-element.217), channel_id=1, source_target_pairs={{0,6},{2,4},{4,2},{6,0},{1,7},{3,5},{5,3},{7,1},{8,14},{10,12},{12... | collective-permute-start | bytes 1474568 | tf_op jit(solution)/shard_map/ppermute | solution.py:31
  269.2 79.3 %collective-permute-start.25 = (bf16[15,128,128]{2,1,0:T(8,128)(2,1)}, bf16[15,128,128]{2,1,0:T(8,128)(2,1)S(1)}, u32[]{:S(2)}, u32[]{:S(2)}) collective-permute-start(bf16[15,128,128]{2,1,0:T(8,128)(2,1)} %get-tuple-element.218), channel_id=1, source_target_pairs={{0,4},{2,6},{4,0},{6,2},{1,5},{3,7},{5,1},{7,3},{8,12},{10,14},{12... | collective-permute-start | bytes 1474568 | tf_op jit(solution)/shard_map/ppermute | solution.py:31
  278.2 57.0 %collective-permute-start.23 = (bf16[32,128,128]{2,1,0:T(8,128)(2,1)}, bf16[32,128,128]{2,1,0:T(8,128)(2,1)S(1)}, u32[]{:S(2)}, u32[]{:S(2)}) collective-permute-start(bf16[32,128,128]{2,1,0:T(8,128)(2,1)} %get-tuple-element.146), channel_id=1, source_target_pairs={{0,2},{2,4},{4,6},{6,0},{1,3},{3,5},{5,7},{7,1},{8,10},{10,12},{12... | collective-permute-start | bytes 3145736 | tf_op jit(solution)/shard_map/ppermute | solution.py:153
  295.7 50.1 %collective-permute-start.24 = (bf16[32,128,128]{2,1,0:T(8,128)(2,1)S(1)}, bf16[32,128,128]{2,1,0:T(8,128)(2,1)S(1)}, u32[]{:S(2)}, u32[]{:S(2)}) collective-permute-start(bf16[32,128,128]{2,1,0:T(8,128)(2,1)S(1)} %get-tuple-element.147), channel_id=1, source_target_pairs={{0,6},{2,0},{4,2},{6,4},{1,7},{3,1},{5,3},{7,5},{8,14},{10,8},{12,... | collective-permute-start | bytes 3145736 | tf_op jit(solution)/shard_map/ppermute | solution.py:153
  377.2 55.9 %collective-permute-start.32 = (bf16[32,128,256]{2,1,0:T(8,128)(2,1)S(1)}, bf16[32,128,256]{2,1,0:T(8,128)(2,1)}, u32[]{:S(2)}, u32[]{:S(2)}) collective-permute-start(bf16[32,128,256]{2,1,0:T(8,128)(2,1)S(1)} %get-tuple-element.166), channel_id=1, source_target_pairs={{0,2},{2,4},{4,6},{6,0},{1,3},{3,5},{5,7},{7,1},{8,10},{10,12},{12... | collective-permute-start | bytes 6291464 | tf_op jit(solution)/shard_map/ppermute | solution.py:153
  377.2 92.1 %collective-permute-start.33 = (bf16[32,128,256]{2,1,0:T(8,128)(2,1)S(1)}, bf16[32,128,256]{2,1,0:T(8,128)(2,1)S(1)}, u32[]{:S(2)}, u32[]{:S(2)}) collective-permute-start(bf16[32,128,256]{2,1,0:T(8,128)(2,1)S(1)} %get-tuple-element.167), channel_id=1, source_target_pairs={{0,6},{2,0},{4,2},{6,4},{1,7},{3,1},{5,3},{7,5},{8,14},{10,8},{12,... | collective-permute-start | bytes 6291464 | tf_op jit(solution)/shard_map/ppermute | solution.py:153
  474.0 49.8 %collective-permute-start.35 = (bf16[32,128,256]{2,1,0:T(8,128)(2,1)S(1)}, bf16[32,128,256]{2,1,0:T(8,128)(2,1)S(1)}, u32[]{:S(2)}, u32[]{:S(2)}) collective-permute-start(bf16[32,128,256]{2,1,0:T(8,128)(2,1)S(1)} %fusion.15), channel_id=1, source_target_pairs={{0,2},{2,4},{4,6},{6,0},{1,3},{3,5},{5,7},{7,1},{8,10},{10,12},{12... | collective-permute-start | bytes 6291464 | tf_op jit(solution)/shard_map/ppermute | solution.py:153
  523.9 47.3 %collective-permute-start.38 = (bf16[32,128,128]{2,1,0:T(8,128)(2,1)S(1)}, bf16[32,128,128]{2,1,0:T(8,128)(2,1)}, u32[]{:S(2)}, u32[]{:S(2)}) collective-permute-start(bf16[32,128,128]{2,1,0:T(8,128)(2,1)S(1)} %get-tuple-element.179), channel_id=1, source_target_pairs={{0,6},{2,0},{4,2},{6,4},{1,7},{3,1},{5,3},{7,5},{8,14},{10,8},{12,... | collective-permute-start | bytes 3145736 | tf_op jit(solution)/shard_map/ppermute | solution.py:153
  553.2 42.3 %collective-permute-start.37 = (bf16[32,128,128]{2,1,0:T(8,128)(2,1)}, bf16[32,128,128]{2,1,0:T(8,128)(2,1)}, u32[]{:S(2)}, u32[]{:S(2)}) collective-permute-start(bf16[32,128,128]{2,1,0:T(8,128)(2,1)} %fusion.29), channel_id=1, source_target_pairs={{0,2},{2,4},{4,6},{6,0},{1,3},{3,5},{5,7},{7,1},{8,10},{10,12},{12... | collective-permute-start | bytes 3145736 | tf_op jit(solution)/shard_map/ppermute | solution.py:153
  (37 other events, 593.6 us)
